TPU v7x, 32 devices: a whole 2x2x4 slice. The times are simulated.
32 devices in a mesh: grp: 2 (over x), seq: 8 (over z, y), head: 2 (over core).
Axes of the slice: x: 2, y: 2, z: 4, core: 2. Of those that a mesh axis runs over, the one named last changes fastest.
Arguments:
- q_feat: bfloat16 [8192, 256], P(('grp', 'seq'), 'head'), parts along dimension 0, may hold values from -5 to 5
- k_feat: bfloat16 [8192, 256], P(('grp', 'seq'), 'head'), parts along dimension 0, may hold values from -5 to 5
- values: bfloat16 [8192, 2048], P(('grp', 'seq'), 'head'), parts along dimension 0, may hold values from -8 to 8
- win_query: bfloat16 [8192, 2048], P(('grp', 'seq'), 'head'), parts along dimension 0, may hold values from -20 to 20
- win_key: bfloat16 [8192, 2048], P(('grp', 'seq'), 'head'), parts along dimension 0, may hold values from -5 to 5
- log_gates: float32 [8192, 16], P(('grp', 'seq'), 'head'), parts along dimension 0, may hold values from -2.2 to 0
- conv_weight: float32 [3, 2048], P(None, 'head'), may hold values from -2.5 to 2.5
Outputs:
- mixed: bfloat16 [8192, 2048], P(('grp', 'seq'), 'head'), parts along dimension 0
There are 2 independent parts, one for each index of `grp`. A program takes and returns all parts, laid end to end along the dimension named above; an argument that names none is the same for every part. Nothing has to cross between parts.
All inputs are finite; a program needn't handle non-finite values.
Results may differ from a plain program's by a relative error of at most 0.011.
Values may be sent and summed in bfloat16 or wider, within the bound.
No kernel may reach another device: no remote copies, remote signals or barrier semaphores. Data moves between devices by JAX's collectives and lax.ppermute only.
A program may use at most 192 MiB of HBM per device.

v0:
```python
import jax
import jax.numpy as jnp
from jax import lax
from jax.sharding import PartitionSpec as P

WINDOW = 64
BLOCK = 512


def passed_along(block, axis, distance):
    devices = range(lax.axis_size(axis))
    route = [(i - distance, i) for i in devices if i - distance in devices]
    return lax.ppermute(block, axis, route)


def prefix(value, axis, join, neutral):
    count, mine = (lax.axis_size(axis), lax.axis_index(axis))
    pieces = jax.tree.map(lambda part: lax.all_gather(part, axis), value)
    so_far = jax.tree.map(
        lambda part, zero: jnp.full_like(part, 0) + jnp.asarray(zero, part.dtype), value, neutral
    )

    def hop(position, so_far):
        longer = join(so_far, jax.tree.map(lambda part: part[position], pieces))
        return jax.tree.map(lambda new, old: jnp.where(position < mine, new, old), longer, so_far)

    return lax.fori_loop(0, count - 1, hop, so_far)


def taylor_map(features, heads):
    tok_rows = features.shape[0]
    width = features.shape[1] // heads
    spread = features.astype(jnp.float32).reshape(tok_rows, heads, width)
    linear = spread * width ** (-0.25)
    square = (spread[:, :, :, None] * spread[:, :, None, :]).reshape(
        tok_rows, heads, width * width
    ) * (2.0 * width) ** (-0.5)
    ones = jnp.ones((tok_rows, heads, 1), jnp.float32)
    return jnp.concatenate([ones, linear, square], axis=2).astype(jnp.bfloat16)


def three_parts(wide):
    upper = wide.astype(jnp.bfloat16)
    remain = wide - upper.astype(jnp.float32)
    middle = remain.astype(jnp.bfloat16)
    lowest = (remain - middle.astype(jnp.float32)).astype(jnp.bfloat16)
    return (upper, middle, lowest)


def divided_product(form, narrow, wide):
    total = None
    for piece in three_parts(wide):
        term = jnp.einsum(form, narrow, piece, preferred_element_type=jnp.float32)
        total = term if total is None else total + term
    return total


def combine_states(earlier, later):
    decay_a, state_a, norm_a = earlier
    decay_b, state_b, norm_b = later
    return (
        decay_a * decay_b,
        decay_b[:, None, None] * state_a + state_b,
        decay_b[:, None] * norm_a + norm_b,
    )


def local(q_feat, k_feat, values, win_query, win_key, log_gates, conv_weight):
    seq_rows = values.shape[0]
    heads_here = log_gates.shape[1]
    head_size = values.shape[1] // heads_here
    feat_width = q_feat.shape[1] // heads_here
    features = 1 + feat_width + feat_width * feat_width
    block = BLOCK
    window = WINDOW
    prev_key, prev_value = passed_along(
        (win_key[seq_rows - window :], values[seq_rows - window :]), "seq", 1
    )
    value_ext = jnp.concatenate([prev_value, values], axis=0)
    key_ext = jnp.concatenate([prev_key, win_key], axis=0)
    convolved = jnp.zeros(values.shape, jnp.float32)
    for tap in range(conv_weight.shape[0]):
        convolved = convolved + conv_weight[tap][None, :] * value_ext[
            window - tap : window - tap + seq_rows
        ].astype(jnp.float32)
    filtered_values = convolved.astype(jnp.bfloat16).reshape(seq_rows, heads_here, head_size)
    query_features = taylor_map(q_feat, heads_here)
    key_features = taylor_map(k_feat, heads_here)
    device_start = lax.axis_index("seq") * seq_rows
    causal = jnp.arange(block)[:, None] >= jnp.arange(block)[None, :]
    running_state = jnp.zeros((heads_here, features, head_size), jnp.float32)
    norm_total = jnp.zeros((heads_here, features), jnp.float32)
    cumulative = jnp.cumsum(log_gates, axis=0)
    cum_heads = cumulative.T
    decay_factor = jnp.exp(
        jnp.where(causal[None], cum_heads[:, :, None] - cum_heads[:, None, :], -jnp.inf)
    )
    score_matrix = (
        jnp.einsum("sjz,djz->jsd", query_features, key_features, preferred_element_type=jnp.float32)
        * decay_factor
    )
    den_block = jnp.sum(score_matrix, axis=2).T
    num_block = jnp.einsum(
        "hqk,khd->qhd",
        score_matrix.astype(jnp.bfloat16),
        filtered_values,
        preferred_element_type=jnp.float32,
    )
    block_finish = cumulative[-1]
    retention = jnp.exp(block_finish[None, :] - cumulative)
    weighted_values = filtered_values.astype(jnp.float32) * retention[:, :, None]
    running_state = jnp.exp(block_finish)[:, None, None] * running_state + divided_product(
        "mwv,mwr->wvr", key_features, weighted_values
    )
    norm_total = jnp.exp(block_finish)[:, None] * norm_total + divided_product(
        "vin,vi->in", key_features, retention
    )
    decay_parts = jnp.exp(cumulative)
    win_keys = key_ext.reshape(block + window, heads_here, head_size)
    win_values = value_ext.reshape(block + window, heads_here, head_size)
    win_queries = win_query.reshape(block, heads_here, head_size)
    win_scores = jnp.einsum(
        "qhd,khd->hqk", win_queries, win_keys, preferred_element_type=jnp.float32
    ) * head_size ** (-0.5)
    key_pos = 0 - window + jnp.arange(block + window)
    query_pos = 0 + jnp.arange(block)
    valid = (
        (key_pos[None, :] <= query_pos[:, None])
        & (key_pos[None, :] > query_pos[:, None] - window)
        & (device_start + key_pos[None, :] >= 0)
    )
    win_scores = jnp.where(valid[None], win_scores, -jnp.inf)
    top = jnp.max(win_scores, axis=2, keepdims=True)
    weights = jnp.exp(win_scores - top)
    total = jnp.sum(weights, axis=2, keepdims=True)
    probs = (weights / total).astype(jnp.bfloat16)
    window_parts = jnp.einsum("hqk,khd->qhd", probs, win_values, preferred_element_type=jnp.float32)
    numerator = num_block
    denominator = den_block
    decay_total = jnp.exp(block_finish)
    identity = (
        jnp.ones_like(decay_total),
        jnp.zeros_like(running_state),
        jnp.zeros_like(norm_total),
    )
    carried = prefix((decay_total, running_state, norm_total), "seq", combine_states, identity)
    prefix_state = carried[1]
    prefix_norm = carried[2]
    numerator = numerator + decay_parts[:, :, None] * divided_product(
        "thf,hfd->thd", query_features, prefix_state
    )
    denominator = denominator + decay_parts * divided_product(
        "thf,hf->th", query_features, prefix_norm
    )
    mixed = numerator / denominator[:, :, None] + window_parts
    return mixed.astype(jnp.bfloat16).reshape(seq_rows, heads_here * head_size)


def solution(mesh):
    placed = (
        P(("grp", "seq"), "head"),
        P(("grp", "seq"), "head"),
        P(("grp", "seq"), "head"),
        P(("grp", "seq"), "head"),
        P(("grp", "seq"), "head"),
        P(("grp", "seq"), "head"),
        P(None, "head"),
    )
    return jax.shard_map(
        local, mesh=mesh, in_specs=placed, out_specs=P(("grp", "seq"), "head"), check_vma=False
    )
```

profile of v0, /device:TPU:0, one launch (start us, length us, event | category | flops | bytes accessed | tf_op | source)
XLA Modules:
  0.0 220.2 jit_solution(10231950504331805521)
XLA Ops:
  6.5 1.7 slice.32
  8.2 5.5 %collective-permute-start = (bf16[64,1024]{1,0:T(8,128)(2,1)}, bf16[64,1024]{1,0:T(8,128)(2,1)}, u32[]{:S(2)}, u32[]{:S(2)}) collective-permute-start(bf16[64,1024]{1,0:T(8,128)(2,1)} %slice.32), channel_id=1, source_target_pairs={{0,2},{2,4},{4,6},{6,8},{8,10},{10,12},{12,14},{1,3},{3,5},{5,7},{... | collective-permute-start | bytes 393224 | tf_op jit(solution)/shard_map/ppermute | solution.py:13
  14.7 2.0 multiply_convert_fusion
  17.5 2.0 multiply_convert_fusion.1
  21.2 3.3 %pad_maximum_fusion.1 = (bf16[512,8,273]{0,2,1:T(8,128)(2,1)S(1)}, bf16[512,8,273]{0,2,1:T(8,128)(2,1)S(1)}) fusion(bf16[512,8,256]{0,2,1:T(8,128)(2,1)} %bitcast.155, bf16[512,8,16]{0,2,1:T(8,128)(2,1)S(1)} %get-tuple-element.197, bf16[273]{0:T(512)(128)(2,1)S(1)} %pad.5.clone, bf16[512,8,256]{0,2,1:T(8,128)(2,1)} %bitcast.156, ...), kind=kLoop, calls=%fused_computation.28 | loop fusion | flops 12300288 | bytes 8929826 | tf_op jit(solution)/shard_map/concatenate | solution.py:39
  31.6 1.6 slice.39
  33.1 3.4 %collective-permute-start.1 = (bf16[64,1024]{1,0:T(8,128)(2,1)}, bf16[64,1024]{1,0:T(8,128)(2,1)}, u32[]{:S(2)}, u32[]{:S(2)}) collective-permute-start(bf16[64,1024]{1,0:T(8,128)(2,1)} %slice.39), channel_id=1, source_target_pairs={{0,2},{2,4},{4,6},{6,8},{8,10},{10,12},{12,14},{1,3},{3,5},{5,7},{... | collective-permute-start | bytes 393224 | tf_op jit(solution)/shard_map/ppermute | solution.py:13
  37.8 2.6 %fusion.67 = f32[8,1,273]{2,1,0:T(1,128)S(1)} fusion(bf16[512,8,273]{0,2,1:T(8,128)(2,1)} %copy-done.3, bf16[512,8,1]{0,1,2:T(8,128)(2,1)S(1)} %get-tuple-element.184), kind=kOutput, calls=%fused_computation.84 | convolution fusion | flops 2236416 | bytes 2253344 | tf_op jit(solution)/shard_map/vin,vi->in/dot_general | solution.py:53
  41.9 5.8 %fusion.6 = (f32[8,512]{1,0:T(8,128)S(1)}, f32[8,512,512]{1,2,0:T(8,128)}) fusion(f32[8,512]{1,0:T(8,128)S(1)} %add_bitcast_fusion.1, pred[512,512]{0,1:T(8,128)(4,1)S(1)} %iota_compare_fusion.1, bf16[512,8,273]{0,2,1:T(8,128)(2,1)S(1)} %get-tuple-element.192, bf16[512,8,273]{0,2,1:T(8,128)(2,1)S(1)} %copy-done.4), kind=kOutput, calls=%fused_computation.14 | convolution fusion | flops 1153429504 | bytes 13156352 | tf_op jit(solution)/shard_map/sjz,djz->jsd/dot_general | solution.py:99
  47.7 17.2 %all-gather.2 = f32[8,1,8]{2,1,0:T(1,128)S(1)} all-gather(f32[1,1,8]{2,1,0:T(1,128)S(1)} %bitcast.169), channel_id=1, replica_groups=mesh['grp'=2,'seq'=8,'head'=2] {'seq'}, dimensions={0}, use_global_device_ids=true | all-gather | bytes 288 | tf_op jit(solution)/shard_map/all_gather | solution.py:18
  64.9 31.3 %all-gather.1 = f32[64,273]{1,0:T(8,128)S(1)} all-gather(f32[8,273]{1,0:T(8,128)S(1)} %fusion.73), channel_id=3, replica_groups=mesh['grp'=2,'seq'=8,'head'=2] {'seq'}, dimensions={0}, use_global_device_ids=true | all-gather | bytes 78624 | tf_op jit(solution)/shard_map/all_gather | solution.py:18
  96.3 2.7 %fusion.38 = f32[8,576,512]{2,1,0:T(8,128)S(1)} fusion(bf16[512,1024]{1,0:T(8,128)(2,1)} %param.13, bf16[64,1024]{1,0:T(8,128)(2,1)} %collective-permute-done.1, bf16[512,1024]{1,0:T(8,128)(2,1)S(1)} %copy-done), kind=kOutput, calls=%fused_computation.45 | convolution fusion | flops 606339072 | bytes 11665408 | tf_op jit(solution)/shard_map/qhd,khd->hqk/dot_general | solution.py:122
  99.0 6.7 %fusion.91 = (f32[8,512]{1,0:T(8,128)S(1)}, f32[8,512,576]{1,2,0:T(8,128)}) fusion(f32[8,576,512]{2,1,0:T(8,128)S(1)} %fusion.38, pred[512,576]{0,1:T(8,128)(4,1)S(1)} %copy-done.10), kind=kOutput, calls=%fused_computation.127 | output fusion | flops 14156351 | bytes 19185664 | tf_op jit(solution)/shard_map/sub | solution.py:134
  105.7 6.2 %fusion.10 = f32[8,128,512]{2,1,0:T(8,128)} fusion(f32[8,512,576]{1,2,0:T(8,128)} %get-tuple-element.194, f32[8,512]{1,0:T(8,128)S(1)} %get-tuple-element.193, bf16[576,1024]{1,0:T(8,128)(2,1)S(1)} %copy-done.7), kind=kOutput, calls=%fused_computation.18 | convolution fusion | flops 608698368 | bytes 12730368 | tf_op jit(solution)/shard_map/hqk,khd->qhd/dot_general | solution.py:137
  111.9 52.6 %all-gather.5.cloned.1.call-done = f32[64,273,128]{2,0,1:T(8,128)} async-done(((f32[8,273,128]{2,0,1:T(8,128)}), f32[64,273,128]{2,0,1:T(8,128)}) %all-gather.5.cloned.1.call-update) | async-done | bytes 8945680 | tf_op jit(solution)/shard_map/all_gather | solution.py:18
  164.5 37.3 %while.16 = (s32[]{:T(128)}, f32[8,273,128]{2,1,0:T(8,128)}, f32[8,273]{1,0:T(8,128)S(1)}, s32[]{:T(128)}, f32[8,8]{1,0:T(8,128)S(1)}, /*index=5*/f32[8,8,273,12...) while((s32[]{:T(128)}, f32[8,273,128]{2,1,0:T(8,128)}, f32[8,273]{1,0:T(8,128)S(1)}, ...), condition=%wide.region_3.4_spmd.clone, body=%wide.region_2.3_spmd.clone.sunk | while | flops 1126948 | bytes 5617511 | solution.py:27
  164.5 2.3 %constant_dynamic-slice_fusion.3 = f32[1,8,273,128]{3,1,0,2:T(8,128)} fusion(f32[8,8,273,128]{3,1,0,2:T(8,128)} %get-tuple-element.265, s32[]{:T(128)S(6)} %copy.124), kind=kLoop, calls=%fused_computation.5.clone.1 | loop fusion | bytes 2236420 | tf_op jit(solution)/shard_map/while/body/eval_jaxpr/dynamic_slice | solution.py:24
  166.8 2.6 %fusion.112 = f32[8,273,128]{2,1,0:T(8,128)} fusion(f32[1,8,273,128]{3,1,0,2:T(8,128)} %constant_dynamic-slice_fusion.3, f32[8,273,128]{2,1,0:T(8,128)} %get-tuple-element.252, f32[8]{0:T(128)S(1)} %fusion.111, pred[]{:T(512)S(6)} %compare.3, pred[]{:T(512)S(6)} %lt.24), kind=kLoop, calls=%fused_computation.2.clone.1 | loop fusion | flops 1118208 | bytes 3354658 | tf_op jit(solution)/shard_map/while/body/eval_jaxpr/jit(_where)/select_n | solution.py:25
  169.5 2.3 %constant_dynamic-slice_fusion.3 = f32[1,8,273,128]{3,1,0,2:T(8,128)} fusion(f32[8,8,273,128]{3,1,0,2:T(8,128)} %get-tuple-element.265, s32[]{:T(128)S(6)} %copy.124), kind=kLoop, calls=%fused_computation.5.clone.1 | loop fusion | bytes 2236420 | tf_op jit(solution)/shard_map/while/body/eval_jaxpr/dynamic_slice | solution.py:24
  171.8 3.0 %fusion.112 = f32[8,273,128]{2,1,0:T(8,128)} fusion(f32[1,8,273,128]{3,1,0,2:T(8,128)} %constant_dynamic-slice_fusion.3, f32[8,273,128]{2,1,0:T(8,128)} %get-tuple-element.252, f32[8]{0:T(128)S(1)} %fusion.111, pred[]{:T(512)S(6)} %compare.3, pred[]{:T(512)S(6)} %lt.24), kind=kLoop, calls=%fused_computation.2.clone.1 | loop fusion | flops 1118208 | bytes 3354658 | tf_op jit(solution)/shard_map/while/body/eval_jaxpr/jit(_where)/select_n | solution.py:25
  174.9 2.3 %constant_dynamic-slice_fusion.3 = f32[1,8,273,128]{3,1,0,2:T(8,128)} fusion(f32[8,8,273,128]{3,1,0,2:T(8,128)} %get-tuple-element.265, s32[]{:T(128)S(6)} %copy.124), kind=kLoop, calls=%fused_computation.5.clone.1 | loop fusion | bytes 2236420 | tf_op jit(solution)/shard_map/while/body/eval_jaxpr/dynamic_slice | solution.py:24
  177.2 3.0 %fusion.112 = f32[8,273,128]{2,1,0:T(8,128)} fusion(f32[1,8,273,128]{3,1,0,2:T(8,128)} %constant_dynamic-slice_fusion.3, f32[8,273,128]{2,1,0:T(8,128)} %get-tuple-element.252, f32[8]{0:T(128)S(1)} %fusion.111, pred[]{:T(512)S(6)} %compare.3, pred[]{:T(512)S(6)} %lt.24), kind=kLoop, calls=%fused_computation.2.clone.1 | loop fusion | flops 1118208 | bytes 3354658 | tf_op jit(solution)/shard_map/while/body/eval_jaxpr/jit(_where)/select_n | solution.py:25
  180.3 2.3 %constant_dynamic-slice_fusion.3 = f32[1,8,273,128]{3,1,0,2:T(8,128)} fusion(f32[8,8,273,128]{3,1,0,2:T(8,128)} %get-tuple-element.265, s32[]{:T(128)S(6)} %copy.124), kind=kLoop, calls=%fused_computation.5.clone.1 | loop fusion | bytes 2236420 | tf_op jit(solution)/shard_map/while/body/eval_jaxpr/dynamic_slice | solution.py:24
  182.6 3.0 %fusion.112 = f32[8,273,128]{2,1,0:T(8,128)} fusion(f32[1,8,273,128]{3,1,0,2:T(8,128)} %constant_dynamic-slice_fusion.3, f32[8,273,128]{2,1,0:T(8,128)} %get-tuple-element.252, f32[8]{0:T(128)S(1)} %fusion.111, pred[]{:T(512)S(6)} %compare.3, pred[]{:T(512)S(6)} %lt.24), kind=kLoop, calls=%fused_computation.2.clone.1 | loop fusion | flops 1118208 | bytes 3354658 | tf_op jit(solution)/shard_map/while/body/eval_jaxpr/jit(_where)/select_n | solution.py:25
  185.6 2.3 %constant_dynamic-slice_fusion.3 = f32[1,8,273,128]{3,1,0,2:T(8,128)} fusion(f32[8,8,273,128]{3,1,0,2:T(8,128)} %get-tuple-element.265, s32[]{:T(128)S(6)} %copy.124), kind=kLoop, calls=%fused_computation.5.clone.1 | loop fusion | bytes 2236420 | tf_op jit(solution)/shard_map/while/body/eval_jaxpr/dynamic_slice | solution.py:24
  188.0 3.0 %fusion.112 = f32[8,273,128]{2,1,0:T(8,128)} fusion(f32[1,8,273,128]{3,1,0,2:T(8,128)} %constant_dynamic-slice_fusion.3, f32[8,273,128]{2,1,0:T(8,128)} %get-tuple-element.252, f32[8]{0:T(128)S(1)} %fusion.111, pred[]{:T(512)S(6)} %compare.3, pred[]{:T(512)S(6)} %lt.24), kind=kLoop, calls=%fused_computation.2.clone.1 | loop fusion | flops 1118208 | bytes 3354658 | tf_op jit(solution)/shard_map/while/body/eval_jaxpr/jit(_where)/select_n | solution.py:25
  191.0 2.3 %constant_dynamic-slice_fusion.3 = f32[1,8,273,128]{3,1,0,2:T(8,128)} fusion(f32[8,8,273,128]{3,1,0,2:T(8,128)} %get-tuple-element.265, s32[]{:T(128)S(6)} %copy.124), kind=kLoop, calls=%fused_computation.5.clone.1 | loop fusion | bytes 2236420 | tf_op jit(solution)/shard_map/while/body/eval_jaxpr/dynamic_slice | solution.py:24
  193.3 3.0 %fusion.112 = f32[8,273,128]{2,1,0:T(8,128)} fusion(f32[1,8,273,128]{3,1,0,2:T(8,128)} %constant_dynamic-slice_fusion.3, f32[8,273,128]{2,1,0:T(8,128)} %get-tuple-element.252, f32[8]{0:T(128)S(1)} %fusion.111, pred[]{:T(512)S(6)} %compare.3, pred[]{:T(512)S(6)} %lt.24), kind=kLoop, calls=%fused_computation.2.clone.1 | loop fusion | flops 1118208 | bytes 3354658 | tf_op jit(solution)/shard_map/while/body/eval_jaxpr/jit(_where)/select_n | solution.py:25
  196.4 2.3 %constant_dynamic-slice_fusion.3 = f32[1,8,273,128]{3,1,0,2:T(8,128)} fusion(f32[8,8,273,128]{3,1,0,2:T(8,128)} %get-tuple-element.265, s32[]{:T(128)S(6)} %copy.124), kind=kLoop, calls=%fused_computation.5.clone.1 | loop fusion | bytes 2236420 | tf_op jit(solution)/shard_map/while/body/eval_jaxpr/dynamic_slice | solution.py:24
  198.7 3.0 %fusion.112 = f32[8,273,128]{2,1,0:T(8,128)} fusion(f32[1,8,273,128]{3,1,0,2:T(8,128)} %constant_dynamic-slice_fusion.3, f32[8,273,128]{2,1,0:T(8,128)} %get-tuple-element.252, f32[8]{0:T(128)S(1)} %fusion.111, pred[]{:T(512)S(6)} %compare.3, pred[]{:T(512)S(6)} %lt.24), kind=kLoop, calls=%fused_computation.2.clone.1 | loop fusion | flops 1118208 | bytes 3354658 | tf_op jit(solution)/shard_map/while/body/eval_jaxpr/jit(_where)/select_n | solution.py:25
  201.8 2.5 %fusion.65 = f32[8,128,512]{2,1,0:T(8,128)S(1)} fusion(bf16[512,8,273]{0,2,1:T(8,128)(2,1)S(1)} %get-tuple-element.192, f32[8,273,128]{2,1,0:T(8,128)} %get-tuple-element.130), kind=kOutput, calls=%fused_computation.76 | convolution fusion | flops 288218112 | bytes 5451776 | tf_op jit(solution)/shard_map/thf,hfd->thd/dot_general | solution.py:53
  208.9 3.1 %fusion.18 = bf16[512,8,128]{0,2,1:T(8,128)(2,1)S(1)} fusion(f32[8,128,512]{2,1,0:T(8,128)S(1)} %copy-done.18, f32[8,128,512]{2,1,0:T(8,128)S(1)} %fusion.65, f32[8,128,512]{2,1,0:T(8,128)S(1)} %fusion.57, f32[8,128,512]{2,1,0:T(8,128)S(1)} %fusion.59, f32[8,512,512]{1,2,0:T(8,128)S(1)} %bitcast.171, f32[8,512]{1,0:T(8,128)S(1)} %copy-done.16, ...), kind=kOutput, calls=%fused_computation.30 | convolution fusion | flops 548929536 | bytes 19185664 | tf_op jit(solution)/shard_map/hqk,khd->qhd/dot_general | solution.py:103
  (101 shorter events, 19.6 us)
Async XLA Ops:
  6.5 89.7 %copy-start = (bf16[512,1024]{1,0:T(8,128)(2,1)S(1)}, bf16[512,1024]{1,0:T(8,128)(2,1)}, u32[]{:S(2)}) copy-start(bf16[512,1024]{1,0:T(8,128)(2,1)} %param.12) | copy-start | bytes 3145732
  6.5 10.2 %copy-start.13 = (bf16[512,128]{1,0:T(8,128)(2,1)S(1)}, bf16[512,128]{1,0:T(8,128)(2,1)}, u32[]{:S(2)}) copy-start(bf16[512,128]{1,0:T(8,128)(2,1)} %param.9) | copy-start | bytes 393220
  6.5 157.9 %all-gather.5.cloned.1.call-start = ((), (), s32[]{:S(2)}) async-start(), calls=%async_computation | async-start | bytes 10063872 | tf_op jit(solution)/shard_map/all_gather | solution.py:18
  8.2 16.4 %collective-permute-start = (bf16[64,1024]{1,0:T(8,128)(2,1)}, bf16[64,1024]{1,0:T(8,128)(2,1)}, u32[]{:S(2)}, u32[]{:S(2)}) collective-permute-start(bf16[64,1024]{1,0:T(8,128)(2,1)} %slice.32), channel_id=1, source_target_pairs={{0,2},{2,4},{4,6},{6,8},{8,10},{10,12},{12,14},{1,3},{3,5},{5,7},{... | collective-permute-start | bytes 393224 | tf_op jit(solution)/shard_map/ppermute | solution.py:13
  16.7 2.8 %copy-start.14 = (f32[512,8]{0,1:T(8,128)S(1)}, f32[512,8]{0,1:T(8,128)}, u32[]{:S(2)}) copy-start(f32[512,8]{0,1:T(8,128)} %param.14) | copy-start | bytes 49156
  16.7 4.5 %copy-start.17 = (f32[3,1024]{1,0:T(4,128)S(1)}, f32[3,1024]{1,0:T(4,128)}, u32[]{:S(2)}) copy-start(f32[3,1024]{1,0:T(4,128)} %param.15) | copy-start | bytes 36868
  21.2 4.4 %copy-start.5 = (bf16[512,1024]{1,0:T(8,128)(2,1)S(1)}, bf16[512,1024]{1,0:T(8,128)(2,1)}, u32[]{:S(2)}) copy-start(bf16[512,1024]{1,0:T(8,128)(2,1)} %param.11) | copy-start | bytes 3145732
  24.5 4.5 %copy-start.3 = (bf16[512,8,273]{0,2,1:T(8,128)(2,1)}, bf16[512,8,273]{0,2,1:T(8,128)(2,1)S(1)}, u32[]{:S(2)}) copy-start(bf16[512,8,273]{0,2,1:T(8,128)(2,1)S(1)} %get-tuple-element.191) | copy-start | bytes 6709252
  25.7 2.1 copy-start.6
  26.6 2.5 %copy-start.8 = (bf16[64,8,8,128]{3,2,1,0:T(8,128)(2,1)}, bf16[64,8,8,128]{3,2,1,0:T(8,128)(2,1)S(1)}, u32[]{:S(2)}) copy-start(bf16[64,8,8,128]{3,2,1,0:T(8,128)(2,1)S(1)} %fusion.45) | copy-start | bytes 3145732
  33.1 63.1 %collective-permute-start.1 = (bf16[64,1024]{1,0:T(8,128)(2,1)}, bf16[64,1024]{1,0:T(8,128)(2,1)}, u32[]{:S(2)}, u32[]{:S(2)}) collective-permute-start(bf16[64,1024]{1,0:T(8,128)(2,1)} %slice.39), channel_id=1, source_target_pairs={{0,2},{2,4},{4,6},{6,8},{8,10},{10,12},{12,14},{1,3},{3,5},{5,7},{... | collective-permute-start | bytes 393224 | tf_op jit(solution)/shard_map/ppermute | solution.py:13
  36.6 3.9 %copy-start.4 = (bf16[512,8,273]{0,2,1:T(8,128)(2,1)S(1)}, bf16[512,8,273]{0,2,1:T(8,128)(2,1)}, u32[]{:S(2)}) copy-start(bf16[512,8,273]{0,2,1:T(8,128)(2,1)} %copy-done.3) | copy-start | bytes 6709252
  36.7 5.2 %copy-start.11 = (pred[512,512]{0,1:T(8,128)(4,1)}, pred[512,512]{0,1:T(8,128)(4,1)S(1)}, u32[]{:S(2)}) copy-start(pred[512,512]{0,1:T(8,128)(4,1)S(1)} %iota_compare_fusion.1) | copy-start | bytes 786436
  36.8 5.1 %copy-start.15 = (f32[8,512]{1,0:T(8,128)}, f32[8,512]{1,0:T(8,128)S(1)}, u32[]{:S(2)}) copy-start(f32[8,512]{1,0:T(8,128)S(1)} %add_bitcast_fusion.1) | copy-start | bytes 49156
  96.2 2.7 %copy-start.10 = (pred[512,576]{0,1:T(8,128)(4,1)S(1)}, pred[512,576]{0,1:T(8,128)(4,1)}, u32[]{:S(2)}) copy-start(pred[512,576]{0,1:T(8,128)(4,1)} %fusion.44) | copy-start | bytes 884740
  99.0 6.7 %copy-start.7 = (bf16[576,1024]{1,0:T(8,128)(2,1)S(1)}, bf16[576,1024]{1,0:T(8,128)(2,1)}, u32[]{:S(2)}) copy-start(bf16[576,1024]{1,0:T(8,128)(2,1)} %copy-done.6) | copy-start | bytes 3538948
  201.8 2.5 %copy-start.2 = (f32[8,273,128]{2,1,0:T(8,128)S(1)}, f32[8,273,128]{2,1,0:T(8,128)}, u32[]{:S(2)}) copy-start(f32[8,273,128]{2,1,0:T(8,128)} %get-tuple-element.130) | copy-start | bytes 3354628
  204.3 2.9 %slice-start = ((s8[8388608]{0:T(1024)(128)(4,1)}), s8[4194304]{0:T(1024)(128)(4,1)S(1)}, s32[]{:S(2)}) async-start(s8[8388608]{0:T(1024)(128)(4,1)} %bitcast.170), calls=%async_computation.1 | async-start | bytes 8388608
  205.1 2.9 %slice-start.1 = ((s8[8388608]{0:T(1024)(128)(4,1)}), s8[4194304]{0:T(1024)(128)(4,1)S(1)}, s32[]{:S(2)}) async-start(s8[8388608]{0:T(1024)(128)(4,1)} %bitcast.170), calls=%async_computation.2 | async-start | bytes 8388608
  206.4 1.8 copy-start.9
  206.4 1.8 copy-start.12
  206.4 1.8 copy-start.16
  206.4 2.6 %copy-start.18 = (f32[8,128,512]{2,1,0:T(8,128)S(1)}, f32[8,128,512]{2,1,0:T(8,128)}, u32[]{:S(2)}) copy-start(f32[8,128,512]{2,1,0:T(8,128)} %fusion.10) | copy-start | bytes 6291460
  208.9 4.4 %copy-start.1 = (bf16[512,1024]{1,0:T(8,128)(2,1)S(1)}, bf16[512,1024]{1,0:T(8,128)(2,1)}, u32[]{:S(2)}) copy-start(bf16[512,1024]{1,0:T(8,128)(2,1)} %param.12) | copy-start | bytes 3145732
Sparse Core Ops, SparseCore 0:
  31.7 132.6 all-gather.4
where the time goes:
time: 221 us; the launch traced here: 220 us
  waiting for transfers between devices  52.6 us (24%)
  blocking collectives  48.5 us (22%)
  other arithmetic  39.2 us (18%)
  matrix products  30.8 us (14%)
  local copies, waits for them, and re-layouts  26.4 us (12%)
  between operations  13.7 us (6%)
  starting transfers between devices  8.95 us (4%)
    all_gather x1, waiting for transfers between devices, prefix(): pieces = jax.tree.map(lambda part: lax.all_gather(part, axis), value)  52.6 us
    all_gather x2, blocking collectives, prefix(): pieces = jax.tree.map(lambda part: lax.all_gather(part, axis), value)  48.5 us
    select_n x14, other arithmetic, hop(): jnp.where(position < mine, new, old)  21.1 us
    dynamic_slice x7, local copies, waits for them, and re-layouts, hop(): longer = join(so_far, jax.tree.map(lambda part: part[position], pieces))  16.2 us
    dot_general x12, matrix products, divided_product(): term = jnp.einsum(form, narrow, piece, preferred_element_type=jnp.float32)  13.1 us
    ppermute x2, starting transfers between devices, passed_along(): return lax.ppermute(block, axis, route)  8.95 us
    sub x1, other arithmetic, local(): weights = jnp.exp(win_scores - top)  6.71 us
    dot_general x1, matrix products, local(): jnp.einsum('hqk,khd->qhd', probs, win_values, preferred_element_type=jnp....  6.18 us
  transfers between devices with their start and end apart: 3, of which 1 were waited for; matrix products, arithmetic and copies ran while one was open for 18% of the time, Pallas kernels for 0%

commit v1 on v0

v1 whole, which is shorter than its diff:
```python
import numpy as np
import jax
import jax.numpy as jnp
from jax import lax
from jax.experimental import pallas as pl
from jax.experimental.pallas import tpu as pltpu
from jax.sharding import PartitionSpec as P

WINDOW = 64
ROWS = 160
MISC = 157
LOG2E = float(np.log2(np.e))
F32 = jnp.float32
BF16 = jnp.bfloat16
VMEM_LIMIT = 48 * 1024 * 1024


def feature_tables(width):
    first = -np.ones(ROWS, np.int32)
    second = -np.ones(ROWS, np.int32)
    scale = np.zeros(ROWS, np.float32)
    twice = np.ones(ROWS, np.float32)
    scale[0] = 1.0
    at = 1
    for i in range(width):
        first[at], scale[at] = i, width ** (-0.25)
        at += 1
    for i in range(width):
        for j in range(i, width):
            first[at], second[at], scale[at] = i, j, (2.0 * width) ** (-0.5)
            twice[at] = 1.0 if i == j else 2.0
            at += 1
    one_a = ((first < 0) & (scale > 0)).astype(np.float32)
    one_b = ((second < 0) & (scale > 0)).astype(np.float32)
    return first, second, one_a, one_b, scale, twice


def key_tables(width):
    first, second, one_a, one_b, scale, _ = feature_tables(width)
    lanes = lambda column: np.repeat(column[:, None], 128, axis=1)
    index = np.stack([lanes(np.where(first < 0, -1000, first)), lanes(np.where(second < 0, -1000, second))])
    real = np.stack([lanes(one_a), lanes(one_b), lanes(scale)])
    return jnp.asarray(index, jnp.int32), jnp.asarray(real, F32)


def query_tables(width):
    first, second, one_a, one_b, scale, twice = feature_tables(width)

    def row(values, fill):
        wide = np.full((1, 256), fill, np.float32)
        wide[0, :ROWS] = values
        return wide

    index = np.concatenate(
        [row(np.where(first < 0, -1000, first), -1000), row(np.where(second < 0, -1000, second), -1000)]
        + [np.full((6, 256), -1000, np.float32)]
    )
    real = np.concatenate([row(one_a, 0), row(one_b, 0), row(scale * twice, 0), np.zeros((5, 256), np.float32)])
    return jnp.asarray(index, jnp.int32), jnp.asarray(real, F32)


def nt(a, b):
    return lax.dot_general(a, b, (((1,), (1,)), ((), ())), preferred_element_type=F32)


def nn(a, b):
    return lax.dot_general(a, b, (((1,), (0,)), ((), ())), preferred_element_type=F32)


def tn(a, b):
    return lax.dot_general(a, b, (((0,), (0,)), ((), ())), preferred_element_type=F32)


def parts(wide):
    upper = wide.astype(BF16)
    rest = wide - upper.astype(F32)
    middle = rest.astype(BF16)
    lower = (rest - middle.astype(F32)).astype(BF16)
    return upper, middle, lower


def iota(shape, dim):
    return lax.broadcasted_iota(jnp.int32, shape, dim)


def cumulative_rows(gates):
    rows = gates.shape[0]
    upto = (iota((rows, rows), 0) <= iota((rows, rows), 1)).astype(BF16)
    return sum(tn(piece, upto) for piece in parts(gates))


def cumulative_columns(gates):
    rows = gates.shape[0]
    upto = (iota((rows, rows), 1) <= iota((rows, rows), 0)).astype(BF16)
    return sum(nn(upto, piece) for piece in parts(gates))


def tile4(table, count):
    return jnp.concatenate([table] * count, axis=1)


def shifted(x, by):
    return jnp.where(iota(x.shape, 0) < by, 0.0, pltpu.roll(x, by, 0))


def state_kernel(order, quarter_heads, group_ref, k_ref, v_ref, g_ref, w_ref, index_ref, real_ref, *refs):
    outs, (cum_ref, norm_ref) = refs[: len(order)], refs[len(order) :]
    rows, wide = k_ref.shape
    heads = g_ref.shape[1]
    width = wide // heads
    k = k_ref[...]
    cum_ref[...] = cumulative_rows(g_ref[...])
    norm_ref[...] = jnp.zeros(norm_ref.shape, F32)
    lane = iota((ROWS, wide), 1)
    lane1 = iota((1, 128), 1)
    sub = iota((8, 128), 0)
    one_a, one_b, scale = (tile4(real_ref[i], rows // 128) for i in range(3))
    keys8 = k[0:16].astype(F32)[0:8]
    for out_ref, distance in zip(outs, order):
        quarter = group_ref[0] ^ distance
        for j in range(quarter_heads):
            head = quarter * quarter_heads + j
            at = pl.ds(pl.multiple_of(head * 128, 128), 128)
            pick_a = (lane == index_ref[0] + head * width).astype(BF16)
            pick_b = (lane == index_ref[1] + head * width).astype(BF16)
            cum = cum_ref[pl.ds(head, 1), :]
            last = cum[:, rows - 1 :]
            keep = jnp.exp(last - cum)
            phi = (((nt(pick_a, k) + one_a) * (nt(pick_b, k) + one_b) * scale) * keep).astype(BF16)
            v = v_ref[:, at].astype(F32)
            w = w_ref[:, at]
            conv = (w[0:1] * v + w[1:2] * shifted(v, 1) + w[2:3] * shifted(v, 2)).astype(BF16)
            state = nn(phi, conv)
            norm_ref[:, 0:ROWS] = nt(jnp.ones((8, rows), BF16), phi)
            norm = norm_ref[0:1, :]
            high = norm.astype(BF16).astype(F32)
            low = norm - high
            turned = pltpu.roll(keys8, (wide - head * width) % wide, 1)
            turned2 = pltpu.roll(keys8, (wide - head * width + width) % wide, 1)
            misc = jnp.where(lane1 < width, turned[0:1], 0.0)
            misc = jnp.where((lane1 >= width) & (lane1 < 2 * width), turned2[1:2], misc)
            place = 2 * width
            for value in (keep[:, 0:1], keep[:, 1:2], jnp.exp(last)):
                for piece in parts(value):
                    misc = jnp.where(lane1 == place, piece.astype(F32), misc)
                    place += 1
            tail = state[ROWS - 8 :]
            for row, line in enumerate((high[:, :128], high[:, 128:], low[:, :128], low[:, 128:], misc)):
                tail = jnp.where(sub == row + 1, line, tail)
            tail = jnp.where(sub >= 6, v[rows - 8 :], tail)
            out_ref[j, 0 : ROWS - 16, :] = state[: ROWS - 16].astype(BF16)
            out_ref[j, ROWS - 16 :, :] = jnp.concatenate([state[ROWS - 16 : ROWS - 8], tail]).astype(BF16)


class Element:
    def __init__(self, tile, width):
        self.tile = tile
        self.width = width
        tail = tile[ROWS - 8 :]
        misc = tail[5:6]
        lane1 = iota((1, 128), 1)
        place = 2 * width

        def value(i):
            here = (lane1 >= place + 3 * i) & (lane1 < place + 3 * i + 3)
            return jnp.sum(jnp.where(here, misc, 0.0), axis=1, keepdims=True)

        self.misc = misc
        self.enter = (value(0), value(1))
        self.decay = value(2)
        self.last = (tail[6:7], tail[7:8])


def first_keys(miscs, index_ref, real_ref, width):
    lane = iota((ROWS, 128), 1)
    rows = jnp.concatenate(miscs + [jnp.zeros((8 - len(miscs), 128), F32)] if len(miscs) < 8 else miscs).astype(BF16)
    one_a, one_b, scale = (real_ref[i][:, 0:8] for i in range(3))
    found = []
    for token in range(2):
        pick_a = (lane == index_ref[0] + token * width).astype(BF16)
        pick_b = (lane == index_ref[1] + token * width).astype(BF16)
        found.append((nt(pick_a, rows) + one_a) * (nt(pick_b, rows) + one_b) * scale)
    return found


def merge(left, right, columns, w):
    before, last = left.last
    carry0 = w[1:2] * last + w[2:3] * before
    carry1 = w[2:3] * last
    enter0, enter1 = right.enter
    joined = right.decay * left.tile + right.tile
    joined = joined + columns[0] * (enter0 * carry0) + columns[1] * (enter1 * carry1)
    sub = iota((8, 128), 0)
    lane1 = iota((1, 128), 1)
    misc = jnp.where(lane1 < 2 * left.width, left.misc, left.misc * right.decay)
    tail = jnp.where(sub == 5, misc, joined[ROWS - 8 :])
    tail = jnp.where(sub >= 6, right.tile[ROWS - 8 :], tail)
    return Element(jnp.concatenate([joined[: ROWS - 8], tail]), left.width)


def packed(tile, width):
    tail = tile[ROWS - 8 :]
    sub = iota((8, 128), 0)
    lane1 = iota((1, 128), 1)
    for row in (1, 2):
        norm = tail[row : row + 1] + tail[row + 2 : row + 3]
        high = norm.astype(BF16).astype(F32)
        tail = jnp.where(sub == row, high, jnp.where(sub == row + 2, norm - high, tail))
    misc = tail[5:6]
    place = 2 * width
    fresh = jnp.where(lane1 < place, misc, 0.0)
    for i in range(3):
        here = (lane1 >= place) & (lane1 < place + 3)
        value = jnp.sum(jnp.where(here, misc, 0.0), axis=1, keepdims=True)
        for piece in parts(value):
            fresh = jnp.where(lane1 == place, piece.astype(F32), fresh)
            place += 1
    tail = jnp.where(sub == 5, fresh, tail)
    return jnp.concatenate([tile[: ROWS - 8], tail]).astype(BF16)


def group_kernel(width, group_ref, w_ref, index_ref, real_ref, x0, x1, x2, x3, total_ref, before_ref, held):
    group = group_ref[0]
    count = x0.shape[0]
    for distance, ref in enumerate((x0, x1, x2, x3)):
        held[group ^ distance] = ref[...]
    elements = [[Element(held[p, j].astype(F32), width) for j in range(count)] for p in range(4)]
    columns = first_keys([elements[p][j].misc for p in range(4) for j in range(count)], index_ref, real_ref, width)
    for j in range(count):
        w = w_ref[:, pl.ds(pl.multiple_of((group * count + j) * 128, 128), 128)]
        so_far = elements[0][j]
        for p in range(1, 4):
            before_ref[p - 1, j] = so_far.tile
            pick = p * count + j
            so_far = merge(so_far, elements[p][j], [c[:, pick : pick + 1] for c in columns], w)
        total_ref[j] = packed(so_far.tile, width)


def pair_kernel(width, group_ref, w_ref, index_ref, real_ref, left_ref, right_ref, out_ref):
    count = left_ref.shape[0]
    group = group_ref[0]
    rights = [Element(right_ref[j].astype(F32), width) for j in range(count)]
    columns = first_keys([right.misc for right in rights], index_ref, real_ref, width)
    for j in range(count):
        w = w_ref[:, pl.ds(pl.multiple_of((group * count + j) * 128, 128), 128)]
        left = Element(left_ref[j].astype(F32), width)
        out_ref[j] = packed(merge(left, rights[j], [c[:, j : j + 1] for c in columns], w).tile, width)


def spread_kernel(width, group_ref, w_ref, index_ref, real_ref, base_ref, before_ref, o0, o1, o2, o3, held):
    group = group_ref[0]
    live = group_ref[1] > 0
    count = base_ref.shape[0]
    for j in range(count):
        w = w_ref[:, pl.ds(pl.multiple_of((group * count + j) * 128, 128), 128)]
        base = Element(jnp.where(live, base_ref[j].astype(F32), 0.0), width)
        held[0, j] = base.tile.astype(BF16)
        rights = [Element(before_ref[p, j], width) for p in range(3)]
        columns = first_keys([right.misc for right in rights], index_ref, real_ref, width)
        for p in range(3):
            held[p + 1, j] = packed(merge(base, rights[p], [c[:, p : p + 1] for c in columns], w).tile, width)
    for distance, ref in enumerate((o0, o1, o2, o3)):
        ref[...] = held[group ^ distance]


def block_kernel(edge_ref, q_ref, k_ref, v_ref, wq_ref, wk_ref, g_ref, w_ref, pk_ref, pv_ref, num_ref, den_ref, win_ref):
    rows, wide = q_ref.shape
    heads = g_ref.shape[1]
    width = wide // heads
    q = q_ref[...]
    k = k_ref[...]
    gates = g_ref[...]
    cum_row = cumulative_rows(gates) * LOG2E
    cum_col = cumulative_columns(gates) * LOG2E
    lane = iota(k.shape, 1)
    step = 128
    ones = jnp.ones((rows, 128), BF16)
    causal = iota((step, step), 0) >= iota((step, step), 1)
    half = WINDOW
    seen = iota((half, 2 * half), 1)
    mine = iota((half, 2 * half), 0)
    valid = (seen > mine) & (seen <= mine + half)
    first_valid = valid & ((seen >= half) | (edge_ref[0] > 0))
    for h in range(heads):
        at = slice(128 * h, 128 * h + 128)
        k_here = jnp.where((lane >= h * width) & (lane < (h + 1) * width), k, jnp.zeros_like(k)) * BF16(0.25)
        v = v_ref[:, at]
        prev = pv_ref[:, at]
        v32 = v.astype(F32)
        ahead = jnp.concatenate([prev[WINDOW - 16 :].astype(F32)[8:], v32])
        w = w_ref[:, at]
        conv = w[0:1] * v32 + w[1:2] * pltpu.roll(ahead, 1, 0)[8:] + w[2:3] * pltpu.roll(ahead, 2, 0)[8:]
        right = jnp.concatenate([conv.astype(BF16), ones], axis=1)
        for i in range(rows // step):
            here = slice(i * step, (i + 1) * step)
            upto = (i + 1) * step
            x = nt(q[here], k_here[:upto])
            diff = cum_col[here, h : h + 1] - cum_row[h : h + 1, :upto]
            if i:
                masked = jnp.where(causal, diff[:, i * step :], -jnp.inf)
                diff = jnp.concatenate([diff[:, : i * step], masked], axis=1)
            else:
                diff = jnp.where(causal, diff, -jnp.inf)
            score = ((0.5 * x + 1.0) * x + 1.0) * jnp.exp2(diff)
            both = nn(score.astype(BF16), right[:upto])
            num_ref[here, at] = both[:, :128]
            den_ref[here, at] = both[:, 128:]
        keys = jnp.concatenate([pk_ref[:, at], wk_ref[:, at]])
        vals = jnp.concatenate([jnp.concatenate([prev, v]), jnp.ones((rows + WINDOW, 128), BF16)], axis=1)
        for i in range(rows // half):
            here = slice(i * half, (i + 1) * half)
            span = slice(i * half, (i + 2) * half)
            s = nt(wq_ref[here, at], keys[span]) * (128 ** (-0.5) * LOG2E)
            s = jnp.where(first_valid if i == 0 else valid, s, -jnp.inf)
            p = jnp.exp2(s - jnp.max(s, axis=1, keepdims=True)).astype(BF16)
            both = nn(p, vals[span])
            win_ref[here, at] = both[:, :128] / both[:, 128:]


def finish_kernel(group_ref, q_ref, g_ref, index_ref, real_ref, x0, x1, x2, x3, num_ref, den_ref, win_ref, out_ref, held):
    group = group_ref[0]
    rows, wide = q_ref.shape
    heads = g_ref.shape[1]
    width = wide // heads
    count = x0.shape[0]
    for distance, ref in enumerate((x0, x1, x2, x3)):
        held[group ^ distance] = ref[...]
    q = q_ref[...]
    enter = jnp.exp(cumulative_columns(g_ref[...]))
    row = iota((wide, 256), 0)
    one_a, one_b, scale = (real_ref[i : i + 1] for i in range(3))
    for h in range(heads):
        at = slice(128 * h, 128 * h + 128)
        pick_a = (row == index_ref[0:1] + h * width).astype(BF16)
        pick_b = (row == index_ref[1:2] + h * width).astype(BF16)
        phi = ((nn(q, pick_a) + one_a) * (nn(q, pick_b) + one_b) * scale).astype(BF16)
        tile = held[h // count, h % count]
        tail = tile[ROWS - 16 :].astype(F32)[8:]
        high = jnp.concatenate([tail[1:2], tail[2:3]], axis=1)
        low = jnp.concatenate([tail[3:4], tail[4:5]], axis=1)
        norm = nt(phi, jnp.broadcast_to(high, (128, 256)).astype(BF16)) + nt(
            phi, jnp.broadcast_to(low, (128, 256)).astype(BF16)
        )
        add = nn(phi[:, :ROWS], tile)
        e = enter[:, h : h + 1]
        num = num_ref[:, at] + e * add
        den = den_ref[:, at] + e * norm
        out_ref[:, at] = (num / den + win_ref[:, at]).astype(BF16)


def call(kernel, inputs, outs, scratch=(), smem=(0,)):
    where = [pl.BlockSpec(memory_space=pltpu.SMEM if i in smem else pltpu.VMEM) for i in range(len(inputs))]
    return pl.pallas_call(
        kernel,
        out_shape=outs,
        in_specs=where,
        out_specs=jax.tree.map(lambda _: pl.BlockSpec(memory_space=pltpu.VMEM), outs),
        scratch_shapes=scratch,
        compiler_params=pltpu.CompilerParams(vmem_limit_bytes=VMEM_LIMIT),
    )(*inputs)


def local(count, q_feat, k_feat, values, win_query, win_key, log_gates, conv_weight):
    rows = values.shape[0]
    heads = log_gates.shape[1]
    width = q_feat.shape[1] // heads
    quarter = heads // 4
    position = lax.axis_index("seq")
    group = (position % 4).astype(jnp.int32)
    one = lambda *numbers: jnp.stack([jnp.asarray(n, jnp.int32) for n in numbers])
    k_index, k_real = key_tables(width)
    q_index, q_real = query_tables(width)

    def swap(x, distance):
        return lax.ppermute(x, "seq", [(i, i ^ distance) for i in range(count)])

    def states(order):
        shape = jax.ShapeDtypeStruct((quarter, ROWS, 128), BF16)
        return call(
            lambda *refs: state_kernel(order, quarter, *refs),
            (one(group), k_feat, values, log_gates, conv_weight, k_index, k_real),
            [shape] * len(order),
            [pltpu.VMEM((heads, rows), F32), pltpu.VMEM((8, 256), F32)],
        )

    sent = states((1, 2, 3))
    (own,) = states((0,))
    others = [swap(x, d) for d, x in zip((1, 2, 3), sent)]
    shape = jax.ShapeDtypeStruct((quarter, ROWS, 128), BF16)
    total, before = call(
        lambda *refs: group_kernel(width, *refs),
        (one(group), conv_weight, k_index, k_real, own, *others),
        [shape, jax.ShapeDtypeStruct((3, quarter, ROWS, 128), F32)],
        [pltpu.VMEM((4, quarter, ROWS, 128), BF16)],
    )
    base = jnp.zeros_like(total)
    live = position < 0
    distance = 4
    while distance < count:
        got = swap(total, distance)
        upper = (position & distance) > 0
        if distance == 4:
            base = got
            live = upper
        else:
            pair = lambda left, right: call(
                lambda *refs: pair_kernel(width, *refs), (one(group), conv_weight, k_index, k_real, left, right), shape
            )
            base = jnp.where(upper, jnp.where(live, pair(got, base), got), base)
            live = live | upper
        if 2 * distance < count:
            lower_half = jnp.where(upper, got, total)
            upper_half = jnp.where(upper, total, got)
            total = call(
                lambda *refs: pair_kernel(width, *refs),
                (one(group), conv_weight, k_index, k_real, lower_half, upper_half),
                shape,
            )
        distance *= 2
    here, *sent = call(
        lambda *refs: spread_kernel(width, *refs),
        (one(group, live), conv_weight, k_index, k_real, base, before),
        [shape] * 4,
        [pltpu.VMEM((4, quarter, ROWS, 128), BF16)],
    )
    prefixes = [here] + [swap(x, d) for d, x in zip((1, 2, 3), sent)]

    shift = [(i, i + 1) for i in range(count - 1)]
    prev_key, prev_value = lax.ppermute((win_key[rows - WINDOW :], values[rows - WINDOW :]), "seq", shift)
    flat = jax.ShapeDtypeStruct(values.shape, F32)
    num, den, win = call(
        block_kernel,
        (one(position > 0), q_feat, k_feat, values, win_query, win_key, log_gates, conv_weight, prev_key, prev_value),
        [flat, flat, flat],
    )
    return call(
        finish_kernel,
        (one(group), q_feat, log_gates, q_index, q_real, *prefixes, num, den, win),
        jax.ShapeDtypeStruct(values.shape, BF16),
        [pltpu.VMEM((4, quarter, ROWS, 128), BF16)],
    )


def solution(mesh):
    rows = P(("grp", "seq"), "head")
    count = mesh.shape["seq"]
    return jax.shard_map(
        lambda *args: local(count, *args),
        mesh=mesh,
        in_specs=(rows,) * 6 + (P(None, "head"),),
        out_specs=rows,
        check_vma=False,
    )
```

time: 221 us -> 66 us (0.30)
  waiting for transfers between devices: 52.6 us -> 2.7 us
  blocking collectives: 48.5 us -> 0 us
  other arithmetic: 39.2 us -> 0.07 us
  Pallas kernels: 0 us -> 33.8 us
  matrix products: 30.8 us -> 0 us
  local copies, waits for them, and re-layouts: 26.4 us -> 10.7 us
  between operations: 13.7 us -> 0.19 us
  starting transfers between devices: 8.95 us -> 18.1 us
    all_gather x1 -> x0, waiting for transfers between devices: 52.6 us -> none  [prefix(): pieces = jax.tree.map(lambda part: lax.all_gather(part, axis), value)]
    all_gather x2 -> x0, blocking collectives: 48.5 us -> none  [prefix(): pieces = jax.tree.map(lambda part: lax.all_gather(part, axis), value)]
    pallas_call x0 -> x6, Pallas kernels: none -> 33.8 us  [call(): pl.pallas_call(kernel, out_shape=outs, in_specs=where, out_specs=jax.tree...]
    dot_general x16 -> x0, matrix products: 30.8 us -> none  [the longest x12 13.1 us: divided_product(): term = jnp.einsum(form, narrow, piece, preferred_element_type=jnp.float32)]
    select_n x14 -> x0, other arithmetic: 21.1 us -> none  [hop(): jnp.where(position < mine, new, old)]
    dynamic_slice x7 -> x0, local copies, waits for them, and re-layouts: 16.2 us -> none  [hop(): longer = join(so_far, jax.tree.map(lambda part: part[position], pieces))]
    ppermute x2 -> x9, starting transfers between devices: 8.95 us -> 18.1 us  [the longest x7 10.7 us: swap(): return lax.ppermute(x, 'seq', [(i, i ^ distance) for i in range(count)])]
    sub x2 -> x0, other arithmetic: 6.71 us -> none  [the longest x1 6.71 us: local(): weights = jnp.exp(win_scores - top)]
  transfers between devices with their start and end apart: 3 -> 9, of which waited for: 1 -> 1; matrix products, arithmetic and copies ran while one was open for 18% -> 4% of each run, Pallas kernels for 0% -> 37%
where the time goes in v1:
time: 66 us; the launch traced here: 65.6 us
  Pallas kernels  33.8 us (51%)
  starting transfers between devices  18.1 us (27%)
  local copies, waits for them, and re-layouts  10.7 us (16%)
  waiting for transfers between devices  2.7 us (4%)
    pallas_call x6, Pallas kernels, call(): pl.pallas_call(kernel, out_shape=outs, in_specs=where, out_specs=jax.tree...  33.8 us
    ppermute x7, starting transfers between devices, swap(): return lax.ppermute(x, 'seq', [(i, i ^ distance) for i in range(count)])  10.7 us
    unnamed x33, local copies, waits for them, and re-layouts  8.42 us
    ppermute x2, starting transfers between devices, local(): lax.ppermute((win_key[rows - WINDOW:], values[rows - WINDOW:]), 'seq', sh...  7.41 us
    ppermute x7, waiting for transfers between devices, swap(): return lax.ppermute(x, 'seq', [(i, i ^ distance) for i in range(count)])  2.7 us
    slice x1, local copies, waits for them, and re-layouts, local(): win_key[rows - WINDOW:]  1.57 us
  transfers between devices with their start and end apart: 9, of which 1 were waited for; matrix products, arithmetic and copies ran while one was open for 4% of the time, Pallas kernels for 37%

profile of v1, /device:TPU:0, one launch (start us, length us, event | category | flops | bytes accessed | tf_op | source)
XLA Modules:
  0.0 65.6 jit_solution(7026989247206362614)
XLA Ops:
  0.0 0.9 %copy.15.refs_3_.g_ref = f32[512,8]{1,0:T(8,128)S(1)} copy(f32[512,8]{0,1:T(8,128)} %param.16) | data formatting | bytes 32768 | tf_op args[5]
  0.9 0.0 copy-start
  0.9 1.2 %copy-done = bf16[512,1024]{1,0:T(8,128)(2,1)S(1)} copy-done((bf16[512,1024]{1,0:T(8,128)(2,1)S(1)}, bf16[512,1024]{1,0:T(8,128)(2,1)}, u32[]{:S(2)}) %copy-start) | copy-done | bytes 1048600
  2.1 0.9 %copy-done.2 = f32[3,160,128]{2,1,0:T(8,128)S(1)} copy-done((f32[3,160,128]{2,1,0:T(8,128)S(1)}, f32[3,160,128]{2,1,0:T(8,128)}, u32[]{:S(2)}) %copy-start.2) | copy-done | bytes 245784
  3.1 0.9 %copy-done.4 = s32[2,160,128]{2,1,0:T(8,128)S(1)} copy-done((s32[2,160,128]{2,1,0:T(8,128)S(1)}, s32[2,160,128]{2,1,0:T(8,128)}, u32[]{:S(2)}) %copy-start.4) | copy-done | bytes 163864
  4.0 0.9 %copy-done.8 = bf16[512,128]{1,0:T(8,128)(2,1)S(1)} copy-done((bf16[512,128]{1,0:T(8,128)(2,1)S(1)}, bf16[512,128]{1,0:T(8,128)(2,1)}, u32[]{:S(2)}) %copy-start.8) | copy-done | bytes 131096
  4.9 0.7 %copy-done.12 = f32[3,1024]{1,0:T(4,128)S(1)} copy-done((f32[3,1024]{1,0:T(4,128)S(1)}, f32[3,1024]{1,0:T(4,128)}, u32[]{:S(2)}) %copy-start.12) | copy-done | bytes 12312
  5.6 2.7 %shard_map.110 = (bf16[2,160,128]{2,1,0:T(8,128)(2,1)}, bf16[2,160,128]{2,1,0:T(8,128)(2,1)}, bf16[2,160,128]{2,1,0:T(8,128)(2,1)}) custom-call(s32[1]{0:T(128)} %bitcast.refs_0_.group_ref, bf16[512,128]{1,0:T(8,128)(2,1)S(1)} %copy-done.8, bf16[512,1024]{1,0:T(8,128)(2,1)S(1)} %copy-done, f32[512,8]{1,0:T(8,128)S(1)} %copy.15.refs_3_.g_ref, ...), custom_call_target="tpu_custom_call" | custom-call | tf_op jit(solution)/shard_map/pallas_call | solution.py:353
  8.3 3.0 %collective-permute-start = (bf16[2,160,128]{2,1,0:T(8,128)(2,1)}, bf16[2,160,128]{2,1,0:T(8,128)(2,1)S(1)}, u32[]{:S(2)}, u32[]{:S(2)}) collective-permute-start(bf16[2,160,128]{2,1,0:T(8,128)(2,1)} %get-tuple-element.17), channel_id=1, source_target_pairs={{0,2},{2,0},{4,6},{6,4},{8,10},{10,8},{12,14},{14,12},{1,3},{3,1},... | collective-permute-start | bytes 245768 | tf_op jit(solution)/shard_map/ppermute | solution.py:375
  11.3 1.6 %collective-permute-start.1 = (bf16[2,160,128]{2,1,0:T(8,128)(2,1)}, bf16[2,160,128]{2,1,0:T(8,128)(2,1)S(1)}, u32[]{:S(2)}, u32[]{:S(2)}) collective-permute-start(bf16[2,160,128]{2,1,0:T(8,128)(2,1)} %get-tuple-element.18), channel_id=1, source_target_pairs={{0,4},{2,6},{4,0},{6,2},{8,12},{10,14},{12,8},{14,10},{1,5},{3,7},... | collective-permute-start | bytes 245768 | tf_op jit(solution)/shard_map/ppermute | solution.py:375
  12.9 0.0 collective-permute-start.2
  12.9 0.7 %slice.7 = bf16[64,1024]{1,0:T(8,128)(2,1)} slice(bf16[512,1024]{1,0:T(8,128)(2,1)S(1)} %copy-done), slice={[448:512], [0:1024]} | slice | bytes 262144 | tf_op jit(solution)/shard_map/slice | solution.py:429
  13.5 3.8 %collective-permute-start.8 = (bf16[64,1024]{1,0:T(8,128)(2,1)}, bf16[64,1024]{1,0:T(8,128)(2,1)S(1)}, u32[]{:S(2)}, u32[]{:S(2)}) collective-permute-start(bf16[64,1024]{1,0:T(8,128)(2,1)} %slice.7), channel_id=1, source_target_pairs={{0,2},{2,4},{4,6},{6,8},{8,10},{10,12},{12,14},{1,3},{3,5},{5,7},{... | collective-permute-start | bytes 393224 | tf_op jit(solution)/shard_map/ppermute | solution.py:429
  17.4 1.6 %slice.6 = bf16[64,1024]{1,0:T(8,128)(2,1)} slice(bf16[512,1024]{1,0:T(8,128)(2,1)} %wk_ref.1), slice={[448:512], [0:1024]} | slice | bytes 262144 | tf_op jit(solution)/shard_map/slice | solution.py:429
  18.9 3.6 %collective-permute-start.7 = (bf16[64,1024]{1,0:T(8,128)(2,1)}, bf16[64,1024]{1,0:T(8,128)(2,1)S(1)}, u32[]{:S(2)}, u32[]{:S(2)}) collective-permute-start(bf16[64,1024]{1,0:T(8,128)(2,1)} %slice.6), channel_id=1, source_target_pairs={{0,2},{2,4},{4,6},{6,8},{8,10},{10,12},{12,14},{1,3},{3,5},{5,7},{... | collective-permute-start | bytes 393224 | tf_op jit(solution)/shard_map/ppermute | solution.py:429
  22.6 1.0 %shard_map.109.refs_4_ = bf16[2,160,128]{2,1,0:T(8,128)(2,1)S(1)} custom-call(s32[1]{0:T(128)} %bitcast.refs_0_.group_ref, bf16[512,128]{1,0:T(8,128)(2,1)S(1)} %copy-done.9, bf16[512,1024]{1,0:T(8,128)(2,1)S(1)} %copy-done.1, f32[512,8]{1,0:T(8,128)S(1)} %copy.15.refs_3_.g_ref, f32[3,1024]{1,0:T(4,128)S(1)} %copy-done.13, s32[2,160,128]{2,1,0:T(8,128)S(1)} %copy-done.5, ...), custom_call_target="tpu_custom_call" | custom-call | tf_op jit(solution)/shard_map/pallas_call | solution.py:353
  23.6 0.0 collective-permute-done.1.refs_6_
  23.6 1.5 %shard_map.111 = (bf16[2,160,128]{2,1,0:T(8,128)(2,1)S(1)}, f32[3,2,160,128]{3,2,1,0:T(8,128)S(1)}) custom-call(s32[1]{0:T(128)} %bitcast.refs_0_.group_ref, f32[3,1024]{1,0:T(4,128)S(1)} %copy-done.13, s32[2,160,128]{2,1,0:T(8,128)S(1)} %copy-done.5, f32[3,160,128]{2,1,0:T(8,128)S(1)} %copy-done.3, bf16[2,160,128]{2,1,0:T(8,128)(2,1)S(1)} %shard_map.109.refs_4_, ...), custom_call_target="tpu_custom_call" | custom-call | tf_op jit(solution)/shard_map/pallas_call | solution.py:353
  25.1 2.6 %collective-permute-start.3 = (bf16[2,160,128]{2,1,0:T(8,128)(2,1)S(1)}, bf16[2,160,128]{2,1,0:T(8,128)(2,1)S(1)}, u32[]{:S(2)}, u32[]{:S(2)}) collective-permute-start(bf16[2,160,128]{2,1,0:T(8,128)(2,1)S(1)} %get-tuple-element.20), channel_id=1, source_target_pairs={{0,8},{2,10},{4,12},{6,14},{8,0},{10,2},{12,4},{14,6},{1,9},{3,11}... | collective-permute-start | bytes 245768 | tf_op jit(solution)/shard_map/ppermute | solution.py:375
  27.8 0.1 pad_add_fusion.refs_0_
  27.9 2.7 %collective-permute-done.3.refs_4_ = bf16[2,160,128]{2,1,0:T(8,128)(2,1)S(1)} collective-permute-done((bf16[2,160,128]{2,1,0:T(8,128)(2,1)S(1)}, bf16[2,160,128]{2,1,0:T(8,128)(2,1)S(1)}, u32[]{:S(2)}, u32[]{:S(2)}) %collective-permute-start.3) | collective-permute-done | bytes 81952 | tf_op jit(solution)/shard_map/ppermute | solution.py:375
  30.5 2.1 %shard_map.112 = (bf16[2,160,128]{2,1,0:T(8,128)(2,1)S(1)}, bf16[2,160,128]{2,1,0:T(8,128)(2,1)}, bf16[2,160,128]{2,1,0:T(8,128)(2,1)}, bf16[2,160,128]{2,1,0:T(8,128)(2,1)S(1)}) custom-call(s32[2]{0:T(128)S(1)} %pad_add_fusion.refs_0_, f32[3,1024]{1,0:T(4,128)S(1)} %copy-done.13, s32[2,160,128]{2,1,0:T(8,128)S(1)} %copy-done.5, ...), custom_call_target="tpu_custom_call" | custom-call | tf_op jit(solution)/shard_map/pallas_call | solution.py:353
  32.6 1.5 %collective-permute-start.4 = (bf16[2,160,128]{2,1,0:T(8,128)(2,1)}, bf16[2,160,128]{2,1,0:T(8,128)(2,1)S(1)}, u32[]{:S(2)}, u32[]{:S(2)}) collective-permute-start(bf16[2,160,128]{2,1,0:T(8,128)(2,1)} %get-tuple-element.23), channel_id=1, source_target_pairs={{0,2},{2,0},{4,6},{6,4},{8,10},{10,8},{12,14},{14,12},{1,3},{3,1},... | collective-permute-start | bytes 245768 | tf_op jit(solution)/shard_map/ppermute | solution.py:375
  34.1 1.6 %collective-permute-start.5 = (bf16[2,160,128]{2,1,0:T(8,128)(2,1)}, bf16[2,160,128]{2,1,0:T(8,128)(2,1)S(1)}, u32[]{:S(2)}, u32[]{:S(2)}) collective-permute-start(bf16[2,160,128]{2,1,0:T(8,128)(2,1)} %get-tuple-element.24), channel_id=1, source_target_pairs={{0,4},{2,6},{4,0},{6,2},{8,12},{10,14},{12,8},{14,10},{1,5},{3,7},... | collective-permute-start | bytes 245768 | tf_op jit(solution)/shard_map/ppermute | solution.py:375
  35.7 0.4 collective-permute-start.6
  36.1 0.0 collective-permute-done.8.pv_ref
  36.1 0.0 collective-permute-done.7.pk_ref
  36.1 0.0 copy-start.10
  36.1 1.2 %copy-done.10 = bf16[512,1024]{1,0:T(8,128)(2,1)S(1)} copy-done((bf16[512,1024]{1,0:T(8,128)(2,1)S(1)}, bf16[512,1024]{1,0:T(8,128)(2,1)}, u32[]{:S(2)}) %copy-start.10) | copy-done | bytes 1048600
  37.3 19.9 %shard_map.113 = (f32[512,1024]{1,0:T(8,128)S(1)}, f32[512,1024]{1,0:T(8,128)}, f32[512,1024]{1,0:T(8,128)}) custom-call(s32[1]{0:T(128)} %bitcast.2.edge_ref, bf16[512,128]{1,0:T(8,128)(2,1)S(1)} %copy-done.11, bf16[512,128]{1,0:T(8,128)(2,1)S(1)} %copy-done.9, bf16[512,1024]{1,0:T(8,128)(2,1)S(1)} %copy-done.1, bf16[512,1024]{1,0:T(8,128)(2,1)S(1)} %copy-done.10, ...), custom_call_target="tpu_custom_call" | custom-call | tf_op jit(solution)/shard_map/pallas_call | solution.py:353
  57.3 1.6 %copy-done.6 = f32[512,1024]{1,0:T(8,128)S(1)} copy-done((f32[512,1024]{1,0:T(8,128)S(1)}, f32[512,1024]{1,0:T(8,128)}, u32[]{:S(2)}) %copy-start.6) | copy-done | bytes 2097176
  58.9 6.7 %shard_map.114 = bf16[512,1024]{1,0:T(8,128)(2,1)} custom-call(s32[1]{0:T(128)} %bitcast.refs_0_.group_ref, bf16[512,128]{1,0:T(8,128)(2,1)S(1)} %copy-done.11, f32[512,8]{1,0:T(8,128)S(1)} %copy.15.refs_3_.g_ref, s32[8,256]{1,0:T(8,128)S(1)} %copy-done.15, f32[8,256]{1,0:T(8,128)S(1)} %copy-done.14, bf16[2,160,128]{2,1,0:T(8,128)(2,1)S(1)} %get-tuple-element.22.x0, ...), custom_call_target="tpu_custom_call" | custom-call | tf_op jit(solution)/shard_map/pallas_call | solution.py:353
  (28 shorter events, 0.1 us)
Async XLA Ops:
  0.0 22.5 %copy-start.3 = (f32[3,160,128]{2,1,0:T(8,128)S(1)}, f32[3,160,128]{2,1,0:T(8,128)}, u32[]{:S(2)}) copy-start(f32[3,160,128]{2,1,0:T(8,128)} %constant.29.clone.refs_6_.refs_3_) | copy-start | bytes 737284
  0.0 22.5 %copy-start.13 = (f32[3,1024]{1,0:T(4,128)S(1)}, f32[3,1024]{1,0:T(4,128)}, u32[]{:S(2)}) copy-start(f32[3,1024]{1,0:T(4,128)} %w_ref.1) | copy-start | bytes 36868
  0.9 1.2 %copy-start = (bf16[512,1024]{1,0:T(8,128)(2,1)S(1)}, bf16[512,1024]{1,0:T(8,128)(2,1)}, u32[]{:S(2)}) copy-start(bf16[512,1024]{1,0:T(8,128)(2,1)} %v_ref.1) | copy-start | bytes 3145732
  2.1 0.9 %copy-start.2 = (f32[3,160,128]{2,1,0:T(8,128)S(1)}, f32[3,160,128]{2,1,0:T(8,128)}, u32[]{:S(2)}) copy-start(f32[3,160,128]{2,1,0:T(8,128)} %constant.29.clone.refs_6_.refs_3_) | copy-start | bytes 737284
  3.1 0.9 %copy-start.4 = (s32[2,160,128]{2,1,0:T(8,128)S(1)}, s32[2,160,128]{2,1,0:T(8,128)}, u32[]{:S(2)}) copy-start(s32[2,160,128]{2,1,0:T(8,128)} %constant.28.clone.refs_5_.refs_2_) | copy-start | bytes 491524
  4.0 0.9 %copy-start.8 = (bf16[512,128]{1,0:T(8,128)(2,1)S(1)}, bf16[512,128]{1,0:T(8,128)(2,1)}, u32[]{:S(2)}) copy-start(bf16[512,128]{1,0:T(8,128)(2,1)} %k_ref.1) | copy-start | bytes 393220
  4.9 0.7 %copy-start.12 = (f32[3,1024]{1,0:T(4,128)S(1)}, f32[3,1024]{1,0:T(4,128)}, u32[]{:S(2)}) copy-start(f32[3,1024]{1,0:T(4,128)} %w_ref.1) | copy-start | bytes 36868
  5.6 16.9 %copy-start.1 = (bf16[512,1024]{1,0:T(8,128)(2,1)S(1)}, bf16[512,1024]{1,0:T(8,128)(2,1)}, u32[]{:S(2)}) copy-start(bf16[512,1024]{1,0:T(8,128)(2,1)} %v_ref.1) | copy-start | bytes 3145732
  5.6 16.9 %copy-start.5 = (s32[2,160,128]{2,1,0:T(8,128)S(1)}, s32[2,160,128]{2,1,0:T(8,128)}, u32[]{:S(2)}) copy-start(s32[2,160,128]{2,1,0:T(8,128)} %constant.28.clone.refs_5_.refs_2_) | copy-start | bytes 491524
  5.6 17.0 %copy-start.9 = (bf16[512,128]{1,0:T(8,128)(2,1)S(1)}, bf16[512,128]{1,0:T(8,128)(2,1)}, u32[]{:S(2)}) copy-start(bf16[512,128]{1,0:T(8,128)(2,1)} %k_ref.1) | copy-start | bytes 393220
  8.3 15.2 %collective-permute-start = (bf16[2,160,128]{2,1,0:T(8,128)(2,1)}, bf16[2,160,128]{2,1,0:T(8,128)(2,1)S(1)}, u32[]{:S(2)}, u32[]{:S(2)}) collective-permute-start(bf16[2,160,128]{2,1,0:T(8,128)(2,1)} %get-tuple-element.17), channel_id=1, source_target_pairs={{0,2},{2,0},{4,6},{6,4},{8,10},{10,8},{12,14},{14,12},{1,3},{3,1},... | collective-permute-start | bytes 245768 | tf_op jit(solution)/shard_map/ppermute | solution.py:375
  11.3 12.3 %collective-permute-start.1 = (bf16[2,160,128]{2,1,0:T(8,128)(2,1)}, bf16[2,160,128]{2,1,0:T(8,128)(2,1)S(1)}, u32[]{:S(2)}, u32[]{:S(2)}) collective-permute-start(bf16[2,160,128]{2,1,0:T(8,128)(2,1)} %get-tuple-element.18), channel_id=1, source_target_pairs={{0,4},{2,6},{4,0},{6,2},{8,12},{10,14},{12,8},{14,10},{1,5},{3,7},... | collective-permute-start | bytes 245768 | tf_op jit(solution)/shard_map/ppermute | solution.py:375
  12.9 23.2 %copy-start.7 = (bf16[512,1024]{1,0:T(8,128)(2,1)S(1)}, bf16[512,1024]{1,0:T(8,128)(2,1)}, u32[]{:S(2)}) copy-start(bf16[512,1024]{1,0:T(8,128)(2,1)} %wk_ref.1) | copy-start | bytes 3145732
  12.9 23.3 %copy-start.11 = (bf16[512,128]{1,0:T(8,128)(2,1)S(1)}, bf16[512,128]{1,0:T(8,128)(2,1)}, u32[]{:S(2)}) copy-start(bf16[512,128]{1,0:T(8,128)(2,1)} %q_ref.3) | copy-start | bytes 393220
  12.9 10.7 %collective-permute-start.2 = (bf16[2,160,128]{2,1,0:T(8,128)(2,1)}, bf16[2,160,128]{2,1,0:T(8,128)(2,1)}, u32[]{:S(2)}, u32[]{:S(2)}) collective-permute-start(bf16[2,160,128]{2,1,0:T(8,128)(2,1)} %get-tuple-element.19), channel_id=1, source_target_pairs={{0,6},{2,4},{4,2},{6,0},{8,14},{10,12},{12,10},{14,8},{1,7},{3,5},... | collective-permute-start | bytes 245768 | tf_op jit(solution)/shard_map/ppermute | solution.py:375
  13.5 22.6 %collective-permute-start.8 = (bf16[64,1024]{1,0:T(8,128)(2,1)}, bf16[64,1024]{1,0:T(8,128)(2,1)S(1)}, u32[]{:S(2)}, u32[]{:S(2)}) collective-permute-start(bf16[64,1024]{1,0:T(8,128)(2,1)} %slice.7), channel_id=1, source_target_pairs={{0,2},{2,4},{4,6},{6,8},{8,10},{10,12},{12,14},{1,3},{3,5},{5,7},{... | collective-permute-start | bytes 393224 | tf_op jit(solution)/shard_map/ppermute | solution.py:429
  18.9 17.2 %collective-permute-start.7 = (bf16[64,1024]{1,0:T(8,128)(2,1)}, bf16[64,1024]{1,0:T(8,128)(2,1)S(1)}, u32[]{:S(2)}, u32[]{:S(2)}) collective-permute-start(bf16[64,1024]{1,0:T(8,128)(2,1)} %slice.6), channel_id=1, source_target_pairs={{0,2},{2,4},{4,6},{6,8},{8,10},{10,12},{12,14},{1,3},{3,5},{5,7},{... | collective-permute-start | bytes 393224 | tf_op jit(solution)/shard_map/ppermute | solution.py:429
  25.1 5.4 %collective-permute-start.3 = (bf16[2,160,128]{2,1,0:T(8,128)(2,1)S(1)}, bf16[2,160,128]{2,1,0:T(8,128)(2,1)S(1)}, u32[]{:S(2)}, u32[]{:S(2)}) collective-permute-start(bf16[2,160,128]{2,1,0:T(8,128)(2,1)S(1)} %get-tuple-element.20), channel_id=1, source_target_pairs={{0,8},{2,10},{4,12},{6,14},{8,0},{10,2},{12,4},{14,6},{1,9},{3,11}... | collective-permute-start | bytes 245768 | tf_op jit(solution)/shard_map/ppermute | solution.py:375
  30.5 26.7 %copy-start.15 = (s32[8,256]{1,0:T(8,128)S(1)}, s32[8,256]{1,0:T(8,128)}, u32[]{:S(2)}) copy-start(s32[8,256]{1,0:T(8,128)} %constant.30.clone.index_ref) | copy-start | bytes 24580
  32.6 24.7 %copy-start.14 = (f32[8,256]{1,0:T(8,128)S(1)}, f32[8,256]{1,0:T(8,128)}, u32[]{:S(2)}) copy-start(f32[8,256]{1,0:T(8,128)} %constant.31.clone.real_ref) | copy-start | bytes 24580
  32.6 24.7 %collective-permute-start.4 = (bf16[2,160,128]{2,1,0:T(8,128)(2,1)}, bf16[2,160,128]{2,1,0:T(8,128)(2,1)S(1)}, u32[]{:S(2)}, u32[]{:S(2)}) collective-permute-start(bf16[2,160,128]{2,1,0:T(8,128)(2,1)} %get-tuple-element.23), channel_id=1, source_target_pairs={{0,2},{2,0},{4,6},{6,4},{8,10},{10,8},{12,14},{14,12},{1,3},{3,1},... | collective-permute-start | bytes 245768 | tf_op jit(solution)/shard_map/ppermute | solution.py:375
  34.1 23.1 %collective-permute-start.5 = (bf16[2,160,128]{2,1,0:T(8,128)(2,1)}, bf16[2,160,128]{2,1,0:T(8,128)(2,1)S(1)}, u32[]{:S(2)}, u32[]{:S(2)}) collective-permute-start(bf16[2,160,128]{2,1,0:T(8,128)(2,1)} %get-tuple-element.24), channel_id=1, source_target_pairs={{0,4},{2,6},{4,0},{6,2},{8,12},{10,14},{12,8},{14,10},{1,5},{3,7},... | collective-permute-start | bytes 245768 | tf_op jit(solution)/shard_map/ppermute | solution.py:375
  35.7 21.6 %collective-permute-start.6 = (bf16[2,160,128]{2,1,0:T(8,128)(2,1)S(1)}, bf16[2,160,128]{2,1,0:T(8,128)(2,1)S(1)}, u32[]{:S(2)}, u32[]{:S(2)}) collective-permute-start(bf16[2,160,128]{2,1,0:T(8,128)(2,1)S(1)} %get-tuple-element.25), channel_id=1, source_target_pairs={{0,6},{2,4},{4,2},{6,0},{8,14},{10,12},{12,10},{14,8},{1,7},{3,5},... | collective-permute-start | bytes 245768 | tf_op jit(solution)/shard_map/ppermute | solution.py:375
  36.1 1.2 %copy-start.10 = (bf16[512,1024]{1,0:T(8,128)(2,1)S(1)}, bf16[512,1024]{1,0:T(8,128)(2,1)}, u32[]{:S(2)}) copy-start(bf16[512,1024]{1,0:T(8,128)(2,1)} %wq_ref.1) | copy-start | bytes 3145732
  57.3 1.6 %copy-start.6 = (f32[512,1024]{1,0:T(8,128)S(1)}, f32[512,1024]{1,0:T(8,128)}, u32[]{:S(2)}) copy-start(f32[512,1024]{1,0:T(8,128)} %get-tuple-element.27.den_ref) | copy-start | bytes 6291460

commit v2 on v1

v2 whole, which is shorter than its diff:
```python
import numpy as np
import jax
import jax.numpy as jnp
from jax import lax
from jax.experimental import pallas as pl
from jax.experimental.pallas import tpu as pltpu
from jax.sharding import PartitionSpec as P

WINDOW = 64
ROWS = 160
MISC = 157
LOG2E = float(np.log2(np.e))
F32 = jnp.float32
BF16 = jnp.bfloat16
VMEM_LIMIT = 24 * 1024 * 1024


def feature_tables(width):
    first = -np.ones(ROWS, np.int32)
    second = -np.ones(ROWS, np.int32)
    scale = np.zeros(ROWS, np.float32)
    twice = np.ones(ROWS, np.float32)
    scale[0] = 1.0
    at = 1
    for i in range(width):
        first[at], scale[at] = i, width ** (-0.25)
        at += 1
    for i in range(width):
        for j in range(i, width):
            first[at], second[at], scale[at] = i, j, (2.0 * width) ** (-0.5)
            twice[at] = 1.0 if i == j else 2.0
            at += 1
    one_a = ((first < 0) & (scale > 0)).astype(np.float32)
    one_b = ((second < 0) & (scale > 0)).astype(np.float32)
    return first, second, one_a, one_b, scale, twice


def key_table(width):
    first, second, one_a, one_b, scale, _ = feature_tables(width)
    table = np.zeros((ROWS, 128), np.float32)
    table[:, :5] = np.stack([first, second, one_a, one_b, scale], axis=1)
    return jnp.asarray(np.where(table < 0, -1000, table), F32)


def query_table(width):
    first, second, one_a, one_b, scale, twice = feature_tables(width)
    table = np.zeros((8, 256), np.float32)
    table[:2] = -1000
    for row, line in enumerate((first, second, one_a, one_b, scale * twice)):
        table[row, :ROWS] = np.where(line < 0, -1000, line)
    return jnp.asarray(table, F32)


def nt(a, b):
    return lax.dot_general(a, b, (((1,), (1,)), ((), ())), preferred_element_type=F32)


def nn(a, b):
    return lax.dot_general(a, b, (((1,), (0,)), ((), ())), preferred_element_type=F32)


def tn(a, b):
    return lax.dot_general(a, b, (((0,), (0,)), ((), ())), preferred_element_type=F32)


def parts(wide):
    upper = wide.astype(BF16)
    rest = wide - upper.astype(F32)
    middle = rest.astype(BF16)
    lower = (rest - middle.astype(F32)).astype(BF16)
    return upper, middle, lower


def iota(shape, dim):
    return lax.broadcasted_iota(jnp.int32, shape, dim)


def cumulative_rows(gates):
    heads, rows = gates.shape
    upto = (iota((128, 128), 0) <= iota((128, 128), 1)).astype(BF16)
    blocks = [gates[:, i : i + 128] for i in range(0, rows, 128)]
    stacked = jnp.concatenate([piece for block in blocks for piece in parts(block)], axis=0)
    inside = nn(stacked, upto)
    done, before = [], 0.0
    for i in range(len(blocks)):
        three = [inside[(3 * i + p) * heads : (3 * i + p + 1) * heads] for p in range(3)]
        done.append(three[0] + three[1] + three[2] + before)
        before = done[-1][:, 127:]
    return jnp.concatenate(done, axis=1)


def columns_of(table_ref):
    return [jnp.broadcast_to(table_ref[:, i : i + 1], (ROWS, 128)) for i in range(5)]


def shifted(x, by):
    return jnp.where(iota(x.shape, 0) < by, 0.0, pltpu.roll(x, by, 0))


def edge_kernel(k_ref, v_ref, out_ref, sems):
    rows = k_ref.shape[0]
    copies = [
        pltpu.make_async_copy(
            ref.at[pl.ds(rows - WINDOW, WINDOW)], out_ref.at[pl.ds(i * WINDOW, WINDOW)], sems.at[i]
        )
        for i, ref in enumerate((k_ref, v_ref))
    ]
    for copy in copies:
        copy.start()
    for copy in copies:
        copy.wait()


def one_state(head, out_ref, j, k, v_ref, w_ref, cum_ref, norm_ref, table):
    rows, wide = k.shape
    heads = cum_ref.shape[0]
    width = wide // heads
    first, second, one_a, one_b, scale = table
    lane = iota((ROWS, wide), 1).astype(F32)
    lane1 = iota((1, 128), 1)
    sub = iota((8, 128), 0)
    at = pl.ds(pl.multiple_of(head * 128, 128), 128)
    shift = (head * width).astype(F32)
    pick_a = (lane == first + shift).astype(BF16)
    pick_b = (lane == second + shift).astype(BF16)
    cum = cum_ref[pl.ds(head, 1), :]
    last = cum[:, rows - 1 :]
    keep = jnp.exp(last - cum)
    wide4 = lambda x: jnp.concatenate([x] * (rows // 128), axis=1)
    phi = (((nt(pick_a, k) + wide4(one_a)) * (nt(pick_b, k) + wide4(one_b)) * wide4(scale)) * keep).astype(BF16)
    v = v_ref[:, at].astype(F32)
    w = w_ref[:, at]
    conv = (w[0:1] * v + w[1:2] * shifted(v, 1) + w[2:3] * shifted(v, 2)).astype(BF16)
    state = nn(phi, conv)
    norm_ref[j, :, 0:ROWS] = nt(jnp.ones((8, rows), BF16), phi)
    norm = norm_ref[j, 0:1, :]
    high = norm.astype(BF16).astype(F32)
    low = norm - high
    keys8 = k[0:16].astype(F32)[0:8]
    turned = pltpu.roll(keys8, (wide - head * width) % wide, 1)
    turned2 = pltpu.roll(keys8, (wide - head * width + width) % wide, 1)
    misc = jnp.where(lane1 < width, turned[0:1], 0.0)
    misc = jnp.where((lane1 >= width) & (lane1 < 2 * width), turned2[1:2], misc)
    place = 2 * width
    for value in (keep[:, 0:1], keep[:, 1:2], jnp.exp(last)):
        for piece in parts(value):
            misc = jnp.where(lane1 == place, piece.astype(F32), misc)
            place += 1
    tail = state[ROWS - 8 :]
    for row, line in enumerate((high[:, :128], high[:, 128:], low[:, :128], low[:, 128:], misc)):
        tail = jnp.where(sub == row + 1, line, tail)
    tail = jnp.where(sub >= 6, v[rows - 8 :], tail)
    out_ref[j, 0 : ROWS - 16, :] = state[: ROWS - 16].astype(BF16)
    out_ref[j, ROWS - 16 :, :] = jnp.concatenate([state[ROWS - 16 : ROWS - 8], tail]).astype(BF16)


def state_kernel(order, group_ref, k_ref, v_ref, g_ref, w_ref, table_ref, *refs):
    outs, cum_ref, norm_ref = refs[: len(order)], refs[len(order)], refs[-1]
    cum_ref[...] = cumulative_rows(g_ref[...])
    norm_ref[...] = jnp.zeros(norm_ref.shape, F32)
    table = columns_of(table_ref)
    k = k_ref[...]
    for i, (out_ref, distance) in enumerate(zip(outs, order)):
        count = out_ref.shape[0]
        for j in range(count):
            head = (group_ref[0] ^ distance) * count + j
            one_state(head, out_ref, j, k, v_ref, w_ref, cum_ref, norm_ref.at[i], table)


def own_kernel(group_ref, k_ref, v_ref, cum_ref, w_ref, table_ref, after_ref, out_ref, column_ref, norm_ref):
    norm_ref[...] = jnp.zeros(norm_ref.shape, F32)
    table = columns_of(table_ref)
    k = k_ref[...]
    count = out_ref.shape[0]
    for j in range(count):
        one_state(group_ref[0] * count + j, out_ref, j, k, v_ref, w_ref, cum_ref, norm_ref, table)
    column_ref[...] = cum_ref[...].T


def tail_of(tile):
    return tile[ROWS - 8 :]


def value_of(tile, i, width):
    lane1 = iota((1, 128), 1)
    place = 2 * width + 3 * i
    here = (lane1 >= place) & (lane1 < place + 3)
    return jnp.sum(jnp.where(here, tail_of(tile)[5:6], 0.0), axis=1, keepdims=True)


def first_keys(tiles, table, width):
    lane = iota((ROWS, 128), 1).astype(F32)
    lines = [tail_of(tile)[5:6] for tile in tiles]
    rows = jnp.concatenate(lines + [jnp.zeros((8 - len(lines), 128), F32)] if len(lines) < 8 else lines).astype(BF16)
    first, second, one_a, one_b, scale = table
    found = []
    for token in range(2):
        pick_a = (lane == first + token * width).astype(BF16)
        pick_b = (lane == second + token * width).astype(BF16)
        found.append((nt(pick_a, rows) + one_a[:, 0:8]) * (nt(pick_b, rows) + one_b[:, 0:8]) * scale[:, 0:8])
    return found


def carried(tile, w):
    tail = tail_of(tile)
    return w[1:2] * tail[7:8] + w[2:3] * tail[6:7], w[2:3] * tail[7:8]


def seam(left, columns, enter, w):
    carry0, carry1 = carried(left, w)
    return columns[0] * (enter[0] * carry0) + columns[1] * (enter[1] * carry1)


def merge(left, right, columns, w, width):
    decay = value_of(right, 2, width)
    joined = decay * left + right + seam(left, columns, (value_of(right, 0, width), value_of(right, 1, width)), w)
    sub = iota((8, 128), 0)
    lane1 = iota((1, 128), 1)
    misc = tail_of(left)[5:6]
    misc = jnp.where(lane1 < 2 * width, misc, misc * decay)
    tail = jnp.where(sub == 5, misc, tail_of(joined))
    tail = jnp.where(sub >= 6, tail_of(right), tail)
    return jnp.concatenate([joined[: ROWS - 8], tail])


def packed(tile, width):
    tail = tail_of(tile)
    sub = iota((8, 128), 0)
    lane1 = iota((1, 128), 1)
    misc = tail[5:6]
    fresh = jnp.where(lane1 < 2 * width, misc, 0.0)
    place = 2 * width
    for i in range(3):
        for piece in parts(value_of(tile, i, width)):
            fresh = jnp.where(lane1 == place, piece.astype(F32), fresh)
            place += 1
    tail = jnp.where(sub == 5, fresh, norm_parts(tail))
    return jnp.concatenate([tile[: ROWS - 8], tail]).astype(BF16)


def norm_parts(tail):
    sub = iota((8, 128), 0)
    for row in (1, 2):
        norm = tail[row : row + 1] + tail[row + 2 : row + 3]
        high = norm.astype(BF16).astype(F32)
        tail = jnp.where(sub == row, high, jnp.where(sub == row + 2, norm - high, tail))
    return tail


def head_taps(w_ref, head):
    return w_ref[:, pl.ds(pl.multiple_of(head * 128, 128), 128)]


def group_kernel(width, group_ref, w_ref, table_ref, x0, x1, x2, x3, after_ref, total_ref, before_ref, keys_ref, small_ref, held):
    group = group_ref[0]
    count = x0.shape[0]
    for distance, ref in enumerate((x0, x1, x2, x3)):
        held[group ^ distance] = ref[...]
    tiles = [[held[p, j].astype(F32) for j in range(count)] for p in range(4)]
    columns = first_keys([tiles[p][j] for p in range(4) for j in range(count)], columns_of(table_ref), width)
    sub = iota((8, 128), 0)
    for j in range(count):
        w = head_taps(w_ref, group * count + j)
        so_far = tiles[0][j]
        for p in range(1, 4):
            before_ref[p - 1, j] = so_far
            pick = p * count + j
            so_far = merge(so_far, tiles[p][j], [c[:, pick : pick + 1] for c in columns], w, width)
        total_ref[j] = packed(so_far, width)
        for token in range(2):
            keys_ref[token, j] = jnp.broadcast_to(columns[token][:, j : j + 1], (ROWS, 128))
        decays = [value_of(tiles[p][j], 2, width) for p in range(3)]
        small = jnp.zeros((8, 128), F32)
        lines = decays[0], value_of(tiles[0][j], 0, width), value_of(tiles[0][j], 1, width), decays[1], decays[1] * decays[2]
        for row, value in enumerate(lines):
            small = jnp.where(sub == row, value, small)
        small_ref[j] = small


def pair_kernel(width, group_ref, w_ref, table_ref, left_ref, right_ref, out_ref):
    count = left_ref.shape[0]
    rights = [right_ref[j].astype(F32) for j in range(count)]
    columns = first_keys(rights, columns_of(table_ref), width)
    for j in range(count):
        w = head_taps(w_ref, group_ref[0] * count + j)
        left = left_ref[j].astype(F32)
        out_ref[j] = packed(merge(left, rights[j], [c[:, j : j + 1] for c in columns], w, width), width)


def spread_kernel(group_ref, live_ref, w_ref, base_ref, before_ref, keys_ref, small_ref, after_ref, o0, o1, o2, o3, held):
    group = group_ref[0]
    live = live_ref[0] > 0
    count = base_ref.shape[0]
    for j in range(count):
        w = head_taps(w_ref, group * count + j)
        base = jnp.where(live, base_ref[j].astype(F32), 0.0)
        held[0, j] = base.astype(BF16)
        small = small_ref[j]
        through = small[0:1] * base + seam(base, (keys_ref[0, j], keys_ref[1, j]), (small[1:2], small[2:3]), w)
        for p in range(3):
            tile = before_ref[p, j] + (through if p == 0 else small[2 + p : 3 + p] * through)
            held[p + 1, j] = jnp.concatenate([tile[: ROWS - 8], norm_parts(tail_of(tile))]).astype(BF16)
    for distance, ref in enumerate((o0, o1, o2, o3)):
        ref[...] = held[group ^ distance]


def window_kernel(edge_ref, wq_ref, wk_ref, v_ref, halo_ref, after_ref, win_ref):
    rows = wq_ref.shape[0]
    half = WINDOW
    seen = iota((half, 2 * half), 1)
    mine = iota((half, 2 * half), 0)
    valid = (seen > mine) & (seen <= mine + half)
    start = valid & ((seen >= half) | (edge_ref[0] > 0))
    steps = rows // half
    ones = jnp.ones((rows + half, 128), BF16)
    heads = wq_ref.shape[1] // 128
    for pair in range(0, heads, 2):
        scores, right = [], []
        for h in range(pair, pair + 2):
            at = slice(128 * h, 128 * h + 128)
            keys = jnp.concatenate([halo_ref[:half, at], wk_ref[:, at]])
            right.append(jnp.concatenate([jnp.concatenate([halo_ref[half:, at], v_ref[:, at]]), ones], axis=1))
            scores.append([nt(wq_ref[i * half : (i + 1) * half, at], keys[i * half : (i + 2) * half]) for i in range(steps)])
        probs = []
        for group in scores:
            group = [jnp.where(start if i == 0 else valid, s * (128 ** (-0.5) * LOG2E), -jnp.inf) for i, s in enumerate(group)]
            s = jnp.concatenate(group)
            probs.append(jnp.exp2(s - jnp.max(s, axis=1, keepdims=True)).astype(BF16))
        for h, p, r in zip(range(pair, pair + 2), probs, right):
            both = jnp.concatenate([nn(p[i * half : (i + 1) * half], r[i * half : (i + 2) * half]) for i in range(steps)])
            win_ref[:, 128 * h : 128 * h + 128] = both[:, :128] / both[:, 128:]


def block_kernel(q_ref, k_ref, v_ref, w_ref, cum_ref, column_ref, halo_ref, after_ref, num_ref, den_ref):
    rows, wide = q_ref.shape
    heads = cum_ref.shape[0]
    width = wide // heads
    q = q_ref[...]
    k = k_ref[...]
    cum_row = cum_ref[...] * LOG2E
    cum_col = column_ref[...] * LOG2E
    lane = iota(k.shape, 1)
    step, piece = 256, 128
    ones = jnp.ones((rows, 128), BF16)
    causal = iota((piece, piece), 0) >= iota((piece, piece), 1)
    for h in range(heads):
        at = slice(128 * h, 128 * h + 128)
        k_here = jnp.where((lane >= h * width) & (lane < (h + 1) * width), k, jnp.zeros_like(k)) * BF16(width ** (-0.5))
        v = v_ref[:, at].astype(F32)
        ahead = jnp.concatenate([halo_ref[2 * WINDOW - 16 :, at].astype(F32)[8:], v])
        w = w_ref[:, at]
        conv = w[0:1] * v + w[1:2] * pltpu.roll(ahead, 1, 0)[8:] + w[2:3] * pltpu.roll(ahead, 2, 0)[8:]
        right = jnp.concatenate([conv.astype(BF16), ones], axis=1)
        column = jnp.broadcast_to(cum_col[:, h : h + 1], (rows, piece))
        total = None
        for low in range(0, rows, step):
            x = nt(q[low:], k_here[low : low + step])
            lines = []
            for i in range(low, rows, piece):
                line = []
                for j in range(low, low + step, piece):
                    if j > i:
                        line.append(jnp.zeros((piece, piece), BF16))
                        continue
                    here = x[i - low : i - low + piece, j - low : j - low + piece]
                    gap = column[i : i + piece] - cum_row[h : h + 1, j : j + piece]
                    if i == j:
                        gap = jnp.where(causal, gap, -jnp.inf)
                    line.append((((0.5 * here + 1.0) * here + 1.0) * jnp.exp2(gap)).astype(BF16))
                lines.append(jnp.concatenate(line, axis=1))
            both = nn(jnp.concatenate(lines), right[low : low + step])
            total = both if total is None else jnp.concatenate([total[:low], total[low:] + both])
        num_ref[:, at] = total[:, :128]
        den_ref[:, at] = total[:, 128:]


def query_kernel(q_ref, column_ref, table_ref, after_ref, out_ref):
    rows, wide = q_ref.shape
    heads = column_ref.shape[1]
    width = wide // heads
    q = q_ref[...]
    enter = jnp.exp(column_ref[...])
    row = iota((wide, 256), 0).astype(F32)
    first, second, one_a, one_b, scale = (table_ref[i : i + 1] for i in range(5))
    for h in range(heads):
        pick_a = (row == first + h * width).astype(BF16)
        pick_b = (row == second + h * width).astype(BF16)
        phi = (nn(q, pick_a) + one_a) * (nn(q, pick_b) + one_b) * scale
        out_ref[h] = (phi * enter[:, h : h + 1]).astype(BF16)


def finish_kernel(group_ref, phi_ref, x0, x1, x2, x3, num_ref, den_ref, win_ref, out_ref, held):
    group = group_ref[0]
    heads = phi_ref.shape[0]
    count = x0.shape[0]
    for distance, ref in enumerate((x0, x1, x2, x3)):
        held[group ^ distance] = ref[...]
    tiles = [held[h // count, h % count] for h in range(heads)]
    lines = []
    for tile in tiles:
        tail = tile[ROWS - 16 :].astype(F32)[8:]
        lines.append(jnp.concatenate([tail[1:2] + tail[3:4], tail[2:3] + tail[4:5]], axis=1))
    norms = jnp.concatenate(lines).T
    for h in range(heads):
        at = slice(128 * h, 128 * h + 128)
        norm = jnp.broadcast_to(norms[:ROWS, h : h + 1], (ROWS, 128)).astype(BF16)
        both = nn(phi_ref[h][:, :ROWS], jnp.concatenate([tiles[h], norm], axis=1))
        out = (num_ref[:, at] + both[:, :128]) / (den_ref[:, at] + both[:, 128:]) + win_ref[:, at]
        out_ref[:, at] = out.astype(BF16)


def call(kernel, inputs, outs, scratch=(), smem=(), free=(), far=(), name=None):
    def space(i):
        return pltpu.SMEM if i in smem else pl.ANY if i in free else pltpu.HBM if i in far else pltpu.VMEM

    return pl.pallas_call(
        kernel,
        out_shape=outs,
        in_specs=[pl.BlockSpec(memory_space=space(i)) for i in range(len(inputs))],
        out_specs=jax.tree.map(lambda _: pl.BlockSpec(memory_space=pltpu.VMEM), outs),
        scratch_shapes=scratch,
        compiler_params=pltpu.CompilerParams(vmem_limit_bytes=VMEM_LIMIT),
        name=name,
    )(*inputs)


def local(count, q_feat, k_feat, values, win_query, win_key, log_gates, conv_weight):
    rows = values.shape[0]
    heads = log_gates.shape[1]
    width = q_feat.shape[1] // heads
    quarter = heads // 4
    position = lax.axis_index("seq")
    one = lambda number: jnp.reshape(number, (1,)).astype(jnp.int32)
    group = one(position & 3)
    table = key_table(width)
    shape = jax.ShapeDtypeStruct((quarter, ROWS, 128), BF16)
    wide = lambda *dims: jax.ShapeDtypeStruct(dims, F32)
    norm_scratch = pltpu.VMEM((quarter, 8, 256), F32)
    held = pltpu.VMEM((4, quarter, ROWS, 128), BF16)

    def swap(x, distance):
        return lax.ppermute(x, "seq", [(i, i ^ distance) for i in range(count)])

    edge = call(
        edge_kernel,
        (win_key, values),
        jax.ShapeDtypeStruct((2 * WINDOW, values.shape[1]), BF16),
        [pltpu.SemaphoreType.DMA((2,))],
        far=(0, 1),
        name="edge",
    )
    halo = lax.ppermute(edge, "seq", [(i, i + 1) for i in range(count - 1)])

    *sent, cum = call(
        lambda *refs: state_kernel((1, 2, 3), *refs),
        (group, k_feat, values, log_gates.T, conv_weight, table),
        [shape] * 3 + [wide(heads, rows)],
        [pltpu.VMEM((3, quarter, 8, 256), F32)],
        smem=(0,),
        name="states",
    )
    others = [swap(x, d) for d, x in zip((1, 2, 3), sent)]
    own, column = call(
        own_kernel,
        (group, k_feat, values, cum, conv_weight, table, sent[0]),
        [shape, wide(rows, heads)],
        [norm_scratch],
        smem=(0,),
        free=(6,),
        name="own_states",
    )
    win = call(
        window_kernel,
        (one(position > 0), win_query, win_key, values, halo, own),
        wide(*values.shape),
        smem=(0,),
        free=(5,),
        name="window",
    )
    total, before, keys, small = call(
        lambda *refs: group_kernel(width, *refs),
        (group, conv_weight, table, own, *others, win),
        [shape, wide(3, quarter, ROWS, 128), wide(2, quarter, ROWS, 128), wide(quarter, 8, 128)],
        [held],
        smem=(0,),
        free=(7,),
        name="merge_group",
    )
    base = jnp.zeros_like(total)
    live = position < 0
    distance = 4
    last = total
    while distance < count:
        got = swap(total, distance)
        upper = (position & distance) > 0

        def pair(left, right):
            return call(
                lambda *refs: pair_kernel(width, *refs),
                (group, conv_weight, table, left, right),
                shape,
                smem=(0,),
                name="merge_pair",
            )

        if distance == 4:
            base = got
        else:
            base = jnp.where(upper, jnp.where(live, pair(got, base), got), base)
        live = live | upper
        if 2 * distance < count:
            total = pair(jnp.where(upper, got, total), jnp.where(upper, total, got))
        distance *= 2
    num, den = call(
        block_kernel,
        (q_feat, k_feat, values, conv_weight, cum, column, halo, last),
        [wide(*values.shape)] * 2,
        free=(7,),
        name="block",
    )
    here, *sent = call(
        spread_kernel,
        (group, one(live), conv_weight, base, before, keys, small, num),
        [shape] * 4,
        [held],
        smem=(0, 1),
        free=(7,),
        name="spread",
    )
    prefixes = [here] + [swap(x, d) for d, x in zip((1, 2, 3), sent)]
    phi = call(
        query_kernel,
        (q_feat, column, query_table(width), here),
        jax.ShapeDtypeStruct((heads, rows, 256), BF16),
        free=(3,),
        name="query_features",
    )
    return call(
        finish_kernel,
        (group, phi, *prefixes, num, den, win),
        jax.ShapeDtypeStruct(values.shape, BF16),
        [held],
        smem=(0,),
        name="finish",
    )


def solution(mesh):
    rows = P(("grp", "seq"), "head")
    count = mesh.shape["seq"]
    return jax.shard_map(
        lambda *args: local(count, *args),
        mesh=mesh,
        in_specs=(rows,) * 6 + (P(None, "head"),),
        out_specs=rows,
        check_vma=False,
    )
```

time: 66 us -> 44.5 us (0.67)
  Pallas kernels: 33.8 us -> 16 us
  starting transfers between devices: 18.1 us -> 15.1 us
  local copies, waits for them, and re-layouts: 10.7 us -> 9.76 us
    pallas_call x6 -> x9, Pallas kernels: 33.8 us -> 16 us  [call(): pl.pallas_call(kernel, out_shape=outs, in_specs=[pl.BlockSpec(memory_spac...]
    ppermute x2 -> x1, starting transfers between devices: 7.41 us -> 5.02 us  [local(): halo = lax.ppermute(edge, 'seq', [(i, i + 1) for i in range(count - 1)])]
    slice x2 -> x0, local copies, waits for them, and re-layouts: 2.25 us -> none  [the longest x1 1.57 us: local(): win_key[rows - WINDOW:]]
    unnamed x33 -> x44, local copies, waits for them, and re-layouts: 8.42 us -> 9.76 us
  transfers between devices with their start and end apart: 9 -> 8, of which waited for: 1 -> 3; matrix products, arithmetic and copies ran while one was open for 4% -> 0% of each run, Pallas kernels for 37% -> 23%
where the time goes in v2:
time: 44.5 us; the launch traced here: 44.1 us
  Pallas kernels  16 us (36%)
  starting transfers between devices  15.1 us (34%)
  local copies, waits for them, and re-layouts  9.76 us (22%)
  waiting for transfers between devices  2.97 us (7%)
    pallas_call x9, Pallas kernels, call(): pl.pallas_call(kernel, out_shape=outs, in_specs=[pl.BlockSpec(memory_spac...  16 us
    ppermute x7, starting transfers between devices, swap(): return lax.ppermute(x, 'seq', [(i, i ^ distance) for i in range(count)])  10.1 us
    unnamed x44, local copies, waits for them, and re-layouts  9.76 us
    ppermute x1, starting transfers between devices, local(): halo = lax.ppermute(edge, 'seq', [(i, i + 1) for i in range(count - 1)])  5.02 us
    ppermute x7, waiting for transfers between devices, swap(): return lax.ppermute(x, 'seq', [(i, i ^ distance) for i in range(count)])  2.97 us
  transfers between devices with their start and end apart: 8, of which 3 were waited for; matrix products, arithmetic and copies ran while one was open for 0% of the time, Pallas kernels for 23%

profile of v2, /device:TPU:0, one launch (start us, length us, event | category | flops | bytes accessed | tf_op | source)
XLA Modules:
  0.0 44.1 jit_solution(17292198456885984555)
XLA Ops:
  0.0 1.2 %copy-done = bf16[512,1024]{1,0:T(8,128)(2,1)S(1)} copy-done((bf16[512,1024]{1,0:T(8,128)(2,1)S(1)}, bf16[512,1024]{1,0:T(8,128)(2,1)}, u32[]{:S(2)}) %copy-start) | copy-done | bytes 1048600
  1.2 1.2 %copy-done.2 = bf16[512,1024]{1,0:T(8,128)(2,1)S(1)} copy-done((bf16[512,1024]{1,0:T(8,128)(2,1)S(1)}, bf16[512,1024]{1,0:T(8,128)(2,1)}, u32[]{:S(2)}) %copy-start.2) | copy-done | bytes 1048600
  2.5 0.4 edge.1
  2.8 5.0 %collective-permute-start.3 = (bf16[128,1024]{1,0:T(8,128)(2,1)S(1)}, bf16[128,1024]{1,0:T(8,128)(2,1)S(1)}, u32[]{:S(2)}, u32[]{:S(2)}) collective-permute-start(bf16[128,1024]{1,0:T(8,128)(2,1)S(1)} %edge.1), channel_id=1, source_target_pairs={{0,2},{2,4},{4,6},{6,8},{8,10},{10,12},{12,14},{1,3},{3,5},{5,7},{... | collective-permute-start | bytes 786440 | tf_op jit(solution)/shard_map/ppermute | solution.py:452
  7.9 2.7 %states.1 = (bf16[2,160,128]{2,1,0:T(8,128)(2,1)}, bf16[2,160,128]{2,1,0:T(8,128)(2,1)}, bf16[2,160,128]{2,1,0:T(8,128)(2,1)}, f32[8,512]{1,0:T(8,128)S(1)}) custom-call(s32[1]{0:T(128)} %bitcast.refs_0_.group_ref, bf16[512,128]{1,0:T(8,128)(2,1)S(1)} %copy-done.4, bf16[512,1024]{1,0:T(8,128)(2,1)S(1)} %copy-done.1, f32[8,512]{1,0:T(8,128)S(1)} %bitcast.4, ...), custom_call_target="tpu_custom_call" | custom-call | tf_op jit(solution)/shard_map/states/pallas_call | solution.py:416
  10.6 1.6 %collective-permute-start.1 = (bf16[2,160,128]{2,1,0:T(8,128)(2,1)}, bf16[2,160,128]{2,1,0:T(8,128)(2,1)}, u32[]{:S(2)}, u32[]{:S(2)}) collective-permute-start(bf16[2,160,128]{2,1,0:T(8,128)(2,1)} %get-tuple-element.25), channel_id=1, source_target_pairs={{0,4},{2,6},{4,0},{6,2},{8,12},{10,14},{12,8},{14,10},{1,5},{3,7},... | collective-permute-start | bytes 245768 | tf_op jit(solution)/shard_map/ppermute | solution.py:442
  12.2 1.4 %collective-permute-start.2 = (bf16[2,160,128]{2,1,0:T(8,128)(2,1)}, bf16[2,160,128]{2,1,0:T(8,128)(2,1)}, u32[]{:S(2)}, u32[]{:S(2)}) collective-permute-start(bf16[2,160,128]{2,1,0:T(8,128)(2,1)} %get-tuple-element.26), channel_id=1, source_target_pairs={{0,6},{2,4},{4,2},{6,0},{8,14},{10,12},{12,10},{14,8},{1,7},{3,5},... | collective-permute-start | bytes 245768 | tf_op jit(solution)/shard_map/ppermute | solution.py:442
  13.6 0.5 %collective-permute-start = (bf16[2,160,128]{2,1,0:T(8,128)(2,1)}, bf16[2,160,128]{2,1,0:T(8,128)(2,1)}, u32[]{:S(2)}, u32[]{:S(2)}) collective-permute-start(bf16[2,160,128]{2,1,0:T(8,128)(2,1)} %get-tuple-element.22.after_ref), channel_id=1, source_target_pairs={{0,2},{2,0},{4,6},{6,4},{8,10},{10,8},{12,14},{14,12},{1,3},{3,1},... | collective-permute-start | bytes 245768 | tf_op jit(solution)/shard_map/ppermute | solution.py:442
  14.1 0.8 %own_states.1 = (bf16[2,160,128]{2,1,0:T(8,128)(2,1)S(1)}, f32[512,8]{1,0:T(8,128)S(1)}) custom-call(s32[1]{0:T(128)} %bitcast.refs_0_.group_ref, bf16[512,128]{1,0:T(8,128)(2,1)S(1)} %copy-done.4, bf16[512,1024]{1,0:T(8,128)(2,1)S(1)} %copy-done.1, f32[8,512]{1,0:T(8,128)S(1)} %get-tuple-element.21.cum_ref, f32[3,1024]{1,0:T(4,128)S(1)} %copy-done.13, ...), custom_call_target="tpu_custom_call" | custom-call | tf_op jit(solution)/shard_map/own_states/pallas_call | solution.py:416
  14.9 0.7 %copy-done.6 = f32[512,8]{1,0:T(8,128)} copy-done((f32[512,8]{1,0:T(8,128)}, f32[512,8]{1,0:T(8,128)S(1)}, u32[]{:S(2)}) %copy-start.6) | copy-done | bytes 16408
  15.6 0.0 copy-start.5
  15.6 1.2 %copy-done.5 = bf16[512,1024]{1,0:T(8,128)(2,1)S(1)} copy-done((bf16[512,1024]{1,0:T(8,128)(2,1)S(1)}, bf16[512,1024]{1,0:T(8,128)(2,1)}, u32[]{:S(2)}) %copy-start.5) | copy-done | bytes 1048600
  16.8 2.6 %window.1.refs_7_.win_ref = f32[512,1024]{1,0:T(8,128)S(1)} custom-call(s32[1]{0:T(128)} %bitcast.3.edge_ref, bf16[512,1024]{1,0:T(8,128)(2,1)S(1)} %copy-done.5, bf16[512,1024]{1,0:T(8,128)(2,1)S(1)} %copy-done.3, bf16[512,1024]{1,0:T(8,128)(2,1)S(1)} %copy-done.1, bf16[128,1024]{1,0:T(8,128)(2,1)S(1)} %collective-permute-done.3.halo_ref, ...), custom_call_target="tpu_custom_call" | custom-call | tf_op jit(solution)/shard_map/window/pallas_call | solution.py:416
  19.4 2.5 %merge_group.1 = (bf16[2,160,128]{2,1,0:T(8,128)(2,1)}, f32[3,2,160,128]{3,2,1,0:T(8,128)S(1)}, f32[2,2,160,128]{3,2,1,0:T(8,128)S(1)}, f32[2,8,128]{2,1,0:T(8,128)S(1)}) custom-call(s32[1]{0:T(128)} %bitcast.refs_0_.group_ref, f32[3,1024]{1,0:T(4,128)S(1)} %copy-done.13, f32[160,128]{1,0:T(8,128)S(1)} %copy-done.9, ...), custom_call_target="tpu_custom_call" | custom-call | tf_op jit(solution)/shard_map/merge_group/pallas_call | solution.py:416
  22.0 0.8 %copy-done.11 = f32[3,2,160,128]{3,2,1,0:T(8,128)} copy-done((f32[3,2,160,128]{3,2,1,0:T(8,128)}, f32[3,2,160,128]{3,2,1,0:T(8,128)S(1)}, u32[]{:S(2)}) %copy-start.11) | copy-done | bytes 491544
  22.7 0.7 %copy-done.14 = f32[2,2,160,128]{3,2,1,0:T(8,128)} copy-done((f32[2,2,160,128]{3,2,1,0:T(8,128)}, f32[2,2,160,128]{3,2,1,0:T(8,128)S(1)}, u32[]{:S(2)}) %copy-start.14) | copy-done | bytes 327704
  23.5 0.6 %copy-done.20 = f32[2,8,128]{2,1,0:T(8,128)} copy-done((f32[2,8,128]{2,1,0:T(8,128)}, f32[2,8,128]{2,1,0:T(8,128)S(1)}, u32[]{:S(2)}) %copy-start.20) | copy-done | bytes 8216
  24.1 2.6 %collective-permute-start.4 = (bf16[2,160,128]{2,1,0:T(8,128)(2,1)}, bf16[2,160,128]{2,1,0:T(8,128)(2,1)}, u32[]{:S(2)}, u32[]{:S(2)}) collective-permute-start(bf16[2,160,128]{2,1,0:T(8,128)(2,1)} %get-tuple-element.27.after_ref), channel_id=1, source_target_pairs={{0,8},{2,10},{4,12},{6,14},{8,0},{10,2},{12,4},{14,6},{1,9},{3,11}... | collective-permute-start | bytes 245768 | tf_op jit(solution)/shard_map/ppermute | solution.py:442
  26.6 0.9 %copy-done.7 = f32[512,8]{1,0:T(8,128)S(1)} copy-done((f32[512,8]{1,0:T(8,128)S(1)}, f32[512,8]{1,0:T(8,128)}, u32[]{:S(2)}) %copy-start.7) | copy-done | bytes 16408
  27.6 0.9 %copy-done.10 = bf16[512,128]{1,0:T(8,128)(2,1)S(1)} copy-done((bf16[512,128]{1,0:T(8,128)(2,1)S(1)}, bf16[512,128]{1,0:T(8,128)(2,1)}, u32[]{:S(2)}) %copy-start.10) | copy-done | bytes 131096
  28.5 0.7 %copy-done.17 = f32[8,512]{1,0:T(8,128)S(1)} copy-done((f32[8,512]{1,0:T(8,128)S(1)}, f32[8,512]{1,0:T(8,128)}, u32[]{:S(2)}) %copy-start.17) | copy-done | bytes 16408
  29.2 2.8 %block.1 = (f32[512,1024]{1,0:T(8,128)S(1)}, f32[512,1024]{1,0:T(8,128)S(1)}) custom-call(bf16[512,128]{1,0:T(8,128)(2,1)S(1)} %copy-done.10, bf16[512,128]{1,0:T(8,128)(2,1)S(1)} %copy-done.4, bf16[512,1024]{1,0:T(8,128)(2,1)S(1)} %copy-done.1, f32[3,1024]{1,0:T(4,128)S(1)} %copy-done.13, f32[8,512]{1,0:T(8,128)S(1)} %copy-done.17, f32[512,8]{1,0:T(8,128)S(1)} %copy-done.7, ...), custom_call_target="tpu_custom_call" | custom-call | tf_op jit(solution)/shard_map/block/pallas_call | solution.py:416
  32.0 0.7 %copy-done.21 = f32[2,8,128]{2,1,0:T(8,128)S(1)} copy-done((f32[2,8,128]{2,1,0:T(8,128)S(1)}, f32[2,8,128]{2,1,0:T(8,128)}, u32[]{:S(2)}) %copy-start.21) | copy-done | bytes 8216
  32.7 1.0 %spread.1 = (bf16[2,160,128]{2,1,0:T(8,128)(2,1)S(1)}, bf16[2,160,128]{2,1,0:T(8,128)(2,1)S(1)}, bf16[2,160,128]{2,1,0:T(8,128)(2,1)S(1)}, bf16[2,160,128]{2,1,0:T(8,128)(2,1)S(1)}) custom-call(s32[1]{0:T(128)} %bitcast.refs_0_.group_ref, s32[1]{0:T(128)} %bitcast.2.live_ref, f32[3,1024]{1,0:T(4,128)S(1)} %copy-done.13, ...), custom_call_target="tpu_custom_call" | custom-call | tf_op jit(solution)/shard_map/spread/pallas_call | solution.py:416
  33.7 1.6 %collective-permute-start.5 = (bf16[2,160,128]{2,1,0:T(8,128)(2,1)S(1)}, bf16[2,160,128]{2,1,0:T(8,128)(2,1)S(1)}, u32[]{:S(2)}, u32[]{:S(2)}) collective-permute-start(bf16[2,160,128]{2,1,0:T(8,128)(2,1)S(1)} %get-tuple-element.33), channel_id=1, source_target_pairs={{0,2},{2,0},{4,6},{6,4},{8,10},{10,8},{12,14},{14,12},{1,3},{3,1},... | collective-permute-start | bytes 245768 | tf_op jit(solution)/shard_map/ppermute | solution.py:442
  35.3 1.3 %collective-permute-start.6 = (bf16[2,160,128]{2,1,0:T(8,128)(2,1)S(1)}, bf16[2,160,128]{2,1,0:T(8,128)(2,1)S(1)}, u32[]{:S(2)}, u32[]{:S(2)}) collective-permute-start(bf16[2,160,128]{2,1,0:T(8,128)(2,1)S(1)} %get-tuple-element.34), channel_id=1, source_target_pairs={{0,4},{2,6},{4,0},{6,2},{8,12},{10,14},{12,8},{14,10},{1,5},{3,7},... | collective-permute-start | bytes 245768 | tf_op jit(solution)/shard_map/ppermute | solution.py:442
  36.7 1.1 %collective-permute-start.7 = (bf16[2,160,128]{2,1,0:T(8,128)(2,1)S(1)}, bf16[2,160,128]{2,1,0:T(8,128)(2,1)S(1)}, u32[]{:S(2)}, u32[]{:S(2)}) collective-permute-start(bf16[2,160,128]{2,1,0:T(8,128)(2,1)S(1)} %get-tuple-element.35), channel_id=1, source_target_pairs={{0,6},{2,4},{4,2},{6,0},{8,14},{10,12},{12,10},{14,8},{1,7},{3,5},... | collective-permute-start | bytes 245768 | tf_op jit(solution)/shard_map/ppermute | solution.py:442
  37.8 1.3 %query_features.1.phi_ref = bf16[8,512,256]{2,1,0:T(8,128)(2,1)S(1)} custom-call(bf16[512,128]{1,0:T(8,128)(2,1)S(1)} %copy-done.10, f32[512,8]{1,0:T(8,128)S(1)} %copy-done.7, f32[8,256]{1,0:T(8,128)S(1)} %copy-done.19, bf16[2,160,128]{2,1,0:T(8,128)(2,1)S(1)} %get-tuple-element.32.after_ref.x0), custom_call_target="tpu_custom_call" | custom-call | tf_op jit(solution)/shard_map/query_features/pallas_call | solution.py:416
  39.0 0.1 collective-permute-done.5.x1
  39.1 0.6 %collective-permute-done.6.x2 = bf16[2,160,128]{2,1,0:T(8,128)(2,1)S(1)} collective-permute-done((bf16[2,160,128]{2,1,0:T(8,128)(2,1)S(1)}, bf16[2,160,128]{2,1,0:T(8,128)(2,1)S(1)}, u32[]{:S(2)}, u32[]{:S(2)}) %collective-permute-start.6) | collective-permute-done | bytes 81952 | tf_op jit(solution)/shard_map/ppermute | solution.py:442
  39.8 2.2 %collective-permute-done.7.x3 = bf16[2,160,128]{2,1,0:T(8,128)(2,1)S(1)} collective-permute-done((bf16[2,160,128]{2,1,0:T(8,128)(2,1)S(1)}, bf16[2,160,128]{2,1,0:T(8,128)(2,1)S(1)}, u32[]{:S(2)}, u32[]{:S(2)}) %collective-permute-start.7) | collective-permute-done | bytes 81952 | tf_op jit(solution)/shard_map/ppermute | solution.py:442
  42.0 2.1 %finish.1 = bf16[512,1024]{1,0:T(8,128)(2,1)} custom-call(s32[1]{0:T(128)} %bitcast.refs_0_.group_ref, bf16[8,512,256]{2,1,0:T(8,128)(2,1)S(1)} %query_features.1.phi_ref, bf16[2,160,128]{2,1,0:T(8,128)(2,1)S(1)} %get-tuple-element.32.after_ref.x0, bf16[2,160,128]{2,1,0:T(8,128)(2,1)S(1)} %collective-permute-done.5.x1, ...), custom_call_target="tpu_custom_call" | custom-call | tf_op jit(solution)/shard_map/finish/pallas_call | solution.py:416
  (37 shorter events, 0.1 us)
Async XLA Ops:
  0.0 1.2 %copy-start = (bf16[512,1024]{1,0:T(8,128)(2,1)S(1)}, bf16[512,1024]{1,0:T(8,128)(2,1)}, u32[]{:S(2)}) copy-start(bf16[512,1024]{1,0:T(8,128)(2,1)} %v_ref.7) | copy-start | bytes 3145732
  1.2 1.2 %copy-start.2 = (bf16[512,1024]{1,0:T(8,128)(2,1)S(1)}, bf16[512,1024]{1,0:T(8,128)(2,1)}, u32[]{:S(2)}) copy-start(bf16[512,1024]{1,0:T(8,128)(2,1)} %wk_ref.1) | copy-start | bytes 3145732
  2.5 5.4 %copy-start.1 = (bf16[512,1024]{1,0:T(8,128)(2,1)S(1)}, bf16[512,1024]{1,0:T(8,128)(2,1)}, u32[]{:S(2)}) copy-start(bf16[512,1024]{1,0:T(8,128)(2,1)} %v_ref.7) | copy-start | bytes 3145732
  2.5 5.4 %copy-start.4 = (bf16[512,128]{1,0:T(8,128)(2,1)S(1)}, bf16[512,128]{1,0:T(8,128)(2,1)}, u32[]{:S(2)}) copy-start(bf16[512,128]{1,0:T(8,128)(2,1)} %k_ref.5) | copy-start | bytes 393220
  2.5 5.4 %copy-start.8 = (f32[160,128]{1,0:T(8,128)S(1)}, f32[160,128]{1,0:T(8,128)}, u32[]{:S(2)}) copy-start(f32[160,128]{1,0:T(8,128)} %constant.16.clone.refs_5_.table_ref.refs_2_) | copy-start | bytes 245764
  2.5 5.4 %copy-start.13 = (f32[3,1024]{1,0:T(4,128)S(1)}, f32[3,1024]{1,0:T(4,128)}, u32[]{:S(2)}) copy-start(f32[3,1024]{1,0:T(4,128)} %w_ref.5) | copy-start | bytes 36868
  2.5 5.5 %copy-start.18 = (f32[512,8]{0,1:T(8,128)S(1)}, f32[512,8]{0,1:T(8,128)}, u32[]{:S(2)}) copy-start(f32[512,8]{0,1:T(8,128)} %param.14) | copy-start | bytes 49156
  2.8 12.7 %collective-permute-start.3 = (bf16[128,1024]{1,0:T(8,128)(2,1)S(1)}, bf16[128,1024]{1,0:T(8,128)(2,1)S(1)}, u32[]{:S(2)}, u32[]{:S(2)}) collective-permute-start(bf16[128,1024]{1,0:T(8,128)(2,1)S(1)} %edge.1), channel_id=1, source_target_pairs={{0,2},{2,4},{4,6},{6,8},{8,10},{10,12},{12,14},{1,3},{3,5},{5,7},{... | collective-permute-start | bytes 786440 | tf_op jit(solution)/shard_map/ppermute | solution.py:452
  10.6 5.0 %copy-start.16 = (f32[8,512]{1,0:T(8,128)}, f32[8,512]{1,0:T(8,128)S(1)}, u32[]{:S(2)}) copy-start(f32[8,512]{1,0:T(8,128)S(1)} %get-tuple-element.21.cum_ref) | copy-start | bytes 49156
  10.6 8.8 %collective-permute-start.1 = (bf16[2,160,128]{2,1,0:T(8,128)(2,1)}, bf16[2,160,128]{2,1,0:T(8,128)(2,1)}, u32[]{:S(2)}, u32[]{:S(2)}) collective-permute-start(bf16[2,160,128]{2,1,0:T(8,128)(2,1)} %get-tuple-element.25), channel_id=1, source_target_pairs={{0,4},{2,6},{4,0},{6,2},{8,12},{10,14},{12,8},{14,10},{1,5},{3,7},... | collective-permute-start | bytes 245768 | tf_op jit(solution)/shard_map/ppermute | solution.py:442
  12.2 7.2 %collective-permute-start.2 = (bf16[2,160,128]{2,1,0:T(8,128)(2,1)}, bf16[2,160,128]{2,1,0:T(8,128)(2,1)}, u32[]{:S(2)}, u32[]{:S(2)}) collective-permute-start(bf16[2,160,128]{2,1,0:T(8,128)(2,1)} %get-tuple-element.26), channel_id=1, source_target_pairs={{0,6},{2,4},{4,2},{6,0},{8,14},{10,12},{12,10},{14,8},{1,7},{3,5},... | collective-permute-start | bytes 245768 | tf_op jit(solution)/shard_map/ppermute | solution.py:442
  13.6 5.8 %collective-permute-start = (bf16[2,160,128]{2,1,0:T(8,128)(2,1)}, bf16[2,160,128]{2,1,0:T(8,128)(2,1)}, u32[]{:S(2)}, u32[]{:S(2)}) collective-permute-start(bf16[2,160,128]{2,1,0:T(8,128)(2,1)} %get-tuple-element.22.after_ref), channel_id=1, source_target_pairs={{0,2},{2,0},{4,6},{6,4},{8,10},{10,8},{12,14},{14,12},{1,3},{3,1},... | collective-permute-start | bytes 245768 | tf_op jit(solution)/shard_map/ppermute | solution.py:442
  14.1 1.5 %copy-start.3 = (bf16[512,1024]{1,0:T(8,128)(2,1)S(1)}, bf16[512,1024]{1,0:T(8,128)(2,1)}, u32[]{:S(2)}) copy-start(bf16[512,1024]{1,0:T(8,128)(2,1)} %wk_ref.1) | copy-start | bytes 3145732
  14.9 0.7 %copy-start.6 = (f32[512,8]{1,0:T(8,128)}, f32[512,8]{1,0:T(8,128)S(1)}, u32[]{:S(2)}) copy-start(f32[512,8]{1,0:T(8,128)S(1)} %get-tuple-element.23.column_ref) | copy-start | bytes 49156
  15.6 1.2 %copy-start.5 = (bf16[512,1024]{1,0:T(8,128)(2,1)S(1)}, bf16[512,1024]{1,0:T(8,128)(2,1)}, u32[]{:S(2)}) copy-start(bf16[512,1024]{1,0:T(8,128)(2,1)} %wq_ref.1) | copy-start | bytes 3145732
  16.8 2.6 %copy-start.9 = (f32[160,128]{1,0:T(8,128)S(1)}, f32[160,128]{1,0:T(8,128)}, u32[]{:S(2)}) copy-start(f32[160,128]{1,0:T(8,128)} %constant.16.clone.refs_5_.table_ref.refs_2_) | copy-start | bytes 245764
  22.0 0.8 %copy-start.11 = (f32[3,2,160,128]{3,2,1,0:T(8,128)}, f32[3,2,160,128]{3,2,1,0:T(8,128)S(1)}, u32[]{:S(2)}) copy-start(f32[3,2,160,128]{3,2,1,0:T(8,128)S(1)} %get-tuple-element.28.before_ref) | copy-start | bytes 1474564
  22.7 0.7 %copy-start.14 = (f32[2,2,160,128]{3,2,1,0:T(8,128)}, f32[2,2,160,128]{3,2,1,0:T(8,128)S(1)}, u32[]{:S(2)}) copy-start(f32[2,2,160,128]{3,2,1,0:T(8,128)S(1)} %get-tuple-element.29.keys_ref) | copy-start | bytes 983044
  23.5 0.6 %copy-start.20 = (f32[2,8,128]{2,1,0:T(8,128)}, f32[2,8,128]{2,1,0:T(8,128)S(1)}, u32[]{:S(2)}) copy-start(f32[2,8,128]{2,1,0:T(8,128)S(1)} %get-tuple-element.30.small_ref) | copy-start | bytes 24580
  24.1 7.9 %collective-permute-start.4 = (bf16[2,160,128]{2,1,0:T(8,128)(2,1)}, bf16[2,160,128]{2,1,0:T(8,128)(2,1)}, u32[]{:S(2)}, u32[]{:S(2)}) collective-permute-start(bf16[2,160,128]{2,1,0:T(8,128)(2,1)} %get-tuple-element.27.after_ref), channel_id=1, source_target_pairs={{0,8},{2,10},{4,12},{6,14},{8,0},{10,2},{12,4},{14,6},{1,9},{3,11}... | collective-permute-start | bytes 245768 | tf_op jit(solution)/shard_map/ppermute | solution.py:442
  26.6 0.9 %copy-start.7 = (f32[512,8]{1,0:T(8,128)S(1)}, f32[512,8]{1,0:T(8,128)}, u32[]{:S(2)}) copy-start(f32[512,8]{1,0:T(8,128)} %copy-done.6) | copy-start | bytes 49156
  27.6 0.9 %copy-start.10 = (bf16[512,128]{1,0:T(8,128)(2,1)S(1)}, bf16[512,128]{1,0:T(8,128)(2,1)}, u32[]{:S(2)}) copy-start(bf16[512,128]{1,0:T(8,128)(2,1)} %q_ref.3) | copy-start | bytes 393220
  28.5 0.7 %copy-start.17 = (f32[8,512]{1,0:T(8,128)S(1)}, f32[8,512]{1,0:T(8,128)}, u32[]{:S(2)}) copy-start(f32[8,512]{1,0:T(8,128)} %copy-done.16) | copy-start | bytes 49156
  29.2 2.8 %copy-start.12 = (f32[3,2,160,128]{3,2,1,0:T(8,128)S(1)}, f32[3,2,160,128]{3,2,1,0:T(8,128)}, u32[]{:S(2)}) copy-start(f32[3,2,160,128]{3,2,1,0:T(8,128)} %copy-done.11) | copy-start | bytes 1474564
  29.2 2.8 %copy-start.15 = (f32[2,2,160,128]{3,2,1,0:T(8,128)S(1)}, f32[2,2,160,128]{3,2,1,0:T(8,128)}, u32[]{:S(2)}) copy-start(f32[2,2,160,128]{3,2,1,0:T(8,128)} %copy-done.14) | copy-start | bytes 983044
  29.2 8.5 %copy-start.19 = (f32[8,256]{1,0:T(8,128)S(1)}, f32[8,256]{1,0:T(8,128)}, u32[]{:S(2)}) copy-start(f32[8,256]{1,0:T(8,128)} %constant.17.clone.table_ref) | copy-start | bytes 24580
  32.0 0.7 %copy-start.21 = (f32[2,8,128]{2,1,0:T(8,128)S(1)}, f32[2,8,128]{2,1,0:T(8,128)}, u32[]{:S(2)}) copy-start(f32[2,8,128]{2,1,0:T(8,128)} %copy-done.20) | copy-start | bytes 24580
  33.7 5.4 %collective-permute-start.5 = (bf16[2,160,128]{2,1,0:T(8,128)(2,1)S(1)}, bf16[2,160,128]{2,1,0:T(8,128)(2,1)S(1)}, u32[]{:S(2)}, u32[]{:S(2)}) collective-permute-start(bf16[2,160,128]{2,1,0:T(8,128)(2,1)S(1)} %get-tuple-element.33), channel_id=1, source_target_pairs={{0,2},{2,0},{4,6},{6,4},{8,10},{10,8},{12,14},{14,12},{1,3},{3,1},... | collective-permute-start | bytes 245768 | tf_op jit(solution)/shard_map/ppermute | solution.py:442
  35.3 4.4 %collective-permute-start.6 = (bf16[2,160,128]{2,1,0:T(8,128)(2,1)S(1)}, bf16[2,160,128]{2,1,0:T(8,128)(2,1)S(1)}, u32[]{:S(2)}, u32[]{:S(2)}) collective-permute-start(bf16[2,160,128]{2,1,0:T(8,128)(2,1)S(1)} %get-tuple-element.34), channel_id=1, source_target_pairs={{0,4},{2,6},{4,0},{6,2},{8,12},{10,14},{12,8},{14,10},{1,5},{3,7},... | collective-permute-start | bytes 245768 | tf_op jit(solution)/shard_map/ppermute | solution.py:442
  36.7 5.3 %collective-permute-start.7 = (bf16[2,160,128]{2,1,0:T(8,128)(2,1)S(1)}, bf16[2,160,128]{2,1,0:T(8,128)(2,1)S(1)}, u32[]{:S(2)}, u32[]{:S(2)}) collective-permute-start(bf16[2,160,128]{2,1,0:T(8,128)(2,1)S(1)} %get-tuple-element.35), channel_id=1, source_target_pairs={{0,6},{2,4},{4,2},{6,0},{8,14},{10,12},{12,10},{14,8},{1,7},{3,5},... | collective-permute-start | bytes 245768 | tf_op jit(solution)/shard_map/ppermute | solution.py:442

commit v3 on v2

--- a/solution.py
+++ b/solution.py
@@ -8,7 +8,7 @@
 
 WINDOW = 64
 ROWS = 160
-MISC = 157
+EDGE = 158
 LOG2E = float(np.log2(np.e))
 F32 = jnp.float32
 BF16 = jnp.bfloat16
@@ -48,6 +48,8 @@
     table[:2] = -1000
     for row, line in enumerate((first, second, one_a, one_b, scale * twice)):
         table[row, :ROWS] = np.where(line < 0, -1000, line)
+    table[2:4, EDGE : EDGE + 2] = 1.0
+    table[4:6, EDGE : EDGE + 2] = 0.5
     return jnp.asarray(table, F32)
 
 
@@ -97,7 +99,7 @@
     return jnp.where(iota(x.shape, 0) < by, 0.0, pltpu.roll(x, by, 0))
 
 
-def edge_kernel(k_ref, v_ref, out_ref, sems):
+def edge_kernel(k_ref, v_ref, after_ref, out_ref, sems):
     rows = k_ref.shape[0]
     copies = [
         pltpu.make_async_copy(
@@ -154,27 +156,20 @@
     out_ref[j, ROWS - 16 :, :] = jnp.concatenate([state[ROWS - 16 : ROWS - 8], tail]).astype(BF16)
 
 
-def state_kernel(order, group_ref, k_ref, v_ref, g_ref, w_ref, table_ref, *refs):
-    outs, cum_ref, norm_ref = refs[: len(order)], refs[len(order)], refs[-1]
+def gate_kernel(place_ref, g_ref, cum_ref):
     cum_ref[...] = cumulative_rows(g_ref[...])
+
+
+def state_kernel(order, place_ref, k_ref, v_ref, cum_ref, w_ref, table_ref, after_ref, *refs):
+    outs, norm_ref = refs[:-1], refs[-1]
     norm_ref[...] = jnp.zeros(norm_ref.shape, F32)
     table = columns_of(table_ref)
     k = k_ref[...]
     for i, (out_ref, distance) in enumerate(zip(outs, order)):
         count = out_ref.shape[0]
         for j in range(count):
-            head = (group_ref[0] ^ distance) * count + j
+            head = ((place_ref[0] & 3) ^ distance) * count + j
             one_state(head, out_ref, j, k, v_ref, w_ref, cum_ref, norm_ref.at[i], table)
-
-
-def own_kernel(group_ref, k_ref, v_ref, cum_ref, w_ref, table_ref, after_ref, out_ref, column_ref, norm_ref):
-    norm_ref[...] = jnp.zeros(norm_ref.shape, F32)
-    table = columns_of(table_ref)
-    k = k_ref[...]
-    count = out_ref.shape[0]
-    for j in range(count):
-        one_state(group_ref[0] * count + j, out_ref, j, k, v_ref, w_ref, cum_ref, norm_ref, table)
-    column_ref[...] = cum_ref[...].T
 
 
 def tail_of(tile):
@@ -251,8 +246,8 @@
     return w_ref[:, pl.ds(pl.multiple_of(head * 128, 128), 128)]
 
 
-def group_kernel(width, group_ref, w_ref, table_ref, x0, x1, x2, x3, after_ref, total_ref, before_ref, keys_ref, small_ref, held):
-    group = group_ref[0]
+def group_kernel(width, place_ref, w_ref, table_ref, x0, x1, x2, x3, after_ref, total_ref, before_ref, keys_ref, small_ref, held):
+    group = (place_ref[0] & 3)
     count = x0.shape[0]
     for distance, ref in enumerate((x0, x1, x2, x3)):
         held[group ^ distance] = ref[...]
@@ -277,40 +272,48 @@
         small_ref[j] = small
 
 
-def pair_kernel(width, group_ref, w_ref, table_ref, left_ref, right_ref, out_ref):
+def pair_kernel(width, place_ref, w_ref, table_ref, left_ref, right_ref, out_ref):
     count = left_ref.shape[0]
     rights = [right_ref[j].astype(F32) for j in range(count)]
     columns = first_keys(rights, columns_of(table_ref), width)
     for j in range(count):
-        w = head_taps(w_ref, group_ref[0] * count + j)
+        w = head_taps(w_ref, (place_ref[0] & 3) * count + j)
         left = left_ref[j].astype(F32)
         out_ref[j] = packed(merge(left, rights[j], [c[:, j : j + 1] for c in columns], w, width), width)
 
 
-def spread_kernel(group_ref, live_ref, w_ref, base_ref, before_ref, keys_ref, small_ref, after_ref, o0, o1, o2, o3, held):
-    group = group_ref[0]
-    live = live_ref[0] > 0
+def with_edge(tile, source, w):
+    carry0, carry1 = carried(source, w)
+    sub = iota((8, 128), 0)
+    tail = norm_parts(tail_of(tile))
+    tail = jnp.where(sub == 6, carry0, jnp.where(sub == 7, carry1, tail))
+    return jnp.concatenate([tile[: ROWS - 8], tail]).astype(BF16)
+
+
+def spread_kernel(place_ref, w_ref, base_ref, before_ref, keys_ref, small_ref, after_ref, o0, o1, o2, o3, held):
+    group = (place_ref[0] & 3)
+    live = place_ref[0] > 3
     count = base_ref.shape[0]
     for j in range(count):
         w = head_taps(w_ref, group * count + j)
         base = jnp.where(live, base_ref[j].astype(F32), 0.0)
-        held[0, j] = base.astype(BF16)
+        held[0, j] = with_edge(base, base, w)
         small = small_ref[j]
         through = small[0:1] * base + seam(base, (keys_ref[0, j], keys_ref[1, j]), (small[1:2], small[2:3]), w)
         for p in range(3):
             tile = before_ref[p, j] + (through if p == 0 else small[2 + p : 3 + p] * through)
-            held[p + 1, j] = jnp.concatenate([tile[: ROWS - 8], norm_parts(tail_of(tile))]).astype(BF16)
+            held[p + 1, j] = with_edge(tile, before_ref[p, j], w)
     for distance, ref in enumerate((o0, o1, o2, o3)):
         ref[...] = held[group ^ distance]
 
 
-def window_kernel(edge_ref, wq_ref, wk_ref, v_ref, halo_ref, after_ref, win_ref):
+def window_kernel(place_ref, wq_ref, wk_ref, v_ref, halo_ref, after_ref, win_ref):
     rows = wq_ref.shape[0]
     half = WINDOW
     seen = iota((half, 2 * half), 1)
     mine = iota((half, 2 * half), 0)
     valid = (seen > mine) & (seen <= mine + half)
-    start = valid & ((seen >= half) | (edge_ref[0] > 0))
+    start = valid & ((seen >= half) | (place_ref[0] > 0))
     steps = rows // half
     ones = jnp.ones((rows + half, 128), BF16)
     heads = wq_ref.shape[1] // 128
@@ -331,14 +334,15 @@
             win_ref[:, 128 * h : 128 * h + 128] = both[:, :128] / both[:, 128:]
 
 
-def block_kernel(q_ref, k_ref, v_ref, w_ref, cum_ref, column_ref, halo_ref, after_ref, num_ref, den_ref):
+def block_kernel(q_ref, k_ref, v_ref, w_ref, cum_ref, after_ref, num_ref, den_ref, token_ref):
     rows, wide = q_ref.shape
     heads = cum_ref.shape[0]
     width = wide // heads
     q = q_ref[...]
     k = k_ref[...]
     cum_row = cum_ref[...] * LOG2E
-    cum_col = column_ref[...] * LOG2E
+    cum_col = cum_row.T
+    token_ref[...] = jnp.zeros(token_ref.shape, F32)
     lane = iota(k.shape, 1)
     step, piece = 256, 128
     ones = jnp.ones((rows, 128), BF16)
@@ -347,9 +351,8 @@
         at = slice(128 * h, 128 * h + 128)
         k_here = jnp.where((lane >= h * width) & (lane < (h + 1) * width), k, jnp.zeros_like(k)) * BF16(width ** (-0.5))
         v = v_ref[:, at].astype(F32)
-        ahead = jnp.concatenate([halo_ref[2 * WINDOW - 16 :, at].astype(F32)[8:], v])
         w = w_ref[:, at]
-        conv = w[0:1] * v + w[1:2] * pltpu.roll(ahead, 1, 0)[8:] + w[2:3] * pltpu.roll(ahead, 2, 0)[8:]
+        conv = w[0:1] * v + w[1:2] * shifted(v, 1) + w[2:3] * shifted(v, 2)
         right = jnp.concatenate([conv.astype(BF16), ones], axis=1)
         column = jnp.broadcast_to(cum_col[:, h : h + 1], (rows, piece))
         total = None
@@ -374,23 +377,35 @@
         den_ref[:, at] = total[:, 128:]
 
 
-def query_kernel(q_ref, column_ref, table_ref, after_ref, out_ref):
+def query_kernel(q_ref, k_ref, cum_ref, table_ref, after_ref, out_ref, token_ref):
     rows, wide = q_ref.shape
-    heads = column_ref.shape[1]
+    heads = cum_ref.shape[0]
     width = wide // heads
     q = q_ref[...]
-    enter = jnp.exp(column_ref[...])
-    row = iota((wide, 256), 0).astype(F32)
-    first, second, one_a, one_b, scale = (table_ref[i : i + 1] for i in range(5))
+    column = cum_ref[...].T
+    token_ref[...] = jnp.zeros(token_ref.shape, F32)
+    row = iota((wide, 256), 0)
+    lane = iota((wide, 256), 1)
+    keys = k_ref[0:16].astype(F32)[0:8].T * width ** (-0.5)
+    keys = jnp.where(lane == EDGE, keys[:, 0:1], jnp.where(lane == EDGE + 1, keys[:, 1:2], 0.0))
+    first, second, one_a, one_b, scale, plus = (table_ref[i : i + 1] for i in range(6))
+    side = iota((1, 128), 1) + 128
+    early = (iota((rows, 128), 0) == 0) & (iota((rows, 128), 1) == EDGE + 1 - 128)
     for h in range(heads):
-        pick_a = (row == first + h * width).astype(BF16)
-        pick_b = (row == second + h * width).astype(BF16)
-        phi = (nn(q, pick_a) + one_a) * (nn(q, pick_b) + one_b) * scale
-        out_ref[h] = (phi * enter[:, h : h + 1]).astype(BF16)
-
-
-def finish_kernel(group_ref, phi_ref, x0, x1, x2, x3, num_ref, den_ref, win_ref, out_ref, held):
-    group = group_ref[0]
+        here = (row >= h * width) & (row < (h + 1) * width)
+        keys_here = jnp.where(here, keys, 0.0)
+        pick_a = jnp.where(row.astype(F32) == first + h * width, 1.0, keys_here).astype(BF16)
+        pick_b = jnp.where(row.astype(F32) == second + h * width, 1.0, keys_here).astype(BF16)
+        phi = (nn(q, pick_a) + one_a) * (nn(q, pick_b) + one_b) * scale + plus
+        since = column[:, h : h + 1]
+        offset = jnp.where(side == EDGE, since[0:1], jnp.where(side == EDGE + 1, since[1:2], 0.0))
+        enter = jnp.where(early, 0.0, jnp.exp(since - offset))
+        out_ref[h, :, :128] = (phi[:, :128] * jnp.exp(since)).astype(BF16)
+        out_ref[h, :, 128:] = (phi[:, 128:] * enter).astype(BF16)
+
+
+def finish_kernel(place_ref, phi_ref, x0, x1, x2, x3, num_ref, den_ref, win_ref, out_ref, held):
+    group = (place_ref[0] & 3)
     heads = phi_ref.shape[0]
     count = x0.shape[0]
     for distance, ref in enumerate((x0, x1, x2, x3)):
@@ -409,7 +424,7 @@
         out_ref[:, at] = out.astype(BF16)
 
 
-def call(kernel, inputs, outs, scratch=(), smem=(), free=(), far=(), name=None):
+def call(kernel, inputs, outs, scratch=(), smem=(), free=(), far=(), name=None, us=1.0):
     def space(i):
         return pltpu.SMEM if i in smem else pl.ANY if i in free else pltpu.HBM if i in far else pltpu.VMEM
 
@@ -421,6 +436,7 @@
         scratch_shapes=scratch,
         compiler_params=pltpu.CompilerParams(vmem_limit_bytes=VMEM_LIMIT),
         name=name,
+        cost_estimate=pl.CostEstimate(flops=int(us * 3e9), bytes_accessed=int(us * 9e6), transcendentals=0),
     )(*inputs)
 
 
@@ -431,60 +447,61 @@
     quarter = heads // 4
     position = lax.axis_index("seq")
     one = lambda number: jnp.reshape(number, (1,)).astype(jnp.int32)
-    group = one(position & 3)
+    place = one(position)
     table = key_table(width)
     shape = jax.ShapeDtypeStruct((quarter, ROWS, 128), BF16)
     wide = lambda *dims: jax.ShapeDtypeStruct(dims, F32)
-    norm_scratch = pltpu.VMEM((quarter, 8, 256), F32)
     held = pltpu.VMEM((4, quarter, ROWS, 128), BF16)
 
     def swap(x, distance):
         return lax.ppermute(x, "seq", [(i, i ^ distance) for i in range(count)])
 
+    cum = call(gate_kernel, (place, log_gates.T), wide(heads, rows), smem=(0,), name="gates", us=6.0)
+
+    def states(order, after, name, us):
+        return call(
+            lambda *refs: state_kernel(order, *refs),
+            (place, k_feat, values, cum, conv_weight, table, after),
+            [shape] * len(order),
+            [pltpu.VMEM((len(order), quarter, 8, 256), F32)],
+            smem=(0,),
+            free=(6,),
+            name=name,
+            us=us,
+        )
+
+    sent = states((1, 2, 3), cum, "states", 2.0)
+    others = [swap(x, d) for d, x in zip((1, 2, 3), sent)]
+    (own,) = states((0,), sent[0], "own_states", 0.8)
     edge = call(
         edge_kernel,
-        (win_key, values),
+        (win_key, values, own),
         jax.ShapeDtypeStruct((2 * WINDOW, values.shape[1]), BF16),
         [pltpu.SemaphoreType.DMA((2,))],
         far=(0, 1),
+        free=(2,),
         name="edge",
+        us=0.4,
     )
     halo = lax.ppermute(edge, "seq", [(i, i + 1) for i in range(count - 1)])
 
-    *sent, cum = call(
-        lambda *refs: state_kernel((1, 2, 3), *refs),
-        (group, k_feat, values, log_gates.T, conv_weight, table),
-        [shape] * 3 + [wide(heads, rows)],
-        [pltpu.VMEM((3, quarter, 8, 256), F32)],
-        smem=(0,),
-        name="states",
-    )
-    others = [swap(x, d) for d, x in zip((1, 2, 3), sent)]
-    own, column = call(
-        own_kernel,
-        (group, k_feat, values, cum, conv_weight, table, sent[0]),
-        [shape, wide(rows, heads)],
-        [norm_scratch],
-        smem=(0,),
-        free=(6,),
-        name="own_states",
-    )
-    win = call(
-        window_kernel,
-        (one(position > 0), win_query, win_key, values, halo, own),
-        wide(*values.shape),
-        smem=(0,),
-        free=(5,),
-        name="window",
+    phi, token = call(
+        query_kernel,
+        (q_feat, k_feat, cum, query_table(width), edge),
+        [jax.ShapeDtypeStruct((heads, rows, 256), BF16), wide(8, 128)],
+        free=(4,),
+        name="query_features",
+        us=1.5,
     )
     total, before, keys, small = call(
         lambda *refs: group_kernel(width, *refs),
-        (group, conv_weight, table, own, *others, win),
+        (place, conv_weight, table, own, *others, token),
         [shape, wide(3, quarter, ROWS, 128), wide(2, quarter, ROWS, 128), wide(quarter, 8, 128)],
         [held],
         smem=(0,),
         free=(7,),
         name="merge_group",
+        us=2.0,
     )
     base = jnp.zeros_like(total)
     live = position < 0
@@ -497,7 +514,7 @@
         def pair(left, right):
             return call(
                 lambda *refs: pair_kernel(width, *refs),
-                (group, conv_weight, table, left, right),
+                (place, conv_weight, table, left, right),
                 shape,
                 smem=(0,),
                 name="merge_pair",
@@ -511,37 +528,42 @@
         if 2 * distance < count:
             total = pair(jnp.where(upper, got, total), jnp.where(upper, total, got))
         distance *= 2
-    num, den = call(
+    num, den, token = call(
         block_kernel,
-        (q_feat, k_feat, values, conv_weight, cum, column, halo, last),
-        [wide(*values.shape)] * 2,
-        free=(7,),
+        (q_feat, k_feat, values, conv_weight, cum, last),
+        [wide(*values.shape)] * 2 + [wide(8, 128)],
+        free=(5,),
         name="block",
+        us=2.7,
     )
     here, *sent = call(
         spread_kernel,
-        (group, one(live), conv_weight, base, before, keys, small, num),
+        (place, conv_weight, base, before, keys, small, token),
         [shape] * 4,
         [held],
-        smem=(0, 1),
-        free=(7,),
+        smem=(0,),
+        free=(6,),
         name="spread",
+        us=1.0,
     )
     prefixes = [here] + [swap(x, d) for d, x in zip((1, 2, 3), sent)]
-    phi = call(
-        query_kernel,
-        (q_feat, column, query_table(width), here),
-        jax.ShapeDtypeStruct((heads, rows, 256), BF16),
-        free=(3,),
-        name="query_features",
+    win = call(
+        window_kernel,
+        (place, win_query, win_key, values, halo, here),
+        wide(*values.shape),
+        smem=(0,),
+        free=(5,),
+        name="window",
+        us=2.6,
     )
     return call(
         finish_kernel,
-        (group, phi, *prefixes, num, den, win),
+        (place, phi, *prefixes, num, den, win),
         jax.ShapeDtypeStruct(values.shape, BF16),
         [held],
         smem=(0,),
         name="finish",
+        us=2.1,
     )
 
 

time: 44.5 us -> 32.7 us (0.73)
  local copies, waits for them, and re-layouts: 9.76 us -> 1.94 us
  Pallas kernels: 16 us -> 13.7 us
  starting transfers between devices: 15.1 us -> 14.4 us
  waiting for transfers between devices: 2.97 us -> 2.3 us
    unnamed x44 -> x18, local copies, waits for them, and re-layouts: 9.76 us -> 1.94 us
    pallas_call x9 -> x10, Pallas kernels: 16 us -> 13.7 us  [call(): pl.pallas_call(kernel, out_shape=outs, in_specs=[pl.BlockSpec(memory_spac...]
    ppermute x1, starting transfers between devices: 5.02 us -> 3.56 us  [local(): halo = lax.ppermute(edge, 'seq', [(i, i + 1) for i in range(count - 1)])]
    ppermute x7, starting transfers between devices: 10.1 us -> 10.8 us  [swap(): return lax.ppermute(x, 'seq', [(i, i ^ distance) for i in range(count)])]
    ppermute x7, waiting for transfers between devices: 2.97 us -> 2.3 us  [swap(): return lax.ppermute(x, 'seq', [(i, i ^ distance) for i in range(count)])]
  transfers between devices with their start and end apart: 8 -> 8, of which waited for: 3 -> 1; matrix products, arithmetic and copies ran while one was open for 0% -> 0% of each run, Pallas kernels for 23% -> 29%
where the time goes in v3:
time: 32.7 us; the launch traced here: 32.5 us
  starting transfers between devices  14.4 us (44%)
  Pallas kernels  13.7 us (42%)
  waiting for transfers between devices  2.3 us (7%)
  local copies, waits for them, and re-layouts  1.94 us (6%)
    pallas_call x10, Pallas kernels, call(): pl.pallas_call(kernel, out_shape=outs, in_specs=[pl.BlockSpec(memory_spac...  13.7 us
    ppermute x7, starting transfers between devices, swap(): return lax.ppermute(x, 'seq', [(i, i ^ distance) for i in range(count)])  10.8 us
    ppermute x1, starting transfers between devices, local(): halo = lax.ppermute(edge, 'seq', [(i, i + 1) for i in range(count - 1)])  3.56 us
    ppermute x7, waiting for transfers between devices, swap(): return lax.ppermute(x, 'seq', [(i, i ^ distance) for i in range(count)])  2.3 us
    unnamed x18, local copies, waits for them, and re-layouts  1.94 us
  transfers between devices with their start and end apart: 8, of which 1 were waited for; matrix products, arithmetic and copies ran while one was open for 0% of the time, Pallas kernels for 29%

profile of v3, /device:TPU:0, one launch (start us, length us, event | category | flops | bytes accessed | tf_op | source)
XLA Modules:
  0.0 32.5 jit_solution(16412972052680920275)
XLA Ops:
  0.0 0.7 %copy-done.5 = f32[512,8]{0,1:T(8,128)S(1)} copy-done((f32[512,8]{0,1:T(8,128)S(1)}, f32[512,8]{0,1:T(8,128)}, u32[]{:S(2)}) %copy-start.5) | copy-done | bytes 16408
  0.7 0.3 %gates.1.refs_3_.refs_6_.cum_ref = f32[8,512]{1,0:T(8,128)S(1)} custom-call(s32[1]{0:T(128)} %bitcast.place_ref.refs_0_, f32[8,512]{1,0:T(8,128)S(1)} %bitcast.2), custom_call_target="tpu_custom_call" | custom-call | flops 17999998976 | bytes 54000000 | tf_op jit(solution)/shard_map/gates/pallas_call | solution.py:431
  1.1 0.9 %copy-done.1 = bf16[512,1024]{1,0:T(8,128)(2,1)S(1)} copy-done((bf16[512,1024]{1,0:T(8,128)(2,1)S(1)}, bf16[512,1024]{1,0:T(8,128)(2,1)}, u32[]{:S(2)}) %copy-start.1) | copy-done | bytes 1048600
  1.9 0.0 copy-done.7
  2.0 1.9 %states.1 = (bf16[2,160,128]{2,1,0:T(8,128)(2,1)S(1)}, bf16[2,160,128]{2,1,0:T(8,128)(2,1)S(1)}, bf16[2,160,128]{2,1,0:T(8,128)(2,1)S(1)}) custom-call(s32[1]{0:T(128)} %bitcast.place_ref.refs_0_, bf16[512,128]{1,0:T(8,128)(2,1)S(1)} %copy-done.4, bf16[512,1024]{1,0:T(8,128)(2,1)S(1)} %copy-done.1, f32[8,512]{1,0:T(8,128)S(1)} %gates.1.refs_3_.refs_6_.cum_ref, ...), custom_call_target="tpu_custom_call" | custom-call | flops 6000000000 | bytes 18000000 | tf_op jit(solution)/shard_map/states/pallas_call | solution.py:431
  3.9 3.1 %collective-permute-start.1 = (bf16[2,160,128]{2,1,0:T(8,128)(2,1)S(1)}, bf16[2,160,128]{2,1,0:T(8,128)(2,1)S(1)}, u32[]{:S(2)}, u32[]{:S(2)}) collective-permute-start(bf16[2,160,128]{2,1,0:T(8,128)(2,1)S(1)} %get-tuple-element.23), channel_id=1, source_target_pairs={{0,4},{2,6},{4,0},{6,2},{8,12},{10,14},{12,8},{14,10},{1,5},{3,7},... | collective-permute-start | bytes 245768 | tf_op jit(solution)/shard_map/ppermute | solution.py:457
  7.0 1.4 %collective-permute-start.2 = (bf16[2,160,128]{2,1,0:T(8,128)(2,1)S(1)}, bf16[2,160,128]{2,1,0:T(8,128)(2,1)S(1)}, u32[]{:S(2)}, u32[]{:S(2)}) collective-permute-start(bf16[2,160,128]{2,1,0:T(8,128)(2,1)S(1)} %get-tuple-element.24), channel_id=1, source_target_pairs={{0,6},{2,4},{4,2},{6,0},{8,14},{10,12},{12,10},{14,8},{1,7},{3,5},... | collective-permute-start | bytes 245768 | tf_op jit(solution)/shard_map/ppermute | solution.py:457
  8.4 0.1 collective-permute-start
  8.5 0.8 %own_states.1.after_ref.refs_3_ = bf16[2,160,128]{2,1,0:T(8,128)(2,1)S(1)} custom-call(s32[1]{0:T(128)} %bitcast.place_ref.refs_0_, bf16[512,128]{1,0:T(8,128)(2,1)S(1)} %copy-done.4, bf16[512,1024]{1,0:T(8,128)(2,1)S(1)} %copy-done.1, f32[8,512]{1,0:T(8,128)S(1)} %gates.1.refs_3_.refs_6_.cum_ref, f32[3,1024]{1,0:T(4,128)S(1)} %copy-done.6, ...), custom_call_target="tpu_custom_call" | custom-call | flops 2400000000 | bytes 7200000 | tf_op jit(solution)/shard_map/own_states/pallas_call | solution.py:431
  9.3 0.3 copy-done
  9.6 0.3 %edge.1.after_ref = bf16[128,1024]{1,0:T(8,128)(2,1)S(1)} custom-call(bf16[512,1024]{1,0:T(8,128)(2,1)S(1)} %copy-done, bf16[512,1024]{1,0:T(8,128)(2,1)S(1)} %copy-done.1, bf16[2,160,128]{2,1,0:T(8,128)(2,1)S(1)} %own_states.1.after_ref.refs_3_), custom_call_target="tpu_custom_call" | custom-call | flops 1200000000 | bytes 3600000 | tf_op jit(solution)/shard_map/edge/pallas_call | solution.py:431
  10.0 3.6 %collective-permute-start.7 = (bf16[128,1024]{1,0:T(8,128)(2,1)S(1)}, bf16[128,1024]{1,0:T(8,128)(2,1)S(1)}, u32[]{:S(2)}, u32[]{:S(2)}) collective-permute-start(bf16[128,1024]{1,0:T(8,128)(2,1)S(1)} %edge.1.after_ref), channel_id=1, source_target_pairs={{0,2},{2,4},{4,6},{6,8},{8,10},{10,12},{12,14},{1,3},{3,5},{5,7},{... | collective-permute-start | bytes 786440 | tf_op jit(solution)/shard_map/ppermute | solution.py:486
  13.5 0.0 copy-done.3
  13.6 1.9 %query_features.1 = (bf16[8,512,256]{2,1,0:T(8,128)(2,1)S(1)}, f32[8,128]{1,0:T(8,128)S(1)}) custom-call(bf16[512,128]{1,0:T(8,128)(2,1)S(1)} %copy-done.3, bf16[512,128]{1,0:T(8,128)(2,1)S(1)} %copy-done.4, f32[8,512]{1,0:T(8,128)S(1)} %gates.1.refs_3_.refs_6_.cum_ref, f32[8,256]{1,0:T(8,128)S(1)} %copy-done.8, bf16[128,1024]{1,0:T(8,128)(2,1)S(1)} %edge.1.after_ref), custom_call_target="tpu_custom_call" | custom-call | flops 4499999744 | bytes 13500000 | tf_op jit(solution)/shard_map/query_features/pallas_call | solution.py:431
  15.5 0.0 collective-permute-done.1.refs_5_
  15.5 0.0 collective-permute-done.2.refs_6_
  15.5 0.0 collective-permute-done.refs_4_
  15.5 0.9 %merge_group.1 = (bf16[2,160,128]{2,1,0:T(8,128)(2,1)S(1)}, f32[3,2,160,128]{3,2,1,0:T(8,128)S(1)}, f32[2,2,160,128]{3,2,1,0:T(8,128)S(1)}, f32[2,8,128]{2,1,0:T(8,128)S(1)}) custom-call(s32[1]{0:T(128)} %bitcast.place_ref.refs_0_, f32[3,1024]{1,0:T(4,128)S(1)} %copy-done.6, f32[160,128]{1,0:T(8,128)S(1)} %copy-done.7, ...), custom_call_target="tpu_custom_call" | custom-call | flops 6000000000 | bytes 18000000 | tf_op jit(solution)/shard_map/merge_group/pallas_call | solution.py:431
  16.4 2.7 %collective-permute-start.3 = (bf16[2,160,128]{2,1,0:T(8,128)(2,1)S(1)}, bf16[2,160,128]{2,1,0:T(8,128)(2,1)S(1)}, u32[]{:S(2)}, u32[]{:S(2)}) collective-permute-start(bf16[2,160,128]{2,1,0:T(8,128)(2,1)S(1)} %get-tuple-element.26.after_ref), channel_id=1, source_target_pairs={{0,8},{2,10},{4,12},{6,14},{8,0},{10,2},{12,4},{14,6},{1,9},{3,11}... | collective-permute-start | bytes 245768 | tf_op jit(solution)/shard_map/ppermute | solution.py:457
  19.1 2.9 %block.1 = (f32[512,1024]{1,0:T(8,128)S(1)}, f32[512,1024]{1,0:T(8,128)S(1)}, f32[8,128]{1,0:T(8,128)S(1)}) custom-call(bf16[512,128]{1,0:T(8,128)(2,1)S(1)} %copy-done.3, bf16[512,128]{1,0:T(8,128)(2,1)S(1)} %copy-done.4, bf16[512,1024]{1,0:T(8,128)(2,1)S(1)} %copy-done.1, f32[3,1024]{1,0:T(4,128)S(1)} %copy-done.6, ...), custom_call_target="tpu_custom_call" | custom-call | flops 8099999744 | bytes 24300000 | tf_op jit(solution)/shard_map/block/pallas_call | solution.py:431
  22.0 0.0 collective-permute-done.3.base_ref
  22.0 0.0 copy-start.2
  22.0 0.1 spread.1
  22.1 1.6 %collective-permute-start.4 = (bf16[2,160,128]{2,1,0:T(8,128)(2,1)S(1)}, bf16[2,160,128]{2,1,0:T(8,128)(2,1)S(1)}, u32[]{:S(2)}, u32[]{:S(2)}) collective-permute-start(bf16[2,160,128]{2,1,0:T(8,128)(2,1)S(1)} %get-tuple-element.32), channel_id=1, source_target_pairs={{0,2},{2,0},{4,6},{6,4},{8,10},{10,8},{12,14},{14,12},{1,3},{3,1},... | collective-permute-start | bytes 245768 | tf_op jit(solution)/shard_map/ppermute | solution.py:457
  23.7 1.5 %collective-permute-start.5 = (bf16[2,160,128]{2,1,0:T(8,128)(2,1)S(1)}, bf16[2,160,128]{2,1,0:T(8,128)(2,1)S(1)}, u32[]{:S(2)}, u32[]{:S(2)}) collective-permute-start(bf16[2,160,128]{2,1,0:T(8,128)(2,1)S(1)} %get-tuple-element.33), channel_id=1, source_target_pairs={{0,4},{2,6},{4,0},{6,2},{8,12},{10,14},{12,8},{14,10},{1,5},{3,7},... | collective-permute-start | bytes 245768 | tf_op jit(solution)/shard_map/ppermute | solution.py:457
  25.2 0.5 %collective-permute-start.6 = (bf16[2,160,128]{2,1,0:T(8,128)(2,1)S(1)}, bf16[2,160,128]{2,1,0:T(8,128)(2,1)S(1)}, u32[]{:S(2)}, u32[]{:S(2)}) collective-permute-start(bf16[2,160,128]{2,1,0:T(8,128)(2,1)S(1)} %get-tuple-element.34), channel_id=1, source_target_pairs={{0,6},{2,4},{4,2},{6,0},{8,14},{10,12},{12,10},{14,8},{1,7},{3,5},... | collective-permute-start | bytes 245768 | tf_op jit(solution)/shard_map/ppermute | solution.py:457
  25.7 0.0 collective-permute-done.7.halo_ref
  25.7 2.5 %window.1.win_ref = f32[512,1024]{1,0:T(8,128)S(1)} custom-call(s32[1]{0:T(128)} %bitcast.place_ref.refs_0_, bf16[512,1024]{1,0:T(8,128)(2,1)S(1)} %copy-done.2, bf16[512,1024]{1,0:T(8,128)(2,1)S(1)} %copy-done, bf16[512,1024]{1,0:T(8,128)(2,1)S(1)} %copy-done.1, bf16[128,1024]{1,0:T(8,128)(2,1)S(1)} %collective-permute-done.7.halo_ref, ...), custom_call_target="tpu_custom_call" | custom-call | flops 7800000000 | bytes 23400000 | tf_op jit(solution)/shard_map/window/pallas_call | solution.py:431
  28.3 0.0 collective-permute-done.4.x1
  28.3 0.0 collective-permute-done.5.x2
  28.3 2.3 %collective-permute-done.6.x3 = bf16[2,160,128]{2,1,0:T(8,128)(2,1)S(1)} collective-permute-done((bf16[2,160,128]{2,1,0:T(8,128)(2,1)S(1)}, bf16[2,160,128]{2,1,0:T(8,128)(2,1)S(1)}, u32[]{:S(2)}, u32[]{:S(2)}) %collective-permute-start.6) | collective-permute-done | bytes 81952 | tf_op jit(solution)/shard_map/ppermute | solution.py:457
  30.6 1.9 %finish.1 = bf16[512,1024]{1,0:T(8,128)(2,1)} custom-call(s32[1]{0:T(128)} %bitcast.place_ref.refs_0_, bf16[8,512,256]{2,1,0:T(8,128)(2,1)S(1)} %get-tuple-element.22.phi_ref, bf16[2,160,128]{2,1,0:T(8,128)(2,1)S(1)} %get-tuple-element.31.after_ref.x0, bf16[2,160,128]{2,1,0:T(8,128)(2,1)S(1)} %collective-permute-done.4.x1, ...), custom_call_target="tpu_custom_call" | custom-call | flops 6300000256 | bytes 18900000 | tf_op jit(solution)/shard_map/finish/pallas_call | solution.py:431
  (12 shorter events, 0.0 us)
Async XLA Ops:
  0.0 0.7 %copy-start.5 = (f32[512,8]{0,1:T(8,128)S(1)}, f32[512,8]{0,1:T(8,128)}, u32[]{:S(2)}) copy-start(f32[512,8]{0,1:T(8,128)} %param.14) | copy-start | bytes 49156
  0.7 1.2 %copy-start.1 = (bf16[512,1024]{1,0:T(8,128)(2,1)S(1)}, bf16[512,1024]{1,0:T(8,128)(2,1)}, u32[]{:S(2)}) copy-start(bf16[512,1024]{1,0:T(8,128)(2,1)} %v_ref.5) | copy-start | bytes 3145732
  0.7 1.2 %copy-start.4 = (bf16[512,128]{1,0:T(8,128)(2,1)S(1)}, bf16[512,128]{1,0:T(8,128)(2,1)}, u32[]{:S(2)}) copy-start(bf16[512,128]{1,0:T(8,128)(2,1)} %k_ref.5) | copy-start | bytes 393220
  0.7 1.2 %copy-start.6 = (f32[3,1024]{1,0:T(4,128)S(1)}, f32[3,1024]{1,0:T(4,128)}, u32[]{:S(2)}) copy-start(f32[3,1024]{1,0:T(4,128)} %w_ref.3) | copy-start | bytes 36868
  0.7 1.3 %copy-start.7 = (f32[160,128]{1,0:T(8,128)S(1)}, f32[160,128]{1,0:T(8,128)}, u32[]{:S(2)}) copy-start(f32[160,128]{1,0:T(8,128)} %constant.10.clone.refs_5_.refs_2_) | copy-start | bytes 245764
  3.9 11.6 %collective-permute-start.1 = (bf16[2,160,128]{2,1,0:T(8,128)(2,1)S(1)}, bf16[2,160,128]{2,1,0:T(8,128)(2,1)S(1)}, u32[]{:S(2)}, u32[]{:S(2)}) collective-permute-start(bf16[2,160,128]{2,1,0:T(8,128)(2,1)S(1)} %get-tuple-element.23), channel_id=1, source_target_pairs={{0,4},{2,6},{4,0},{6,2},{8,12},{10,14},{12,8},{14,10},{1,5},{3,7},... | collective-permute-start | bytes 245768 | tf_op jit(solution)/shard_map/ppermute | solution.py:457
  7.0 8.5 %collective-permute-start.2 = (bf16[2,160,128]{2,1,0:T(8,128)(2,1)S(1)}, bf16[2,160,128]{2,1,0:T(8,128)(2,1)S(1)}, u32[]{:S(2)}, u32[]{:S(2)}) collective-permute-start(bf16[2,160,128]{2,1,0:T(8,128)(2,1)S(1)} %get-tuple-element.24), channel_id=1, source_target_pairs={{0,6},{2,4},{4,2},{6,0},{8,14},{10,12},{12,10},{14,8},{1,7},{3,5},... | collective-permute-start | bytes 245768 | tf_op jit(solution)/shard_map/ppermute | solution.py:457
  8.4 1.2 %copy-start = (bf16[512,1024]{1,0:T(8,128)(2,1)S(1)}, bf16[512,1024]{1,0:T(8,128)(2,1)}, u32[]{:S(2)}) copy-start(bf16[512,1024]{1,0:T(8,128)(2,1)} %wk_ref.1) | copy-start | bytes 3145732
  8.4 7.1 %collective-permute-start = (bf16[2,160,128]{2,1,0:T(8,128)(2,1)S(1)}, bf16[2,160,128]{2,1,0:T(8,128)(2,1)S(1)}, u32[]{:S(2)}, u32[]{:S(2)}) collective-permute-start(bf16[2,160,128]{2,1,0:T(8,128)(2,1)S(1)} %get-tuple-element.21.refs_6_), channel_id=1, source_target_pairs={{0,2},{2,0},{4,6},{6,4},{8,10},{10,8},{12,14},{14,12},{1,3},{3,1},... | collective-permute-start | bytes 245768 | tf_op jit(solution)/shard_map/ppermute | solution.py:457
  9.6 3.9 %copy-start.3 = (bf16[512,128]{1,0:T(8,128)(2,1)S(1)}, bf16[512,128]{1,0:T(8,128)(2,1)}, u32[]{:S(2)}) copy-start(bf16[512,128]{1,0:T(8,128)(2,1)} %q_ref.3) | copy-start | bytes 393220
  9.6 3.9 %copy-start.8 = (f32[8,256]{1,0:T(8,128)S(1)}, f32[8,256]{1,0:T(8,128)}, u32[]{:S(2)}) copy-start(f32[8,256]{1,0:T(8,128)} %constant.11.clone.table_ref) | copy-start | bytes 24580
  10.0 15.7 %collective-permute-start.7 = (bf16[128,1024]{1,0:T(8,128)(2,1)S(1)}, bf16[128,1024]{1,0:T(8,128)(2,1)S(1)}, u32[]{:S(2)}, u32[]{:S(2)}) collective-permute-start(bf16[128,1024]{1,0:T(8,128)(2,1)S(1)} %edge.1.after_ref), channel_id=1, source_target_pairs={{0,2},{2,4},{4,6},{6,8},{8,10},{10,12},{12,14},{1,3},{3,5},{5,7},{... | collective-permute-start | bytes 786440 | tf_op jit(solution)/shard_map/ppermute | solution.py:486
  16.4 5.6 %collective-permute-start.3 = (bf16[2,160,128]{2,1,0:T(8,128)(2,1)S(1)}, bf16[2,160,128]{2,1,0:T(8,128)(2,1)S(1)}, u32[]{:S(2)}, u32[]{:S(2)}) collective-permute-start(bf16[2,160,128]{2,1,0:T(8,128)(2,1)S(1)} %get-tuple-element.26.after_ref), channel_id=1, source_target_pairs={{0,8},{2,10},{4,12},{6,14},{8,0},{10,2},{12,4},{14,6},{1,9},{3,11}... | collective-permute-start | bytes 245768 | tf_op jit(solution)/shard_map/ppermute | solution.py:457
  22.0 3.7 %copy-start.2 = (bf16[512,1024]{1,0:T(8,128)(2,1)S(1)}, bf16[512,1024]{1,0:T(8,128)(2,1)}, u32[]{:S(2)}) copy-start(bf16[512,1024]{1,0:T(8,128)(2,1)} %wq_ref.1) | copy-start | bytes 3145732
  22.1 6.1 %collective-permute-start.4 = (bf16[2,160,128]{2,1,0:T(8,128)(2,1)S(1)}, bf16[2,160,128]{2,1,0:T(8,128)(2,1)S(1)}, u32[]{:S(2)}, u32[]{:S(2)}) collective-permute-start(bf16[2,160,128]{2,1,0:T(8,128)(2,1)S(1)} %get-tuple-element.32), channel_id=1, source_target_pairs={{0,2},{2,0},{4,6},{6,4},{8,10},{10,8},{12,14},{14,12},{1,3},{3,1},... | collective-permute-start | bytes 245768 | tf_op jit(solution)/shard_map/ppermute | solution.py:457
  23.7 4.5 %collective-permute-start.5 = (bf16[2,160,128]{2,1,0:T(8,128)(2,1)S(1)}, bf16[2,160,128]{2,1,0:T(8,128)(2,1)S(1)}, u32[]{:S(2)}, u32[]{:S(2)}) collective-permute-start(bf16[2,160,128]{2,1,0:T(8,128)(2,1)S(1)} %get-tuple-element.33), channel_id=1, source_target_pairs={{0,4},{2,6},{4,0},{6,2},{8,12},{10,14},{12,8},{14,10},{1,5},{3,7},... | collective-permute-start | bytes 245768 | tf_op jit(solution)/shard_map/ppermute | solution.py:457
  25.2 5.3 %collective-permute-start.6 = (bf16[2,160,128]{2,1,0:T(8,128)(2,1)S(1)}, bf16[2,160,128]{2,1,0:T(8,128)(2,1)S(1)}, u32[]{:S(2)}, u32[]{:S(2)}) collective-permute-start(bf16[2,160,128]{2,1,0:T(8,128)(2,1)S(1)} %get-tuple-element.34), channel_id=1, source_target_pairs={{0,6},{2,4},{4,2},{6,0},{8,14},{10,12},{12,10},{14,8},{1,7},{3,5},... | collective-permute-start | bytes 245768 | tf_op jit(solution)/shard_map/ppermute | solution.py:457

commit v4 on v3

--- a/solution.py
+++ b/solution.py
@@ -42,15 +42,36 @@
     return jnp.asarray(np.where(table < 0, -1000, table), F32)
 
 
-def query_table(width):
-    first, second, one_a, one_b, scale, twice = feature_tables(width)
-    table = np.zeros((8, 256), np.float32)
-    table[:2] = -1000
-    for row, line in enumerate((first, second, one_a, one_b, scale * twice)):
-        table[row, :ROWS] = np.where(line < 0, -1000, line)
-    table[2:4, EDGE : EDGE + 2] = 1.0
-    table[4:6, EDGE : EDGE + 2] = 0.5
-    return jnp.asarray(table, F32)
+def wide_rows(width):
+    half = width // 2
+    pair = lambda i, j: i * width + j if i < half else half * width + (i - half) * half + j - half
+    linear = half * width + half * half
+    return pair, linear, linear + width
+
+
+def picks(width):
+    first, second, _, _, _, twice = feature_tables(width)
+    pair, linear, constant = wide_rows(width)
+    keys = np.zeros((ROWS, constant + 16), np.float32)
+    keys[0, constant] = 1.0
+    for row in range(1, ROWS):
+        if second[row] >= 0:
+            keys[row, pair(first[row], second[row])] = 1.0
+        elif first[row] >= 0:
+            keys[row, linear + first[row]] = 1.0
+    queries = keys * twice[:, None]
+    queries[EDGE, constant + 1] = 1.0
+    queries[EDGE + 1, constant + 2] = 1.0
+    return jnp.asarray(keys, BF16), jnp.asarray(queries, BF16)
+
+
+def products(x, factor):
+    width = x.shape[0]
+    half = width // 2
+    scaled = x * (factor * (2.0 * width) ** (-0.5))
+    blocks = [x * scaled[i : i + 1] for i in range(half)]
+    blocks += [x[half:] * scaled[i : i + 1] for i in range(half, width)]
+    return blocks + [x * (factor * width ** (-0.25))]
 
 
 def nt(a, b):
@@ -99,46 +120,29 @@
     return jnp.where(iota(x.shape, 0) < by, 0.0, pltpu.roll(x, by, 0))
 
 
-def edge_kernel(k_ref, v_ref, after_ref, out_ref, sems):
-    rows = k_ref.shape[0]
-    copies = [
-        pltpu.make_async_copy(
-            ref.at[pl.ds(rows - WINDOW, WINDOW)], out_ref.at[pl.ds(i * WINDOW, WINDOW)], sems.at[i]
-        )
-        for i, ref in enumerate((k_ref, v_ref))
-    ]
-    for copy in copies:
-        copy.start()
-    for copy in copies:
-        copy.wait()
-
-
-def one_state(head, out_ref, j, k, v_ref, w_ref, cum_ref, norm_ref, table):
-    rows, wide = k.shape
+def one_state(head, out_ref, j, k_ref, turned_ref, v_ref, w_ref, cum_ref, norm_ref, pick):
+    rows, wide = k_ref.shape
     heads = cum_ref.shape[0]
     width = wide // heads
-    first, second, one_a, one_b, scale = table
-    lane = iota((ROWS, wide), 1).astype(F32)
     lane1 = iota((1, 128), 1)
     sub = iota((8, 128), 0)
     at = pl.ds(pl.multiple_of(head * 128, 128), 128)
-    shift = (head * width).astype(F32)
-    pick_a = (lane == first + shift).astype(BF16)
-    pick_b = (lane == second + shift).astype(BF16)
     cum = cum_ref[pl.ds(head, 1), :]
     last = cum[:, rows - 1 :]
     keep = jnp.exp(last - cum)
-    wide4 = lambda x: jnp.concatenate([x] * (rows // 128), axis=1)
-    phi = (((nt(pick_a, k) + wide4(one_a)) * (nt(pick_b, k) + wide4(one_b)) * wide4(scale)) * keep).astype(BF16)
+    k = turned_ref[pl.ds(pl.multiple_of(head * width, width), width), :]
+    constant = jnp.where(iota((16, rows), 0) == 0, keep, 0.0)
+    phi = jnp.concatenate(products(k, keep) + [constant]).astype(BF16)
     v = v_ref[:, at].astype(F32)
     w = w_ref[:, at]
     conv = (w[0:1] * v + w[1:2] * shifted(v, 1) + w[2:3] * shifted(v, 2)).astype(BF16)
-    state = nn(phi, conv)
-    norm_ref[j, :, 0:ROWS] = nt(jnp.ones((8, rows), BF16), phi)
-    norm = norm_ref[j, 0:1, :]
+    state = nn(pick, nn(phi, conv).astype(BF16))
+    norm = nt(jnp.ones((8, rows), BF16), phi)
     high = norm.astype(BF16).astype(F32)
-    low = norm - high
-    keys8 = k[0:16].astype(F32)[0:8]
+    norm = jnp.where(iota(norm.shape, 0) == 0, high, norm - high).astype(BF16)
+    norm_ref[j, :, 0:ROWS] = nt(norm, pick)
+    high, low = norm_ref[j, 0:1, :], norm_ref[j, 1:2, :]
+    keys8 = k_ref[0:16].astype(F32)[0:8]
     turned = pltpu.roll(keys8, (wide - head * width) % wide, 1)
     turned2 = pltpu.roll(keys8, (wide - head * width + width) % wide, 1)
     misc = jnp.where(lane1 < width, turned[0:1], 0.0)
@@ -156,20 +160,30 @@
     out_ref[j, ROWS - 16 :, :] = jnp.concatenate([state[ROWS - 16 : ROWS - 8], tail]).astype(BF16)
 
 
-def gate_kernel(place_ref, g_ref, cum_ref):
+def open_kernel(place_ref, token_ref):
+    token_ref[...] = jnp.zeros(token_ref.shape, F32)
+
+
+def gate_kernel(g_ref, k_ref, after_ref, cum_ref, turned_ref):
     cum_ref[...] = cumulative_rows(g_ref[...])
-
-
-def state_kernel(order, place_ref, k_ref, v_ref, cum_ref, w_ref, table_ref, after_ref, *refs):
+    turned_ref[...] = k_ref[...].astype(F32).T
+
+
+def state_kernel(order, place_ref, k_ref, turned_ref, v_ref, cum_ref, w_ref, pick_ref, after_ref, *refs):
     outs, norm_ref = refs[:-1], refs[-1]
     norm_ref[...] = jnp.zeros(norm_ref.shape, F32)
-    table = columns_of(table_ref)
-    k = k_ref[...]
+    pick = pick_ref[...]
     for i, (out_ref, distance) in enumerate(zip(outs, order)):
         count = out_ref.shape[0]
         for j in range(count):
             head = ((place_ref[0] & 3) ^ distance) * count + j
-            one_state(head, out_ref, j, k, v_ref, w_ref, cum_ref, norm_ref.at[i], table)
+            one_state(head, out_ref, j, k_ref, turned_ref, v_ref, w_ref, cum_ref, norm_ref.at[i], pick)
+
+
+def own_kernel(place_ref, k_ref, turned_ref, v_ref, cum_ref, w_ref, pick_ref, after_ref, win_key_ref, out_ref, edge_ref, norm_ref):
+    edge_ref[:WINDOW] = win_key_ref[win_key_ref.shape[0] - WINDOW :]
+    edge_ref[WINDOW:] = v_ref[v_ref.shape[0] - WINDOW :]
+    state_kernel((0,), place_ref, k_ref, turned_ref, v_ref, cum_ref, w_ref, pick_ref, after_ref, out_ref, norm_ref)
 
 
 def tail_of(tile):
@@ -316,40 +330,45 @@
     start = valid & ((seen >= half) | (place_ref[0] > 0))
     steps = rows // half
     ones = jnp.ones((rows + half, 128), BF16)
+    zeros = jnp.zeros((rows + half, 128), BF16)
     heads = wq_ref.shape[1] // 128
-    for pair in range(0, heads, 2):
-        scores, right = [], []
-        for h in range(pair, pair + 2):
+    spans = [slice(i * half, (i + 2) * half) for i in range(steps)]
+    for four in range(0, heads, 4):
+        scores = []
+        for h in range(four, four + 4, 2):
+            one, two = slice(128 * h, 128 * h + 128), slice(128 * h + 128, 128 * h + 256)
+            upper = jnp.concatenate([jnp.concatenate([halo_ref[:half, one], wk_ref[:, one]]), zeros], axis=1)
+            lower = jnp.concatenate([zeros, jnp.concatenate([halo_ref[:half, two], wk_ref[:, two]])], axis=1)
+            queries = wq_ref[:, 128 * h : 128 * h + 256]
+            s = [nt(queries[i * half : (i + 1) * half], jnp.concatenate([upper[span], lower[span]])) for i, span in enumerate(spans)]
+            scores += [[x[:, :128] for x in s], [x[:, 128:] for x in s]]
+        probs = []
+        for s in scores:
+            s = jnp.concatenate([jnp.where(valid if i else start, x * (128 ** (-0.5) * LOG2E), -jnp.inf) for i, x in enumerate(s)])
+            probs.append(jnp.exp2(s - jnp.max(s, axis=1, keepdims=True)).astype(BF16))
+        for h, p in zip(range(four, four + 4), probs):
             at = slice(128 * h, 128 * h + 128)
-            keys = jnp.concatenate([halo_ref[:half, at], wk_ref[:, at]])
-            right.append(jnp.concatenate([jnp.concatenate([halo_ref[half:, at], v_ref[:, at]]), ones], axis=1))
-            scores.append([nt(wq_ref[i * half : (i + 1) * half, at], keys[i * half : (i + 2) * half]) for i in range(steps)])
-        probs = []
-        for group in scores:
-            group = [jnp.where(start if i == 0 else valid, s * (128 ** (-0.5) * LOG2E), -jnp.inf) for i, s in enumerate(group)]
-            s = jnp.concatenate(group)
-            probs.append(jnp.exp2(s - jnp.max(s, axis=1, keepdims=True)).astype(BF16))
-        for h, p, r in zip(range(pair, pair + 2), probs, right):
-            both = jnp.concatenate([nn(p[i * half : (i + 1) * half], r[i * half : (i + 2) * half]) for i in range(steps)])
-            win_ref[:, 128 * h : 128 * h + 128] = both[:, :128] / both[:, 128:]
-
-
-def block_kernel(q_ref, k_ref, v_ref, w_ref, cum_ref, after_ref, num_ref, den_ref, token_ref):
+            right = jnp.concatenate([jnp.concatenate([halo_ref[half:, at], v_ref[:, at]]), ones], axis=1)
+            both = jnp.concatenate([nn(p[i * half : (i + 1) * half], right[span]) for i, span in enumerate(spans)])
+            win_ref[:, at] = both[:, :128] / both[:, 128:]
+
+
+def block_kernel(q_ref, turned_ref, v_ref, w_ref, cum_ref, after_ref, num_ref, den_ref, token_ref):
     rows, wide = q_ref.shape
     heads = cum_ref.shape[0]
     width = wide // heads
     q = q_ref[...]
-    k = k_ref[...]
     cum_row = cum_ref[...] * LOG2E
     cum_col = cum_row.T
     token_ref[...] = jnp.zeros(token_ref.shape, F32)
-    lane = iota(k.shape, 1)
+    level = iota(turned_ref.shape, 0)
     step, piece = 256, 128
     ones = jnp.ones((rows, 128), BF16)
     causal = iota((piece, piece), 0) >= iota((piece, piece), 1)
     for h in range(heads):
         at = slice(128 * h, 128 * h + 128)
-        k_here = jnp.where((lane >= h * width) & (lane < (h + 1) * width), k, jnp.zeros_like(k)) * BF16(width ** (-0.5))
+        here = (level >= h * width) & (level < (h + 1) * width)
+        k_here = jnp.where(here, turned_ref[...] * width ** (-0.5), 0.0).astype(BF16)
         v = v_ref[:, at].astype(F32)
         w = w_ref[:, at]
         conv = w[0:1] * v + w[1:2] * shifted(v, 1) + w[2:3] * shifted(v, 2)
@@ -357,7 +376,7 @@
         column = jnp.broadcast_to(cum_col[:, h : h + 1], (rows, piece))
         total = None
         for low in range(0, rows, step):
-            x = nt(q[low:], k_here[low : low + step])
+            x = nn(q[low:], k_here[:, low : low + step])
             lines = []
             for i in range(low, rows, piece):
                 line = []
@@ -377,34 +396,33 @@
         den_ref[:, at] = total[:, 128:]
 
 
-def query_kernel(q_ref, k_ref, cum_ref, table_ref, after_ref, out_ref, token_ref):
+def query_kernel(q_ref, k_ref, cum_ref, pick_ref, after_ref, out_ref):
     rows, wide = q_ref.shape
     heads = cum_ref.shape[0]
     width = wide // heads
     q = q_ref[...]
-    column = cum_ref[...].T
-    token_ref[...] = jnp.zeros(token_ref.shape, F32)
-    row = iota((wide, 256), 0)
-    lane = iota((wide, 256), 1)
-    keys = k_ref[0:16].astype(F32)[0:8].T * width ** (-0.5)
-    keys = jnp.where(lane == EDGE, keys[:, 0:1], jnp.where(lane == EDGE + 1, keys[:, 1:2], 0.0))
-    first, second, one_a, one_b, scale, plus = (table_ref[i : i + 1] for i in range(6))
-    side = iota((1, 128), 1) + 128
-    early = (iota((rows, 128), 0) == 0) & (iota((rows, 128), 1) == EDGE + 1 - 128)
+    turned = q.astype(F32).T
+    pick = pick_ref[...]
+    keys = k_ref[0:16].astype(F32)[0:8] * width ** (-0.5)
+    line = iota((2 * heads, wide), 0)
+    lane = iota((2 * heads, wide), 1)
+    keys = jnp.where(line < heads, keys[0:1], keys[1:2])
+    low = jnp.where(line < heads, line, line - heads) * width
+    x = nt(jnp.where((lane >= low) & (lane < low + width), keys, 0.0).astype(BF16), q)
+    x = (0.5 * x + 1.0) * x + 1.0
+    sub = iota((16, rows), 0)
+    at = iota((1, rows), 1)
     for h in range(heads):
-        here = (row >= h * width) & (row < (h + 1) * width)
-        keys_here = jnp.where(here, keys, 0.0)
-        pick_a = jnp.where(row.astype(F32) == first + h * width, 1.0, keys_here).astype(BF16)
-        pick_b = jnp.where(row.astype(F32) == second + h * width, 1.0, keys_here).astype(BF16)
-        phi = (nn(q, pick_a) + one_a) * (nn(q, pick_b) + one_b) * scale + plus
-        since = column[:, h : h + 1]
-        offset = jnp.where(side == EDGE, since[0:1], jnp.where(side == EDGE + 1, since[1:2], 0.0))
-        enter = jnp.where(early, 0.0, jnp.exp(since - offset))
-        out_ref[h, :, :128] = (phi[:, :128] * jnp.exp(since)).astype(BF16)
-        out_ref[h, :, 128:] = (phi[:, 128:] * enter).astype(BF16)
-
-
-def finish_kernel(place_ref, phi_ref, x0, x1, x2, x3, num_ref, den_ref, win_ref, out_ref, held):
+        cum = cum_ref[h : h + 1, :]
+        enter = jnp.exp(cum)
+        score0 = x[h : h + 1] * jnp.exp(cum - cum[:, 0:1])
+        score1 = x[heads + h : heads + h + 1] * jnp.exp(jnp.where(at < 1, -jnp.inf, cum - cum[:, 1:2]))
+        rest = jnp.where(sub == 0, enter, jnp.where(sub == 1, score0, jnp.where(sub == 2, score1, 0.0)))
+        phi = jnp.concatenate(products(turned[h * width : (h + 1) * width], enter) + [rest]).astype(BF16)
+        out_ref[h, :, 0:ROWS] = nn(pick, phi).astype(BF16).T
+
+
+def finish_kernel(place_ref, phi_ref, x0, x1, x2, x3, num_ref, den_ref, win_ref, out_far, held, out_ref, sems):
     group = (place_ref[0] & 3)
     heads = phi_ref.shape[0]
     count = x0.shape[0]
@@ -416,15 +434,20 @@
         tail = tile[ROWS - 16 :].astype(F32)[8:]
         lines.append(jnp.concatenate([tail[1:2] + tail[3:4], tail[2:3] + tail[4:5]], axis=1))
     norms = jnp.concatenate(lines).T
+    copies = []
     for h in range(heads):
         at = slice(128 * h, 128 * h + 128)
         norm = jnp.broadcast_to(norms[:ROWS, h : h + 1], (ROWS, 128)).astype(BF16)
         both = nn(phi_ref[h][:, :ROWS], jnp.concatenate([tiles[h], norm], axis=1))
         out = (num_ref[:, at] + both[:, :128]) / (den_ref[:, at] + both[:, 128:]) + win_ref[:, at]
-        out_ref[:, at] = out.astype(BF16)
-
-
-def call(kernel, inputs, outs, scratch=(), smem=(), free=(), far=(), name=None, us=1.0):
+        out_ref[h] = out.astype(BF16)
+        copies.append(pltpu.make_async_copy(out_ref.at[h], out_far.at[:, pl.ds(128 * h, 128)], sems.at[h]))
+        copies[-1].start()
+    for copy in copies:
+        copy.wait()
+
+
+def call(kernel, inputs, outs, scratch=(), smem=(), free=(), far=(), name=None, us=1.0, out_space=pltpu.VMEM):
     def space(i):
         return pltpu.SMEM if i in smem else pl.ANY if i in free else pltpu.HBM if i in far else pltpu.VMEM
 
@@ -432,7 +455,7 @@
         kernel,
         out_shape=outs,
         in_specs=[pl.BlockSpec(memory_space=space(i)) for i in range(len(inputs))],
-        out_specs=jax.tree.map(lambda _: pl.BlockSpec(memory_space=pltpu.VMEM), outs),
+        out_specs=jax.tree.map(lambda _: pl.BlockSpec(memory_space=out_space), outs),
         scratch_shapes=scratch,
         compiler_params=pltpu.CompilerParams(vmem_limit_bytes=VMEM_LIMIT),
         name=name,
@@ -449,6 +472,7 @@
     one = lambda number: jnp.reshape(number, (1,)).astype(jnp.int32)
     place = one(position)
     table = key_table(width)
+    pick_keys, pick_queries = picks(width)
     shape = jax.ShapeDtypeStruct((quarter, ROWS, 128), BF16)
     wide = lambda *dims: jax.ShapeDtypeStruct(dims, F32)
     held = pltpu.VMEM((4, quarter, ROWS, 128), BF16)
@@ -456,46 +480,42 @@
     def swap(x, distance):
         return lax.ppermute(x, "seq", [(i, i ^ distance) for i in range(count)])
 
-    cum = call(gate_kernel, (place, log_gates.T), wide(heads, rows), smem=(0,), name="gates", us=6.0)
-
-    def states(order, after, name, us):
-        return call(
-            lambda *refs: state_kernel(order, *refs),
-            (place, k_feat, values, cum, conv_weight, table, after),
-            [shape] * len(order),
-            [pltpu.VMEM((len(order), quarter, 8, 256), F32)],
-            smem=(0,),
-            free=(6,),
-            name=name,
-            us=us,
-        )
-
-    sent = states((1, 2, 3), cum, "states", 2.0)
+    token = call(open_kernel, (place,), wide(8, 128), smem=(0,), name="open", us=6.0)
+    cum, turned = call(
+        gate_kernel,
+        (log_gates.T, k_feat, token),
+        [wide(heads, rows), wide(k_feat.shape[1], rows)],
+        free=(2,),
+        name="gates",
+        us=0.01,
+    )
+
+    sent = call(
+        lambda *refs: state_kernel((1, 2, 3), *refs),
+        (place, k_feat, turned, values, cum, conv_weight, pick_keys, cum),
+        [shape] * 3,
+        [pltpu.VMEM((3, quarter, 8, 256), F32)],
+        smem=(0,),
+        free=(7,),
+        name="states",
+        us=2.0,
+    )
     others = [swap(x, d) for d, x in zip((1, 2, 3), sent)]
-    (own,) = states((0,), sent[0], "own_states", 0.8)
-    edge = call(
-        edge_kernel,
-        (win_key, values, own),
-        jax.ShapeDtypeStruct((2 * WINDOW, values.shape[1]), BF16),
-        [pltpu.SemaphoreType.DMA((2,))],
-        far=(0, 1),
-        free=(2,),
-        name="edge",
-        us=0.4,
+    own, edge = call(
+        own_kernel,
+        (place, k_feat, turned, values, cum, conv_weight, pick_keys, sent[0], win_key),
+        [shape, jax.ShapeDtypeStruct((2 * WINDOW, values.shape[1]), BF16)],
+        [pltpu.VMEM((1, quarter, 8, 256), F32)],
+        smem=(0,),
+        free=(7,),
+        name="own_states",
+        us=0.8,
     )
     halo = lax.ppermute(edge, "seq", [(i, i + 1) for i in range(count - 1)])
 
-    phi, token = call(
-        query_kernel,
-        (q_feat, k_feat, cum, query_table(width), edge),
-        [jax.ShapeDtypeStruct((heads, rows, 256), BF16), wide(8, 128)],
-        free=(4,),
-        name="query_features",
-        us=1.5,
-    )
     total, before, keys, small = call(
         lambda *refs: group_kernel(width, *refs),
-        (place, conv_weight, table, own, *others, token),
+        (place, conv_weight, table, own, *others, edge),
         [shape, wide(3, quarter, ROWS, 128), wide(2, quarter, ROWS, 128), wide(quarter, 8, 128)],
         [held],
         smem=(0,),
@@ -530,7 +550,7 @@
         distance *= 2
     num, den, token = call(
         block_kernel,
-        (q_feat, k_feat, values, conv_weight, cum, last),
+        (q_feat, turned, values, conv_weight, cum, last),
         [wide(*values.shape)] * 2 + [wide(8, 128)],
         free=(5,),
         name="block",
@@ -547,9 +567,17 @@
         us=1.0,
     )
     prefixes = [here] + [swap(x, d) for d, x in zip((1, 2, 3), sent)]
+    phi = call(
+        query_kernel,
+        (q_feat, k_feat, cum, pick_queries, here),
+        jax.ShapeDtypeStruct((heads, rows, 256), BF16),
+        free=(4,),
+        name="query_features",
+        us=1.5,
+    )
     win = call(
         window_kernel,
-        (place, win_query, win_key, values, halo, here),
+        (place, win_query, win_key, values, halo, phi),
         wide(*values.shape),
         smem=(0,),
         free=(5,),
@@ -560,8 +588,9 @@
         finish_kernel,
         (place, phi, *prefixes, num, den, win),
         jax.ShapeDtypeStruct(values.shape, BF16),
-        [held],
+        [held, pltpu.VMEM((heads, rows, 128), BF16), pltpu.SemaphoreType.DMA((heads,))],
         smem=(0,),
+        out_space=pltpu.HBM,
         name="finish",
         us=2.1,
     )

time: 32.7 us -> 31.2 us (0.954)
  Pallas kernels: 13.7 us -> 11.6 us
  waiting for transfers between devices: 2.3 us -> 3.54 us
  local copies, waits for them, and re-layouts: 1.94 us -> 1.06 us
    pallas_call x10, Pallas kernels: 13.7 us -> 11.6 us  [call(): pl.pallas_call(kernel, out_shape=outs, in_specs=[pl.BlockSpec(memory_spac...]
    ppermute x7, waiting for transfers between devices: 2.3 us -> 3.54 us  [swap(): return lax.ppermute(x, 'seq', [(i, i ^ distance) for i in range(count)])]
    unnamed x18 -> x20, local copies, waits for them, and re-layouts: 1.94 us -> 1.06 us
  transfers between devices with their start and end apart: 8 -> 8, of which waited for: 1 -> 3; matrix products, arithmetic and copies ran while one was open for 0% -> 0% of each run, Pallas kernels for 29% -> 25%
where the time goes in v4:
time: 31.2 us; the launch traced here: 31 us
  starting transfers between devices  14.6 us (47%)
  Pallas kernels  11.6 us (37%)
  waiting for transfers between devices  3.54 us (11%)
  local copies, waits for them, and re-layouts  1.06 us (3%)
    pallas_call x10, Pallas kernels, call(): pl.pallas_call(kernel, out_shape=outs, in_specs=[pl.BlockSpec(memory_spac...  11.6 us
    ppermute x7, starting transfers between devices, swap(): return lax.ppermute(x, 'seq', [(i, i ^ distance) for i in range(count)])  10.8 us
    ppermute x1, starting transfers between devices, local(): halo = lax.ppermute(edge, 'seq', [(i, i + 1) for i in range(count - 1)])  3.81 us
    ppermute x7, waiting for transfers between devices, swap(): return lax.ppermute(x, 'seq', [(i, i ^ distance) for i in range(count)])  3.54 us
    unnamed x20, local copies, waits for them, and re-layouts  1.06 us
  transfers between devices with their start and end apart: 8, of which 3 were waited for; matrix products, arithmetic and copies ran while one was open for 0% of the time, Pallas kernels for 25%

profile of v4, /device:TPU:0, one launch (start us, length us, event | category | flops | bytes accessed | tf_op | source)
XLA Modules:
  0.0 31.0 jit_solution(14994425498369940404)
XLA Ops:
  0.0 0.9 %copy-done = bf16[512,128]{1,0:T(8,128)(2,1)S(1)} copy-done((bf16[512,128]{1,0:T(8,128)(2,1)S(1)}, bf16[512,128]{1,0:T(8,128)(2,1)}, u32[]{:S(2)}) %copy-start) | copy-done | bytes 131096
  0.9 0.4 %gates.1 = (f32[8,512]{1,0:T(8,128)S(1)}, f32[128,512]{1,0:T(8,128)S(1)}) custom-call(f32[8,512]{1,0:T(8,128)S(1)} %bitcast.2, bf16[512,128]{1,0:T(8,128)(2,1)S(1)} %copy-done, f32[8,128]{1,0:T(8,128)S(1)} %open.1.after_ref), custom_call_target="tpu_custom_call" | custom-call | flops 30000000 | bytes 90000 | tf_op jit(solution)/shard_map/gates/pallas_call | solution.py:454
  1.3 0.0 copy-done.2
  1.3 0.0 copy-done.6
  1.3 0.0 copy-start.3
  1.3 1.8 %states.1 = (bf16[2,160,128]{2,1,0:T(8,128)(2,1)S(1)}, bf16[2,160,128]{2,1,0:T(8,128)(2,1)S(1)}, bf16[2,160,128]{2,1,0:T(8,128)(2,1)S(1)}) custom-call(s32[1]{0:T(128)} %bitcast.place_ref.refs_0_, bf16[512,128]{1,0:T(8,128)(2,1)S(1)} %copy-done, f32[128,512]{1,0:T(8,128)S(1)} %get-tuple-element.24.refs_2_.turned_ref, bf16[512,1024]{1,0:T(8,128)(2,1)S(1)} %copy-done.2, ...), custom_call_target="tpu_custom_call" | custom-call | flops 6000000000 | bytes 18000000 | tf_op jit(solution)/shard_map/states/pallas_call | solution.py:454
  3.2 3.1 %collective-permute-start.1 = (bf16[2,160,128]{2,1,0:T(8,128)(2,1)S(1)}, bf16[2,160,128]{2,1,0:T(8,128)(2,1)S(1)}, u32[]{:S(2)}, u32[]{:S(2)}) collective-permute-start(bf16[2,160,128]{2,1,0:T(8,128)(2,1)S(1)} %get-tuple-element.27), channel_id=1, source_target_pairs={{0,4},{2,6},{4,0},{6,2},{8,12},{10,14},{12,8},{14,10},{1,5},{3,7},... | collective-permute-start | bytes 245768 | tf_op jit(solution)/shard_map/ppermute | solution.py:481
  6.3 1.4 %collective-permute-start.2 = (bf16[2,160,128]{2,1,0:T(8,128)(2,1)S(1)}, bf16[2,160,128]{2,1,0:T(8,128)(2,1)S(1)}, u32[]{:S(2)}, u32[]{:S(2)}) collective-permute-start(bf16[2,160,128]{2,1,0:T(8,128)(2,1)S(1)} %get-tuple-element.28), channel_id=1, source_target_pairs={{0,6},{2,4},{4,2},{6,0},{8,14},{10,12},{12,10},{14,8},{1,7},{3,5},... | collective-permute-start | bytes 245768 | tf_op jit(solution)/shard_map/ppermute | solution.py:481
  7.7 0.1 collective-permute-start
  7.8 0.0 copy-done.3
  7.8 0.7 %own_states.1 = (bf16[2,160,128]{2,1,0:T(8,128)(2,1)S(1)}, bf16[128,1024]{1,0:T(8,128)(2,1)S(1)}) custom-call(s32[1]{0:T(128)} %bitcast.place_ref.refs_0_, bf16[512,128]{1,0:T(8,128)(2,1)S(1)} %copy-done, f32[128,512]{1,0:T(8,128)S(1)} %get-tuple-element.24.refs_2_.turned_ref, bf16[512,1024]{1,0:T(8,128)(2,1)S(1)} %copy-done.2, ...), custom_call_target="tpu_custom_call" | custom-call | flops 2400000000 | bytes 7200000 | tf_op jit(solution)/shard_map/own_states/pallas_call | solution.py:454
  8.5 3.8 %collective-permute-start.7 = (bf16[128,1024]{1,0:T(8,128)(2,1)S(1)}, bf16[128,1024]{1,0:T(8,128)(2,1)S(1)}, u32[]{:S(2)}, u32[]{:S(2)}) collective-permute-start(bf16[128,1024]{1,0:T(8,128)(2,1)S(1)} %get-tuple-element.29.refs_7_), channel_id=1, source_target_pairs={{0,2},{2,4},{4,6},{6,8},{8,10},{10,12},{12,14},{1,3},{3,5},{5,7},{... | collective-permute-start | bytes 786440 | tf_op jit(solution)/shard_map/ppermute | solution.py:514
  12.4 0.0 collective-permute-done.1.refs_5_
  12.4 0.0 collective-permute-done.2.refs_6_
  12.4 0.5 %collective-permute-done.refs_4_ = bf16[2,160,128]{2,1,0:T(8,128)(2,1)S(1)} collective-permute-done((bf16[2,160,128]{2,1,0:T(8,128)(2,1)S(1)}, bf16[2,160,128]{2,1,0:T(8,128)(2,1)S(1)}, u32[]{:S(2)}, u32[]{:S(2)}) %collective-permute-start) | collective-permute-done | bytes 81952 | tf_op jit(solution)/shard_map/ppermute | solution.py:481
  12.9 0.0 copy-done.8
  12.9 0.9 %merge_group.1 = (bf16[2,160,128]{2,1,0:T(8,128)(2,1)S(1)}, f32[3,2,160,128]{3,2,1,0:T(8,128)S(1)}, f32[2,2,160,128]{3,2,1,0:T(8,128)S(1)}, f32[2,8,128]{2,1,0:T(8,128)S(1)}) custom-call(s32[1]{0:T(128)} %bitcast.place_ref.refs_0_, f32[3,1024]{1,0:T(4,128)S(1)} %copy-done.6, f32[160,128]{1,0:T(8,128)S(1)} %copy-done.8, ...), custom_call_target="tpu_custom_call" | custom-call | flops 6000000000 | bytes 18000000 | tf_op jit(solution)/shard_map/merge_group/pallas_call | solution.py:454
  13.9 2.7 %collective-permute-start.3 = (bf16[2,160,128]{2,1,0:T(8,128)(2,1)S(1)}, bf16[2,160,128]{2,1,0:T(8,128)(2,1)S(1)}, u32[]{:S(2)}, u32[]{:S(2)}) collective-permute-start(bf16[2,160,128]{2,1,0:T(8,128)(2,1)S(1)} %get-tuple-element.30.after_ref), channel_id=1, source_target_pairs={{0,8},{2,10},{4,12},{6,14},{8,0},{10,2},{12,4},{14,6},{1,9},{3,11}... | collective-permute-start | bytes 245768 | tf_op jit(solution)/shard_map/ppermute | solution.py:481
  16.5 2.7 %block.1 = (f32[512,1024]{1,0:T(8,128)S(1)}, f32[512,1024]{1,0:T(8,128)S(1)}, f32[8,128]{1,0:T(8,128)S(1)}) custom-call(bf16[512,128]{1,0:T(8,128)(2,1)S(1)} %copy-done.5, f32[128,512]{1,0:T(8,128)S(1)} %get-tuple-element.24.refs_2_.turned_ref, bf16[512,1024]{1,0:T(8,128)(2,1)S(1)} %copy-done.2, f32[3,1024]{1,0:T(4,128)S(1)} %copy-done.6, ...), custom_call_target="tpu_custom_call" | custom-call | flops 8099999744 | bytes 24300000 | tf_op jit(solution)/shard_map/block/pallas_call | solution.py:454
  19.2 1.0 %collective-permute-done.3.base_ref = bf16[2,160,128]{2,1,0:T(8,128)(2,1)S(1)} collective-permute-done((bf16[2,160,128]{2,1,0:T(8,128)(2,1)S(1)}, bf16[2,160,128]{2,1,0:T(8,128)(2,1)S(1)}, u32[]{:S(2)}, u32[]{:S(2)}) %collective-permute-start.3) | collective-permute-done | bytes 81952 | tf_op jit(solution)/shard_map/ppermute | solution.py:481
  20.2 0.1 spread.1
  20.4 0.2 collective-permute-start.4
  20.5 3.3 %collective-permute-start.5 = (bf16[2,160,128]{2,1,0:T(8,128)(2,1)S(1)}, bf16[2,160,128]{2,1,0:T(8,128)(2,1)S(1)}, u32[]{:S(2)}, u32[]{:S(2)}) collective-permute-start(bf16[2,160,128]{2,1,0:T(8,128)(2,1)S(1)} %get-tuple-element.37), channel_id=1, source_target_pairs={{0,4},{2,6},{4,0},{6,2},{8,12},{10,14},{12,8},{14,10},{1,5},{3,7},... | collective-permute-start | bytes 245768 | tf_op jit(solution)/shard_map/ppermute | solution.py:481
  23.9 0.0 collective-permute-start.6
  23.9 1.1 %query_features.1.after_ref.phi_ref = bf16[8,512,256]{2,1,0:T(8,128)(2,1)S(1)} custom-call(bf16[512,128]{1,0:T(8,128)(2,1)S(1)} %copy-done.5, bf16[512,128]{1,0:T(8,128)(2,1)S(1)} %copy-done, f32[8,512]{1,0:T(8,128)S(1)} %get-tuple-element.23.refs_4_.refs_7_.cum_ref, bf16[160,224]{1,0:T(8,128)(2,1)S(1)} %copy-done.7, ...), custom_call_target="tpu_custom_call" | custom-call | flops 4499999744 | bytes 13500000 | tf_op jit(solution)/shard_map/query_features/pallas_call | solution.py:454
  25.0 0.0 collective-permute-done.7.halo_ref
  25.0 0.1 copy-done.4
  25.2 2.1 %window.1.win_ref = f32[512,1024]{1,0:T(8,128)S(1)} custom-call(s32[1]{0:T(128)} %bitcast.place_ref.refs_0_, bf16[512,1024]{1,0:T(8,128)(2,1)S(1)} %copy-done.4, bf16[512,1024]{1,0:T(8,128)(2,1)S(1)} %copy-done.3, bf16[512,1024]{1,0:T(8,128)(2,1)S(1)} %copy-done.2, bf16[128,1024]{1,0:T(8,128)(2,1)S(1)} %collective-permute-done.7.halo_ref, ...), custom_call_target="tpu_custom_call" | custom-call | flops 7800000000 | bytes 23400000 | tf_op jit(solution)/shard_map/window/pallas_call | solution.py:454
  27.2 0.0 collective-permute-done.4.x1
  27.2 0.0 collective-permute-done.5.x2
  27.3 2.0 %collective-permute-done.6.x3 = bf16[2,160,128]{2,1,0:T(8,128)(2,1)S(1)} collective-permute-done((bf16[2,160,128]{2,1,0:T(8,128)(2,1)S(1)}, bf16[2,160,128]{2,1,0:T(8,128)(2,1)S(1)}, u32[]{:S(2)}, u32[]{:S(2)}) %collective-permute-start.6) | collective-permute-done | bytes 81952 | tf_op jit(solution)/shard_map/ppermute | solution.py:481
  29.2 1.8 %finish.1 = bf16[512,1024]{1,0:T(8,128)(2,1)} custom-call(s32[1]{0:T(128)} %bitcast.place_ref.refs_0_, bf16[8,512,256]{2,1,0:T(8,128)(2,1)S(1)} %query_features.1.after_ref.phi_ref, bf16[2,160,128]{2,1,0:T(8,128)(2,1)S(1)} %get-tuple-element.35.after_ref.x0, bf16[2,160,128]{2,1,0:T(8,128)(2,1)S(1)} %collective-permute-done.4.x1, ...), custom_call_target="tpu_custom_call" | custom-call | flops 6300000256 | bytes 18900000 | tf_op jit(solution)/shard_map/finish/pallas_call | solution.py:454
  (14 shorter events, 0.0 us)
Async XLA Ops:
  0.0 0.9 %copy-start = (bf16[512,128]{1,0:T(8,128)(2,1)S(1)}, bf16[512,128]{1,0:T(8,128)(2,1)}, u32[]{:S(2)}) copy-start(bf16[512,128]{1,0:T(8,128)(2,1)} %k_ref.5) | copy-start | bytes 393220
  0.0 0.9 %copy-start.1 = (f32[512,8]{0,1:T(8,128)S(1)}, f32[512,8]{0,1:T(8,128)}, u32[]{:S(2)}) copy-start(f32[512,8]{0,1:T(8,128)} %param.15) | copy-start | bytes 49156
  0.0 1.3 %copy-start.2 = (bf16[512,1024]{1,0:T(8,128)(2,1)S(1)}, bf16[512,1024]{1,0:T(8,128)(2,1)}, u32[]{:S(2)}) copy-start(bf16[512,1024]{1,0:T(8,128)(2,1)} %v_ref.5) | copy-start | bytes 3145732
  0.0 1.3 %copy-start.6 = (f32[3,1024]{1,0:T(4,128)S(1)}, f32[3,1024]{1,0:T(4,128)}, u32[]{:S(2)}) copy-start(f32[3,1024]{1,0:T(4,128)} %w_ref.5) | copy-start | bytes 36868
  0.0 1.3 %copy-start.9 = (bf16[160,224]{1,0:T(8,128)(2,1)S(1)}, bf16[160,224]{1,0:T(8,128)(2,1)}, u32[]{:S(2)}) copy-start(bf16[160,224]{1,0:T(8,128)(2,1)} %constant.13.clone.refs_6_.pick_ref) | copy-start | bytes 215044
  1.3 6.5 %copy-start.3 = (bf16[512,1024]{1,0:T(8,128)(2,1)S(1)}, bf16[512,1024]{1,0:T(8,128)(2,1)}, u32[]{:S(2)}) copy-start(bf16[512,1024]{1,0:T(8,128)(2,1)} %wk_ref.1) | copy-start | bytes 3145732
  3.2 9.2 %collective-permute-start.1 = (bf16[2,160,128]{2,1,0:T(8,128)(2,1)S(1)}, bf16[2,160,128]{2,1,0:T(8,128)(2,1)S(1)}, u32[]{:S(2)}, u32[]{:S(2)}) collective-permute-start(bf16[2,160,128]{2,1,0:T(8,128)(2,1)S(1)} %get-tuple-element.27), channel_id=1, source_target_pairs={{0,4},{2,6},{4,0},{6,2},{8,12},{10,14},{12,8},{14,10},{1,5},{3,7},... | collective-permute-start | bytes 245768 | tf_op jit(solution)/shard_map/ppermute | solution.py:481
  6.3 6.1 %collective-permute-start.2 = (bf16[2,160,128]{2,1,0:T(8,128)(2,1)S(1)}, bf16[2,160,128]{2,1,0:T(8,128)(2,1)S(1)}, u32[]{:S(2)}, u32[]{:S(2)}) collective-permute-start(bf16[2,160,128]{2,1,0:T(8,128)(2,1)S(1)} %get-tuple-element.28), channel_id=1, source_target_pairs={{0,6},{2,4},{4,2},{6,0},{8,14},{10,12},{12,10},{14,8},{1,7},{3,5},... | collective-permute-start | bytes 245768 | tf_op jit(solution)/shard_map/ppermute | solution.py:481
  7.7 5.3 %copy-start.8 = (f32[160,128]{1,0:T(8,128)S(1)}, f32[160,128]{1,0:T(8,128)}, u32[]{:S(2)}) copy-start(f32[160,128]{1,0:T(8,128)} %constant.12.clone.refs_2_) | copy-start | bytes 245764
  7.7 5.3 %collective-permute-start = (bf16[2,160,128]{2,1,0:T(8,128)(2,1)S(1)}, bf16[2,160,128]{2,1,0:T(8,128)(2,1)S(1)}, u32[]{:S(2)}, u32[]{:S(2)}) collective-permute-start(bf16[2,160,128]{2,1,0:T(8,128)(2,1)S(1)} %get-tuple-element.25.after_ref), channel_id=1, source_target_pairs={{0,2},{2,0},{4,6},{6,4},{8,10},{10,8},{12,14},{14,12},{1,3},{3,1},... | collective-permute-start | bytes 245768 | tf_op jit(solution)/shard_map/ppermute | solution.py:481
  8.5 16.5 %collective-permute-start.7 = (bf16[128,1024]{1,0:T(8,128)(2,1)S(1)}, bf16[128,1024]{1,0:T(8,128)(2,1)S(1)}, u32[]{:S(2)}, u32[]{:S(2)}) collective-permute-start(bf16[128,1024]{1,0:T(8,128)(2,1)S(1)} %get-tuple-element.29.refs_7_), channel_id=1, source_target_pairs={{0,2},{2,4},{4,6},{6,8},{8,10},{10,12},{12,14},{1,3},{3,5},{5,7},{... | collective-permute-start | bytes 786440 | tf_op jit(solution)/shard_map/ppermute | solution.py:514
  12.9 3.6 %copy-start.5 = (bf16[512,128]{1,0:T(8,128)(2,1)S(1)}, bf16[512,128]{1,0:T(8,128)(2,1)}, u32[]{:S(2)}) copy-start(bf16[512,128]{1,0:T(8,128)(2,1)} %q_ref.3) | copy-start | bytes 393220
  13.9 6.4 %collective-permute-start.3 = (bf16[2,160,128]{2,1,0:T(8,128)(2,1)S(1)}, bf16[2,160,128]{2,1,0:T(8,128)(2,1)S(1)}, u32[]{:S(2)}, u32[]{:S(2)}) collective-permute-start(bf16[2,160,128]{2,1,0:T(8,128)(2,1)S(1)} %get-tuple-element.30.after_ref), channel_id=1, source_target_pairs={{0,8},{2,10},{4,12},{6,14},{8,0},{10,2},{12,4},{14,6},{1,9},{3,11}... | collective-permute-start | bytes 245768 | tf_op jit(solution)/shard_map/ppermute | solution.py:481
  20.2 3.7 %copy-start.7 = (bf16[160,224]{1,0:T(8,128)(2,1)S(1)}, bf16[160,224]{1,0:T(8,128)(2,1)}, u32[]{:S(2)}) copy-start(bf16[160,224]{1,0:T(8,128)(2,1)} %constant.14.clone.pick_ref) | copy-start | bytes 215044
  20.4 6.9 %collective-permute-start.4 = (bf16[2,160,128]{2,1,0:T(8,128)(2,1)S(1)}, bf16[2,160,128]{2,1,0:T(8,128)(2,1)S(1)}, u32[]{:S(2)}, u32[]{:S(2)}) collective-permute-start(bf16[2,160,128]{2,1,0:T(8,128)(2,1)S(1)} %get-tuple-element.36), channel_id=1, source_target_pairs={{0,2},{2,0},{4,6},{6,4},{8,10},{10,8},{12,14},{14,12},{1,3},{3,1},... | collective-permute-start | bytes 245768 | tf_op jit(solution)/shard_map/ppermute | solution.py:481
  20.5 6.7 %collective-permute-start.5 = (bf16[2,160,128]{2,1,0:T(8,128)(2,1)S(1)}, bf16[2,160,128]{2,1,0:T(8,128)(2,1)S(1)}, u32[]{:S(2)}, u32[]{:S(2)}) collective-permute-start(bf16[2,160,128]{2,1,0:T(8,128)(2,1)S(1)} %get-tuple-element.37), channel_id=1, source_target_pairs={{0,4},{2,6},{4,0},{6,2},{8,12},{10,14},{12,8},{14,10},{1,5},{3,7},... | collective-permute-start | bytes 245768 | tf_op jit(solution)/shard_map/ppermute | solution.py:481
  23.9 5.3 %collective-permute-start.6 = (bf16[2,160,128]{2,1,0:T(8,128)(2,1)S(1)}, bf16[2,160,128]{2,1,0:T(8,128)(2,1)S(1)}, u32[]{:S(2)}, u32[]{:S(2)}) collective-permute-start(bf16[2,160,128]{2,1,0:T(8,128)(2,1)S(1)} %get-tuple-element.38), channel_id=1, source_target_pairs={{0,6},{2,4},{4,2},{6,0},{8,14},{10,12},{12,10},{14,8},{1,7},{3,5},... | collective-permute-start | bytes 245768 | tf_op jit(solution)/shard_map/ppermute | solution.py:481
  23.9 1.2 %copy-start.4 = (bf16[512,1024]{1,0:T(8,128)(2,1)S(1)}, bf16[512,1024]{1,0:T(8,128)(2,1)}, u32[]{:S(2)}) copy-start(bf16[512,1024]{1,0:T(8,128)(2,1)} %wq_ref.1) | copy-start | bytes 3145732

commit v5 on v4

--- a/solution.py
+++ b/solution.py
@@ -35,11 +35,16 @@
     return first, second, one_a, one_b, scale, twice
 
 
-def key_table(width):
+def key_tables(width):
     first, second, one_a, one_b, scale, _ = feature_tables(width)
-    table = np.zeros((ROWS, 128), np.float32)
-    table[:, :5] = np.stack([first, second, one_a, one_b, scale], axis=1)
-    return jnp.asarray(np.where(table < 0, -1000, table), F32)
+    pick = np.zeros((2, 2, ROWS, 128), np.float32)
+    for token in range(2):
+        for factor, index in enumerate((first, second)):
+            for row in range(ROWS):
+                if index[row] >= 0:
+                    pick[token, factor, row, token * width + index[row]] = 1.0
+    real = np.stack([np.repeat(x[:, None], 8, axis=1) for x in (one_a, one_b, scale)])
+    return jnp.asarray(pick.reshape(4 * ROWS, 128), BF16), jnp.asarray(real, F32)
 
 
 def wide_rows(width):
@@ -112,52 +117,62 @@
     return jnp.concatenate(done, axis=1)
 
 
-def columns_of(table_ref):
-    return [jnp.broadcast_to(table_ref[:, i : i + 1], (ROWS, 128)) for i in range(5)]
-
-
 def shifted(x, by):
     return jnp.where(iota(x.shape, 0) < by, 0.0, pltpu.roll(x, by, 0))
 
 
-def one_state(head, out_ref, j, k_ref, turned_ref, v_ref, w_ref, cum_ref, norm_ref, pick):
+def quarter_states(quarter, out_ref, k_ref, turned_ref, v_ref, w_ref, cum_ref, norm_ref, pick):
     rows, wide = k_ref.shape
     heads = cum_ref.shape[0]
     width = wide // heads
+    count = out_ref.shape[0]
     lane1 = iota((1, 128), 1)
     sub = iota((8, 128), 0)
-    at = pl.ds(pl.multiple_of(head * 128, 128), 128)
-    cum = cum_ref[pl.ds(head, 1), :]
-    last = cum[:, rows - 1 :]
-    keep = jnp.exp(last - cum)
-    k = turned_ref[pl.ds(pl.multiple_of(head * width, width), width), :]
-    constant = jnp.where(iota((16, rows), 0) == 0, keep, 0.0)
-    phi = jnp.concatenate(products(k, keep) + [constant]).astype(BF16)
-    v = v_ref[:, at].astype(F32)
-    w = w_ref[:, at]
-    conv = (w[0:1] * v + w[1:2] * shifted(v, 1) + w[2:3] * shifted(v, 2)).astype(BF16)
-    state = nn(pick, nn(phi, conv).astype(BF16))
-    norm = nt(jnp.ones((8, rows), BF16), phi)
-    high = norm.astype(BF16).astype(F32)
-    norm = jnp.where(iota(norm.shape, 0) == 0, high, norm - high).astype(BF16)
-    norm_ref[j, :, 0:ROWS] = nt(norm, pick)
-    high, low = norm_ref[j, 0:1, :], norm_ref[j, 1:2, :]
     keys8 = k_ref[0:16].astype(F32)[0:8]
-    turned = pltpu.roll(keys8, (wide - head * width) % wide, 1)
-    turned2 = pltpu.roll(keys8, (wide - head * width + width) % wide, 1)
-    misc = jnp.where(lane1 < width, turned[0:1], 0.0)
-    misc = jnp.where((lane1 >= width) & (lane1 < 2 * width), turned2[1:2], misc)
-    place = 2 * width
-    for value in (keep[:, 0:1], keep[:, 1:2], jnp.exp(last)):
-        for piece in parts(value):
-            misc = jnp.where(lane1 == place, piece.astype(F32), misc)
-            place += 1
-    tail = state[ROWS - 8 :]
-    for row, line in enumerate((high[:, :128], high[:, 128:], low[:, :128], low[:, 128:], misc)):
-        tail = jnp.where(sub == row + 1, line, tail)
-    tail = jnp.where(sub >= 6, v[rows - 8 :], tail)
-    out_ref[j, 0 : ROWS - 16, :] = state[: ROWS - 16].astype(BF16)
-    out_ref[j, ROWS - 16 :, :] = jnp.concatenate([state[ROWS - 16 : ROWS - 8], tail]).astype(BF16)
+    wides, norms, values, keeps, lasts = [], [], [], [], []
+    for j in range(count):
+        head = quarter * count + j
+        at = pl.ds(pl.multiple_of(head * 128, 128), 128)
+        cum = cum_ref[pl.ds(head, 1), :]
+        last = cum[:, rows - 1 :]
+        keep = jnp.exp(last - cum)
+        k = turned_ref[pl.ds(pl.multiple_of(head * width, width), width), :]
+        constant = jnp.where(iota((16, rows), 0) == 0, keep, 0.0)
+        phi = jnp.concatenate(products(k, keep) + [constant]).astype(BF16)
+        v = v_ref[:, at].astype(F32)
+        w = w_ref[:, at]
+        conv = (w[0:1] * v + w[1:2] * shifted(v, 1) + w[2:3] * shifted(v, 2)).astype(BF16)
+        wides.append(nn(phi, conv).astype(BF16))
+        norms.append(nt(jnp.ones((8, rows), BF16), phi))
+        values.append(v)
+        keeps.append(keep)
+        lasts.append(last)
+    states = nn(pick, jnp.concatenate(wides, axis=1))
+    line = iota(norms[0].shape, 0)
+    mixed = jnp.zeros(norms[0].shape, F32)
+    for j, norm in enumerate(norms):
+        high = norm.astype(BF16).astype(F32)
+        mixed = jnp.where(line == 2 * j, high, jnp.where(line == 2 * j + 1, norm - high, mixed))
+    norm_ref[:, 0:ROWS] = nt(mixed.astype(BF16), pick)
+    for j in range(count):
+        head = quarter * count + j
+        high, low = norm_ref[2 * j : 2 * j + 1, :], norm_ref[2 * j + 1 : 2 * j + 2, :]
+        turned = pltpu.roll(keys8, (wide - head * width) % wide, 1)
+        turned2 = pltpu.roll(keys8, (wide - head * width + width) % wide, 1)
+        misc = jnp.where(lane1 < width, turned[0:1], 0.0)
+        misc = jnp.where((lane1 >= width) & (lane1 < 2 * width), turned2[1:2], misc)
+        place = 2 * width
+        for value in (keeps[j][:, 0:1], keeps[j][:, 1:2], jnp.exp(lasts[j])):
+            for piece in parts(value):
+                misc = jnp.where(lane1 == place, piece.astype(F32), misc)
+                place += 1
+        state = states[:, 128 * j : 128 * j + 128]
+        tail = state[ROWS - 8 :]
+        for row, text in enumerate((high[:, :128], high[:, 128:], low[:, :128], low[:, 128:], misc)):
+            tail = jnp.where(sub == row + 1, text, tail)
+        tail = jnp.where(sub >= 6, values[j][rows - 8 :], tail)
+        out_ref[j, 0 : ROWS - 16, :] = state[: ROWS - 16].astype(BF16)
+        out_ref[j, ROWS - 16 :, :] = jnp.concatenate([state[ROWS - 16 : ROWS - 8], tail]).astype(BF16)
 
 
 def open_kernel(place_ref, token_ref):
@@ -174,16 +189,13 @@
     norm_ref[...] = jnp.zeros(norm_ref.shape, F32)
     pick = pick_ref[...]
     for i, (out_ref, distance) in enumerate(zip(outs, order)):
-        count = out_ref.shape[0]
-        for j in range(count):
-            head = ((place_ref[0] & 3) ^ distance) * count + j
-            one_state(head, out_ref, j, k_ref, turned_ref, v_ref, w_ref, cum_ref, norm_ref.at[i], pick)
-
-
-def own_kernel(place_ref, k_ref, turned_ref, v_ref, cum_ref, w_ref, pick_ref, after_ref, win_key_ref, out_ref, edge_ref, norm_ref):
+        quarter = (place_ref[0] & 3) ^ distance
+        quarter_states(quarter, out_ref, k_ref, turned_ref, v_ref, w_ref, cum_ref, norm_ref.at[i], pick)
+
+
+def edge_kernel(win_key_ref, v_ref, after_ref, edge_ref):
     edge_ref[:WINDOW] = win_key_ref[win_key_ref.shape[0] - WINDOW :]
     edge_ref[WINDOW:] = v_ref[v_ref.shape[0] - WINDOW :]
-    state_kernel((0,), place_ref, k_ref, turned_ref, v_ref, cum_ref, w_ref, pick_ref, after_ref, out_ref, norm_ref)
 
 
 def tail_of(tile):
@@ -197,17 +209,13 @@
     return jnp.sum(jnp.where(here, tail_of(tile)[5:6], 0.0), axis=1, keepdims=True)
 
 
-def first_keys(tiles, table, width):
-    lane = iota((ROWS, 128), 1).astype(F32)
+def first_keys(tiles, pick_ref, real_ref):
     lines = [tail_of(tile)[5:6] for tile in tiles]
     rows = jnp.concatenate(lines + [jnp.zeros((8 - len(lines), 128), F32)] if len(lines) < 8 else lines).astype(BF16)
-    first, second, one_a, one_b, scale = table
-    found = []
-    for token in range(2):
-        pick_a = (lane == first + token * width).astype(BF16)
-        pick_b = (lane == second + token * width).astype(BF16)
-        found.append((nt(pick_a, rows) + one_a[:, 0:8]) * (nt(pick_b, rows) + one_b[:, 0:8]) * scale[:, 0:8])
-    return found
+    found = nt(pick_ref[...], rows)
+    factors = [found[i * ROWS : (i + 1) * ROWS] for i in range(4)]
+    one_a, one_b, scale = (real_ref[i] for i in range(3))
+    return [(factors[2 * t] + one_a) * (factors[2 * t + 1] + one_b) * scale for t in range(2)]
 
 
 def carried(tile, w):
@@ -260,13 +268,13 @@
     return w_ref[:, pl.ds(pl.multiple_of(head * 128, 128), 128)]
 
 
-def group_kernel(width, place_ref, w_ref, table_ref, x0, x1, x2, x3, after_ref, total_ref, before_ref, keys_ref, small_ref, held):
+def group_kernel(width, place_ref, w_ref, pick_ref, real_ref, x0, x1, x2, x3, after_ref, total_ref, before_ref, keys_ref, small_ref, held):
     group = (place_ref[0] & 3)
     count = x0.shape[0]
     for distance, ref in enumerate((x0, x1, x2, x3)):
         held[group ^ distance] = ref[...]
     tiles = [[held[p, j].astype(F32) for j in range(count)] for p in range(4)]
-    columns = first_keys([tiles[p][j] for p in range(4) for j in range(count)], columns_of(table_ref), width)
+    columns = first_keys([tiles[p][j] for p in range(4) for j in range(count)], pick_ref, real_ref)
     sub = iota((8, 128), 0)
     for j in range(count):
         w = head_taps(w_ref, group * count + j)
@@ -286,10 +294,10 @@
         small_ref[j] = small
 
 
-def pair_kernel(width, place_ref, w_ref, table_ref, left_ref, right_ref, out_ref):
+def pair_kernel(width, place_ref, w_ref, pick_ref, real_ref, left_ref, right_ref, out_ref):
     count = left_ref.shape[0]
     rights = [right_ref[j].astype(F32) for j in range(count)]
-    columns = first_keys(rights, columns_of(table_ref), width)
+    columns = first_keys(rights, pick_ref, real_ref)
     for j in range(count):
         w = head_taps(w_ref, (place_ref[0] & 3) * count + j)
         left = left_ref[j].astype(F32)
@@ -321,13 +329,9 @@
         ref[...] = held[group ^ distance]
 
 
-def window_kernel(place_ref, wq_ref, wk_ref, v_ref, halo_ref, after_ref, win_ref):
+def windowed(wq_ref, keys, values, valid, out_ref):
+    half = WINDOW
     rows = wq_ref.shape[0]
-    half = WINDOW
-    seen = iota((half, 2 * half), 1)
-    mine = iota((half, 2 * half), 0)
-    valid = (seen > mine) & (seen <= mine + half)
-    start = valid & ((seen >= half) | (place_ref[0] > 0))
     steps = rows // half
     ones = jnp.ones((rows + half, 128), BF16)
     zeros = jnp.zeros((rows + half, 128), BF16)
@@ -337,20 +341,39 @@
         scores = []
         for h in range(four, four + 4, 2):
             one, two = slice(128 * h, 128 * h + 128), slice(128 * h + 128, 128 * h + 256)
-            upper = jnp.concatenate([jnp.concatenate([halo_ref[:half, one], wk_ref[:, one]]), zeros], axis=1)
-            lower = jnp.concatenate([zeros, jnp.concatenate([halo_ref[:half, two], wk_ref[:, two]])], axis=1)
+            upper = jnp.concatenate([keys(one), zeros], axis=1)
+            lower = jnp.concatenate([zeros, keys(two)], axis=1)
             queries = wq_ref[:, 128 * h : 128 * h + 256]
             s = [nt(queries[i * half : (i + 1) * half], jnp.concatenate([upper[span], lower[span]])) for i, span in enumerate(spans)]
             scores += [[x[:, :128] for x in s], [x[:, 128:] for x in s]]
         probs = []
         for s in scores:
-            s = jnp.concatenate([jnp.where(valid if i else start, x * (128 ** (-0.5) * LOG2E), -jnp.inf) for i, x in enumerate(s)])
+            s = jnp.concatenate([jnp.where(valid, x * (128 ** (-0.5) * LOG2E), -jnp.inf) for x in s])
             probs.append(jnp.exp2(s - jnp.max(s, axis=1, keepdims=True)).astype(BF16))
         for h, p in zip(range(four, four + 4), probs):
             at = slice(128 * h, 128 * h + 128)
-            right = jnp.concatenate([jnp.concatenate([halo_ref[half:, at], v_ref[:, at]]), ones], axis=1)
+            right = jnp.concatenate([values(at), ones], axis=1)
             both = jnp.concatenate([nn(p[i * half : (i + 1) * half], right[span]) for i, span in enumerate(spans)])
-            win_ref[:, at] = both[:, :128] / both[:, 128:]
+            out_ref[:, at] = both[:, :128] / both[:, 128:]
+
+
+def window_masks():
+    seen = iota((WINDOW, 2 * WINDOW), 1)
+    mine = iota((WINDOW, 2 * WINDOW), 0)
+    return (seen > mine) & (seen <= mine + WINDOW), seen >= WINDOW
+
+
+def window_kernel(wq_ref, wk_ref, v_ref, after_ref, win_ref):
+    valid, _ = window_masks()
+    windowed(wq_ref.at[pl.ds(WINDOW, win_ref.shape[0])], lambda at: wk_ref[:, at], lambda at: v_ref[:, at], valid, win_ref)
+
+
+def early_kernel(place_ref, wq_ref, wk_ref, v_ref, halo_ref, after_ref, win_ref):
+    valid, own = window_masks()
+    valid = valid & (own | ((place_ref[0]) > 0))
+    keys = lambda at: jnp.concatenate([halo_ref[:WINDOW, at], wk_ref[:WINDOW, at]])
+    values = lambda at: jnp.concatenate([halo_ref[WINDOW:, at], v_ref[:WINDOW, at]])
+    windowed(wq_ref.at[pl.ds(0, WINDOW)], keys, values, valid, win_ref)
 
 
 def block_kernel(q_ref, turned_ref, v_ref, w_ref, cum_ref, after_ref, num_ref, den_ref, token_ref):
@@ -396,12 +419,13 @@
         den_ref[:, at] = total[:, 128:]
 
 
-def query_kernel(q_ref, k_ref, cum_ref, pick_ref, after_ref, out_ref):
+def query_kernel(q_ref, k_ref, cum_ref, pick_ref, after_ref, out_ref, token_ref):
     rows, wide = q_ref.shape
     heads = cum_ref.shape[0]
     width = wide // heads
     q = q_ref[...]
     turned = q.astype(F32).T
+    token_ref[...] = jnp.zeros(token_ref.shape, F32)
     pick = pick_ref[...]
     keys = k_ref[0:16].astype(F32)[0:8] * width ** (-0.5)
     line = iota((2 * heads, wide), 0)
@@ -422,7 +446,7 @@
         out_ref[h, :, 0:ROWS] = nn(pick, phi).astype(BF16).T
 
 
-def finish_kernel(place_ref, phi_ref, x0, x1, x2, x3, num_ref, den_ref, win_ref, out_far, held, out_ref, sems):
+def finish_kernel(place_ref, phi_ref, x0, x1, x2, x3, num_ref, den_ref, win_ref, early_ref, out_far, held, out_ref, sems):
     group = (place_ref[0] & 3)
     heads = phi_ref.shape[0]
     count = x0.shape[0]
@@ -439,7 +463,8 @@
         at = slice(128 * h, 128 * h + 128)
         norm = jnp.broadcast_to(norms[:ROWS, h : h + 1], (ROWS, 128)).astype(BF16)
         both = nn(phi_ref[h][:, :ROWS], jnp.concatenate([tiles[h], norm], axis=1))
-        out = (num_ref[:, at] + both[:, :128]) / (den_ref[:, at] + both[:, 128:]) + win_ref[:, at]
+        out = (num_ref[:, at] + both[:, :128]) / (den_ref[:, at] + both[:, 128:])
+        out = out + jnp.concatenate([early_ref[:, at], win_ref[:, at]])
         out_ref[h] = out.astype(BF16)
         copies.append(pltpu.make_async_copy(out_ref.at[h], out_far.at[:, pl.ds(128 * h, 128)], sems.at[h]))
         copies[-1].start()
@@ -471,7 +496,7 @@
     position = lax.axis_index("seq")
     one = lambda number: jnp.reshape(number, (1,)).astype(jnp.int32)
     place = one(position)
-    table = key_table(width)
+    tables = key_tables(width)
     pick_keys, pick_queries = picks(width)
     shape = jax.ShapeDtypeStruct((quarter, ROWS, 128), BF16)
     wide = lambda *dims: jax.ShapeDtypeStruct(dims, F32)
@@ -494,32 +519,38 @@
         lambda *refs: state_kernel((1, 2, 3), *refs),
         (place, k_feat, turned, values, cum, conv_weight, pick_keys, cum),
         [shape] * 3,
-        [pltpu.VMEM((3, quarter, 8, 256), F32)],
+        [pltpu.VMEM((3, 8, 256), F32)],
         smem=(0,),
         free=(7,),
         name="states",
         us=2.0,
     )
     others = [swap(x, d) for d, x in zip((1, 2, 3), sent)]
-    own, edge = call(
-        own_kernel,
-        (place, k_feat, turned, values, cum, conv_weight, pick_keys, sent[0], win_key),
-        [shape, jax.ShapeDtypeStruct((2 * WINDOW, values.shape[1]), BF16)],
-        [pltpu.VMEM((1, quarter, 8, 256), F32)],
+    (own,) = call(
+        lambda *refs: state_kernel((0,), *refs),
+        (place, k_feat, turned, values, cum, conv_weight, pick_keys, sent[0]),
+        [shape],
+        [pltpu.VMEM((1, 8, 256), F32)],
         smem=(0,),
         free=(7,),
         name="own_states",
         us=0.8,
     )
-    halo = lax.ppermute(edge, "seq", [(i, i + 1) for i in range(count - 1)])
-
+    num, den, token = call(
+        block_kernel,
+        (q_feat, turned, values, conv_weight, cum, own),
+        [wide(*values.shape)] * 2 + [wide(8, 128)],
+        free=(5,),
+        name="block",
+        us=2.7,
+    )
     total, before, keys, small = call(
         lambda *refs: group_kernel(width, *refs),
-        (place, conv_weight, table, own, *others, edge),
+        (place, conv_weight, *tables, own, *others, token),
         [shape, wide(3, quarter, ROWS, 128), wide(2, quarter, ROWS, 128), wide(quarter, 8, 128)],
         [held],
         smem=(0,),
-        free=(7,),
+        free=(8,),
         name="merge_group",
         us=2.0,
     )
@@ -534,7 +565,7 @@
         def pair(left, right):
             return call(
                 lambda *refs: pair_kernel(width, *refs),
-                (place, conv_weight, table, left, right),
+                (place, conv_weight, *tables, left, right),
                 shape,
                 smem=(0,),
                 name="merge_pair",
@@ -548,13 +579,23 @@
         if 2 * distance < count:
             total = pair(jnp.where(upper, got, total), jnp.where(upper, total, got))
         distance *= 2
-    num, den, token = call(
-        block_kernel,
-        (q_feat, turned, values, conv_weight, cum, last),
-        [wide(*values.shape)] * 2 + [wide(8, 128)],
-        free=(5,),
-        name="block",
-        us=2.7,
+    edge = call(
+        edge_kernel,
+        (win_key, values, last),
+        jax.ShapeDtypeStruct((2 * WINDOW, values.shape[1]), BF16),
+        free=(2,),
+        name="edge",
+        us=0.2,
+    )
+    halo = lax.ppermute(edge, "seq", [(i, i + 1) for i in range(count - 1)])
+
+    phi, token = call(
+        query_kernel,
+        (q_feat, k_feat, cum, pick_queries, edge),
+        [jax.ShapeDtypeStruct((heads, rows, 256), BF16), wide(8, 128)],
+        free=(4,),
+        name="query_features",
+        us=1.5,
     )
     here, *sent = call(
         spread_kernel,
@@ -567,26 +608,26 @@
         us=1.0,
     )
     prefixes = [here] + [swap(x, d) for d, x in zip((1, 2, 3), sent)]
-    phi = call(
-        query_kernel,
-        (q_feat, k_feat, cum, pick_queries, here),
-        jax.ShapeDtypeStruct((heads, rows, 256), BF16),
-        free=(4,),
-        name="query_features",
-        us=1.5,
-    )
     win = call(
         window_kernel,
-        (place, win_query, win_key, values, halo, phi),
-        wide(*values.shape),
+        (win_query, win_key, values, here),
+        wide(rows - WINDOW, values.shape[1]),
+        free=(3,),
+        name="window",
+        us=2.0,
+    )
+    early = call(
+        early_kernel,
+        (place, win_query, win_key, values, halo, win),
+        wide(WINDOW, values.shape[1]),
         smem=(0,),
         free=(5,),
-        name="window",
-        us=2.6,
+        name="window_first",
+        us=0.4,
     )
     return call(
         finish_kernel,
-        (place, phi, *prefixes, num, den, win),
+        (place, phi, *prefixes, num, den, win, early),
         jax.ShapeDtypeStruct(values.shape, BF16),
         [held, pltpu.VMEM((heads, rows, 128), BF16), pltpu.SemaphoreType.DMA((heads,))],
         smem=(0,),

time: 31.2 us -> 29.7 us (0.952)
  starting transfers between devices: 14.6 us -> 13.5 us
  waiting for transfers between devices: 3.54 us -> 2.81 us
    ppermute x1, starting transfers between devices: 3.81 us -> 2.55 us  [local(): halo = lax.ppermute(edge, 'seq', [(i, i + 1) for i in range(count - 1)])]
    ppermute x7, waiting for transfers between devices: 3.54 us -> 2.81 us  [swap(): return lax.ppermute(x, 'seq', [(i, i ^ distance) for i in range(count)])]
    pallas_call x10 -> x12, Pallas kernels: 11.6 us -> 11.8 us  [call(): pl.pallas_call(kernel, out_shape=outs, in_specs=[pl.BlockSpec(memory_spac...]
    unnamed x20 -> x22, local copies, waits for them, and re-layouts: 1.06 us -> 1.09 us
  transfers between devices with their start and end apart: 8 -> 8, of which waited for: 3 -> 4; matrix products, arithmetic and copies ran while one was open for 0% -> 0% of each run, Pallas kernels for 25% -> 25%
where the time goes in v5:
time: 29.7 us; the launch traced here: 29.3 us
  starting transfers between devices  13.5 us (45%)
  Pallas kernels  11.8 us (40%)
  waiting for transfers between devices  2.81 us (9%)
  local copies, waits for them, and re-layouts  1.09 us (4%)
    pallas_call x12, Pallas kernels, call(): pl.pallas_call(kernel, out_shape=outs, in_specs=[pl.BlockSpec(memory_spac...  11.8 us
    ppermute x7, starting transfers between devices, swap(): return lax.ppermute(x, 'seq', [(i, i ^ distance) for i in range(count)])  10.9 us
    ppermute x7, waiting for transfers between devices, swap(): return lax.ppermute(x, 'seq', [(i, i ^ distance) for i in range(count)])  2.81 us
    ppermute x1, starting transfers between devices, local(): halo = lax.ppermute(edge, 'seq', [(i, i + 1) for i in range(count - 1)])  2.55 us
    unnamed x22, local copies, waits for them, and re-layouts  1.09 us
  transfers between devices with their start and end apart: 8, of which 4 were waited for; matrix products, arithmetic and copies ran while one was open for 0% of the time, Pallas kernels for 25%

profile of v5, /device:TPU:0, one launch (start us, length us, event | category | flops | bytes accessed | tf_op | source)
XLA Modules:
  0.0 29.3 jit_solution(7853545210690000931)
XLA Ops:
  0.0 0.9 %copy-done.3 = bf16[512,128]{1,0:T(8,128)(2,1)S(1)} copy-done((bf16[512,128]{1,0:T(8,128)(2,1)S(1)}, bf16[512,128]{1,0:T(8,128)(2,1)}, u32[]{:S(2)}) %copy-start.3) | copy-done | bytes 131096
  0.9 0.0 copy-done.4
  0.9 0.4 %gates.1 = (f32[8,512]{1,0:T(8,128)S(1)}, f32[128,512]{1,0:T(8,128)S(1)}) custom-call(f32[8,512]{1,0:T(8,128)S(1)} %bitcast.2, bf16[512,128]{1,0:T(8,128)(2,1)S(1)} %copy-done.3, f32[8,128]{1,0:T(8,128)S(1)} %open.1.after_ref), custom_call_target="tpu_custom_call" | custom-call | flops 30000000 | bytes 90000 | tf_op jit(solution)/shard_map/gates/pallas_call | solution.py:479
  1.3 0.0 copy-done.1
  1.3 1.6 %states.1 = (bf16[2,160,128]{2,1,0:T(8,128)(2,1)S(1)}, bf16[2,160,128]{2,1,0:T(8,128)(2,1)S(1)}, bf16[2,160,128]{2,1,0:T(8,128)(2,1)S(1)}) custom-call(s32[1]{0:T(128)} %bitcast.place_ref.refs_0_, bf16[512,128]{1,0:T(8,128)(2,1)S(1)} %copy-done.3, f32[128,512]{1,0:T(8,128)S(1)} %get-tuple-element.24.refs_2_.turned_ref, bf16[512,1024]{1,0:T(8,128)(2,1)S(1)} %copy-done.1, ...), custom_call_target="tpu_custom_call" | custom-call | flops 6000000000 | bytes 18000000 | tf_op jit(solution)/shard_map/states/pallas_call | solution.py:479
  2.9 3.0 %collective-permute-start.1 = (bf16[2,160,128]{2,1,0:T(8,128)(2,1)S(1)}, bf16[2,160,128]{2,1,0:T(8,128)(2,1)S(1)}, u32[]{:S(2)}, u32[]{:S(2)}) collective-permute-start(bf16[2,160,128]{2,1,0:T(8,128)(2,1)S(1)} %get-tuple-element.26), channel_id=1, source_target_pairs={{0,4},{2,6},{4,0},{6,2},{8,12},{10,14},{12,8},{14,10},{1,5},{3,7},... | collective-permute-start | bytes 245768 | tf_op jit(solution)/shard_map/ppermute | solution.py:506
  5.9 1.4 %collective-permute-start.2 = (bf16[2,160,128]{2,1,0:T(8,128)(2,1)S(1)}, bf16[2,160,128]{2,1,0:T(8,128)(2,1)S(1)}, u32[]{:S(2)}, u32[]{:S(2)}) collective-permute-start(bf16[2,160,128]{2,1,0:T(8,128)(2,1)S(1)} %get-tuple-element.27), channel_id=1, source_target_pairs={{0,6},{2,4},{4,2},{6,0},{8,14},{10,12},{12,10},{14,8},{1,7},{3,5},... | collective-permute-start | bytes 245768 | tf_op jit(solution)/shard_map/ppermute | solution.py:506
  7.3 0.1 collective-permute-start
  7.5 0.6 %own_states.1.after_ref.refs_4_ = bf16[2,160,128]{2,1,0:T(8,128)(2,1)S(1)} custom-call(s32[1]{0:T(128)} %bitcast.place_ref.refs_0_, bf16[512,128]{1,0:T(8,128)(2,1)S(1)} %copy-done.3, f32[128,512]{1,0:T(8,128)S(1)} %get-tuple-element.24.refs_2_.turned_ref, bf16[512,1024]{1,0:T(8,128)(2,1)S(1)} %copy-done.1, ...), custom_call_target="tpu_custom_call" | custom-call | flops 2400000000 | bytes 7200000 | tf_op jit(solution)/shard_map/own_states/pallas_call | solution.py:479
  8.1 0.2 copy-done.5
  8.2 2.7 %block.1 = (f32[512,1024]{1,0:T(8,128)S(1)}, f32[512,1024]{1,0:T(8,128)S(1)}, f32[8,128]{1,0:T(8,128)S(1)}) custom-call(bf16[512,128]{1,0:T(8,128)(2,1)S(1)} %copy-done.5, f32[128,512]{1,0:T(8,128)S(1)} %get-tuple-element.24.refs_2_.turned_ref, bf16[512,1024]{1,0:T(8,128)(2,1)S(1)} %copy-done.1, f32[3,1024]{1,0:T(4,128)S(1)} %copy-done.6, ...), custom_call_target="tpu_custom_call" | custom-call | flops 8099999744 | bytes 24300000 | tf_op jit(solution)/shard_map/block/pallas_call | solution.py:479
  10.9 0.0 collective-permute-done.1.refs_6_
  10.9 0.7 %collective-permute-done.2.refs_7_ = bf16[2,160,128]{2,1,0:T(8,128)(2,1)S(1)} collective-permute-done((bf16[2,160,128]{2,1,0:T(8,128)(2,1)S(1)}, bf16[2,160,128]{2,1,0:T(8,128)(2,1)S(1)}, u32[]{:S(2)}, u32[]{:S(2)}) %collective-permute-start.2) | collective-permute-done | bytes 81952 | tf_op jit(solution)/shard_map/ppermute | solution.py:506
  11.6 1.0 %collective-permute-done.refs_5_ = bf16[2,160,128]{2,1,0:T(8,128)(2,1)S(1)} collective-permute-done((bf16[2,160,128]{2,1,0:T(8,128)(2,1)S(1)}, bf16[2,160,128]{2,1,0:T(8,128)(2,1)S(1)}, u32[]{:S(2)}, u32[]{:S(2)}) %collective-permute-start) | collective-permute-done | bytes 81952 | tf_op jit(solution)/shard_map/ppermute | solution.py:506
  12.6 0.0 copy-done.8
  12.6 0.9 %merge_group.1 = (bf16[2,160,128]{2,1,0:T(8,128)(2,1)S(1)}, f32[3,2,160,128]{3,2,1,0:T(8,128)S(1)}, f32[2,2,160,128]{3,2,1,0:T(8,128)S(1)}, f32[2,8,128]{2,1,0:T(8,128)S(1)}) custom-call(s32[1]{0:T(128)} %bitcast.place_ref.refs_0_, f32[3,1024]{1,0:T(4,128)S(1)} %copy-done.6, bf16[640,128]{1,0:T(8,128)(2,1)S(1)} %copy-done.8, f32[3,160,8]{2,1,0:T(8,128)S(1)} %copy-done.7, ...), custom_call_target="tpu_custom_call" | custom-call | flops 6000000000 | bytes 18000000 | tf_op jit(solution)/shard_map/merge_group/pallas_call | solution.py:479
  13.5 0.0 copy-start.9
  13.5 2.7 %collective-permute-start.3 = (bf16[2,160,128]{2,1,0:T(8,128)(2,1)S(1)}, bf16[2,160,128]{2,1,0:T(8,128)(2,1)S(1)}, u32[]{:S(2)}, u32[]{:S(2)}) collective-permute-start(bf16[2,160,128]{2,1,0:T(8,128)(2,1)S(1)} %get-tuple-element.29.after_ref), channel_id=1, source_target_pairs={{0,8},{2,10},{4,12},{6,14},{8,0},{10,2},{12,4},{14,6},{1,9},{3,11}... | collective-permute-start | bytes 245768 | tf_op jit(solution)/shard_map/ppermute | solution.py:506
  16.2 2.5 %collective-permute-start.7 = (bf16[128,1024]{1,0:T(8,128)(2,1)S(1)}, bf16[128,1024]{1,0:T(8,128)(2,1)S(1)}, u32[]{:S(2)}, u32[]{:S(2)}) collective-permute-start(bf16[128,1024]{1,0:T(8,128)(2,1)S(1)} %edge.1.after_ref), channel_id=1, source_target_pairs={{0,2},{2,4},{4,6},{6,8},{8,10},{10,12},{12,14},{1,3},{3,5},{5,7},{... | collective-permute-start | bytes 786440 | tf_op jit(solution)/shard_map/ppermute | solution.py:590
  18.8 1.1 %query_features.1 = (bf16[8,512,256]{2,1,0:T(8,128)(2,1)S(1)}, f32[8,128]{1,0:T(8,128)S(1)}) custom-call(bf16[512,128]{1,0:T(8,128)(2,1)S(1)} %copy-done.5, bf16[512,128]{1,0:T(8,128)(2,1)S(1)} %copy-done.3, f32[8,512]{1,0:T(8,128)S(1)} %get-tuple-element.23.refs_4_.refs_7_.cum_ref, bf16[160,224]{1,0:T(8,128)(2,1)S(1)} %copy-done.9, ...), custom_call_target="tpu_custom_call" | custom-call | flops 4499999744 | bytes 13500000 | tf_op jit(solution)/shard_map/query_features/pallas_call | solution.py:479
  19.9 0.0 collective-permute-done.3.base_ref
  19.9 0.1 spread.1
  20.0 2.2 %collective-permute-start.4 = (bf16[2,160,128]{2,1,0:T(8,128)(2,1)S(1)}, bf16[2,160,128]{2,1,0:T(8,128)(2,1)S(1)}, u32[]{:S(2)}, u32[]{:S(2)}) collective-permute-start(bf16[2,160,128]{2,1,0:T(8,128)(2,1)S(1)} %get-tuple-element.36), channel_id=1, source_target_pairs={{0,2},{2,0},{4,6},{6,4},{8,10},{10,8},{12,14},{14,12},{1,3},{3,1},... | collective-permute-start | bytes 245768 | tf_op jit(solution)/shard_map/ppermute | solution.py:506
  22.2 0.0 collective-permute-start.5
  22.2 1.5 %collective-permute-start.6 = (bf16[2,160,128]{2,1,0:T(8,128)(2,1)S(1)}, bf16[2,160,128]{2,1,0:T(8,128)(2,1)S(1)}, u32[]{:S(2)}, u32[]{:S(2)}) collective-permute-start(bf16[2,160,128]{2,1,0:T(8,128)(2,1)S(1)} %get-tuple-element.38), channel_id=1, source_target_pairs={{0,6},{2,4},{4,2},{6,0},{8,14},{10,12},{12,10},{14,8},{1,7},{3,5},... | collective-permute-start | bytes 245768 | tf_op jit(solution)/shard_map/ppermute | solution.py:506
  23.7 1.9 %window.1.after_ref.win_ref = f32[448,1024]{1,0:T(8,128)S(1)} custom-call(bf16[512,1024]{1,0:T(8,128)(2,1)S(1)} %copy-done.2, bf16[512,1024]{1,0:T(8,128)(2,1)S(1)} %copy-done, bf16[512,1024]{1,0:T(8,128)(2,1)S(1)} %copy-done.1, bf16[2,160,128]{2,1,0:T(8,128)(2,1)S(1)} %get-tuple-element.35.after_ref.x0), custom_call_target="tpu_custom_call" | custom-call | flops 6000000000 | bytes 18000000 | tf_op jit(solution)/shard_map/window/pallas_call | solution.py:479
  25.6 0.0 collective-permute-done.7.halo_ref
  25.7 0.7 %window_first.1.early_ref = f32[64,1024]{1,0:T(8,128)S(1)} custom-call(s32[1]{0:T(128)} %bitcast.place_ref.refs_0_, bf16[512,1024]{1,0:T(8,128)(2,1)S(1)} %copy-done.2, bf16[512,1024]{1,0:T(8,128)(2,1)S(1)} %copy-done, bf16[512,1024]{1,0:T(8,128)(2,1)S(1)} %copy-done.1, bf16[128,1024]{1,0:T(8,128)(2,1)S(1)} %collective-permute-done.7.halo_ref, ...), custom_call_target="tpu_custom_call" | custom-call | flops 1200000000 | bytes 3600000 | tf_op jit(solution)/shard_map/window_first/pallas_call | solution.py:479
  26.4 0.0 collective-permute-done.4.x1
  26.4 0.2 collective-permute-done.5.x2
  26.6 0.9 %collective-permute-done.6.x3 = bf16[2,160,128]{2,1,0:T(8,128)(2,1)S(1)} collective-permute-done((bf16[2,160,128]{2,1,0:T(8,128)(2,1)S(1)}, bf16[2,160,128]{2,1,0:T(8,128)(2,1)S(1)}, u32[]{:S(2)}, u32[]{:S(2)}) %collective-permute-start.6) | collective-permute-done | bytes 81952 | tf_op jit(solution)/shard_map/ppermute | solution.py:506
  27.5 1.7 %finish.1 = bf16[512,1024]{1,0:T(8,128)(2,1)} custom-call(s32[1]{0:T(128)} %bitcast.place_ref.refs_0_, bf16[8,512,256]{2,1,0:T(8,128)(2,1)S(1)} %get-tuple-element.30.phi_ref, bf16[2,160,128]{2,1,0:T(8,128)(2,1)S(1)} %get-tuple-element.35.after_ref.x0, bf16[2,160,128]{2,1,0:T(8,128)(2,1)S(1)} %collective-permute-done.4.x1, ...), custom_call_target="tpu_custom_call" | custom-call | flops 6300000256 | bytes 18900000 | tf_op jit(solution)/shard_map/finish/pallas_call | solution.py:479
  (18 shorter events, 0.0 us)
Async XLA Ops:
  0.0 0.9 %copy-start.3 = (bf16[512,128]{1,0:T(8,128)(2,1)S(1)}, bf16[512,128]{1,0:T(8,128)(2,1)}, u32[]{:S(2)}) copy-start(bf16[512,128]{1,0:T(8,128)(2,1)} %k_ref.3) | copy-start | bytes 393220
  0.0 0.9 %copy-start.4 = (f32[512,8]{0,1:T(8,128)S(1)}, f32[512,8]{0,1:T(8,128)}, u32[]{:S(2)}) copy-start(f32[512,8]{0,1:T(8,128)} %param.16) | copy-start | bytes 49156
  0.0 1.3 %copy-start.1 = (bf16[512,1024]{1,0:T(8,128)(2,1)S(1)}, bf16[512,1024]{1,0:T(8,128)(2,1)}, u32[]{:S(2)}) copy-start(bf16[512,1024]{1,0:T(8,128)(2,1)} %v_ref.7) | copy-start | bytes 3145732
  0.0 1.3 %copy-start.6 = (f32[3,1024]{1,0:T(4,128)S(1)}, f32[3,1024]{1,0:T(4,128)}, u32[]{:S(2)}) copy-start(f32[3,1024]{1,0:T(4,128)} %w_ref.3) | copy-start | bytes 36868
  0.0 1.3 %copy-start.10 = (bf16[160,224]{1,0:T(8,128)(2,1)S(1)}, bf16[160,224]{1,0:T(8,128)(2,1)}, u32[]{:S(2)}) copy-start(bf16[160,224]{1,0:T(8,128)(2,1)} %constant.16.clone.refs_6_) | copy-start | bytes 215044
  2.9 8.0 %collective-permute-start.1 = (bf16[2,160,128]{2,1,0:T(8,128)(2,1)S(1)}, bf16[2,160,128]{2,1,0:T(8,128)(2,1)S(1)}, u32[]{:S(2)}, u32[]{:S(2)}) collective-permute-start(bf16[2,160,128]{2,1,0:T(8,128)(2,1)S(1)} %get-tuple-element.26), channel_id=1, source_target_pairs={{0,4},{2,6},{4,0},{6,2},{8,12},{10,14},{12,8},{14,10},{1,5},{3,7},... | collective-permute-start | bytes 245768 | tf_op jit(solution)/shard_map/ppermute | solution.py:506
  5.9 5.7 %collective-permute-start.2 = (bf16[2,160,128]{2,1,0:T(8,128)(2,1)S(1)}, bf16[2,160,128]{2,1,0:T(8,128)(2,1)S(1)}, u32[]{:S(2)}, u32[]{:S(2)}) collective-permute-start(bf16[2,160,128]{2,1,0:T(8,128)(2,1)S(1)} %get-tuple-element.27), channel_id=1, source_target_pairs={{0,6},{2,4},{4,2},{6,0},{8,14},{10,12},{12,10},{14,8},{1,7},{3,5},... | collective-permute-start | bytes 245768 | tf_op jit(solution)/shard_map/ppermute | solution.py:506
  7.3 0.9 %copy-start.5 = (bf16[512,128]{1,0:T(8,128)(2,1)S(1)}, bf16[512,128]{1,0:T(8,128)(2,1)}, u32[]{:S(2)}) copy-start(bf16[512,128]{1,0:T(8,128)(2,1)} %q_ref.3) | copy-start | bytes 393220
  7.3 5.3 %collective-permute-start = (bf16[2,160,128]{2,1,0:T(8,128)(2,1)S(1)}, bf16[2,160,128]{2,1,0:T(8,128)(2,1)S(1)}, u32[]{:S(2)}, u32[]{:S(2)}) collective-permute-start(bf16[2,160,128]{2,1,0:T(8,128)(2,1)S(1)} %get-tuple-element.25.refs_7_), channel_id=1, source_target_pairs={{0,2},{2,0},{4,6},{6,4},{8,10},{10,8},{12,14},{14,12},{1,3},{3,1},... | collective-permute-start | bytes 245768 | tf_op jit(solution)/shard_map/ppermute | solution.py:506
  8.2 4.4 %copy-start.7 = (f32[3,160,8]{2,1,0:T(8,128)S(1)}, f32[3,160,8]{2,1,0:T(8,128)}, u32[]{:S(2)}) copy-start(f32[3,160,8]{2,1,0:T(8,128)} %constant.15.clone.refs_3_) | copy-start | bytes 46084
  8.2 4.4 %copy-start.8 = (bf16[640,128]{1,0:T(8,128)(2,1)S(1)}, bf16[640,128]{1,0:T(8,128)(2,1)}, u32[]{:S(2)}) copy-start(bf16[640,128]{1,0:T(8,128)(2,1)} %constant.14.clone.refs_2_) | copy-start | bytes 491524
  12.6 3.6 %copy-start = (bf16[512,1024]{1,0:T(8,128)(2,1)S(1)}, bf16[512,1024]{1,0:T(8,128)(2,1)}, u32[]{:S(2)}) copy-start(bf16[512,1024]{1,0:T(8,128)(2,1)} %wk_ref.3) | copy-start | bytes 3145732
  13.5 5.2 %copy-start.9 = (bf16[160,224]{1,0:T(8,128)(2,1)S(1)}, bf16[160,224]{1,0:T(8,128)(2,1)}, u32[]{:S(2)}) copy-start(bf16[160,224]{1,0:T(8,128)(2,1)} %constant.17.clone.pick_ref) | copy-start | bytes 215044
  13.5 6.4 %collective-permute-start.3 = (bf16[2,160,128]{2,1,0:T(8,128)(2,1)S(1)}, bf16[2,160,128]{2,1,0:T(8,128)(2,1)S(1)}, u32[]{:S(2)}, u32[]{:S(2)}) collective-permute-start(bf16[2,160,128]{2,1,0:T(8,128)(2,1)S(1)} %get-tuple-element.29.after_ref), channel_id=1, source_target_pairs={{0,8},{2,10},{4,12},{6,14},{8,0},{10,2},{12,4},{14,6},{1,9},{3,11}... | collective-permute-start | bytes 245768 | tf_op jit(solution)/shard_map/ppermute | solution.py:506
  16.2 9.5 %collective-permute-start.7 = (bf16[128,1024]{1,0:T(8,128)(2,1)S(1)}, bf16[128,1024]{1,0:T(8,128)(2,1)S(1)}, u32[]{:S(2)}, u32[]{:S(2)}) collective-permute-start(bf16[128,1024]{1,0:T(8,128)(2,1)S(1)} %edge.1.after_ref), channel_id=1, source_target_pairs={{0,2},{2,4},{4,6},{6,8},{8,10},{10,12},{12,14},{1,3},{3,5},{5,7},{... | collective-permute-start | bytes 786440 | tf_op jit(solution)/shard_map/ppermute | solution.py:590
  19.9 3.9 %copy-start.2 = (bf16[512,1024]{1,0:T(8,128)(2,1)S(1)}, bf16[512,1024]{1,0:T(8,128)(2,1)}, u32[]{:S(2)}) copy-start(bf16[512,1024]{1,0:T(8,128)(2,1)} %wq_ref.3) | copy-start | bytes 3145732
  20.0 6.4 %collective-permute-start.4 = (bf16[2,160,128]{2,1,0:T(8,128)(2,1)S(1)}, bf16[2,160,128]{2,1,0:T(8,128)(2,1)S(1)}, u32[]{:S(2)}, u32[]{:S(2)}) collective-permute-start(bf16[2,160,128]{2,1,0:T(8,128)(2,1)S(1)} %get-tuple-element.36), channel_id=1, source_target_pairs={{0,2},{2,0},{4,6},{6,4},{8,10},{10,8},{12,14},{14,12},{1,3},{3,1},... | collective-permute-start | bytes 245768 | tf_op jit(solution)/shard_map/ppermute | solution.py:506
  22.2 4.4 %collective-permute-start.5 = (bf16[2,160,128]{2,1,0:T(8,128)(2,1)S(1)}, bf16[2,160,128]{2,1,0:T(8,128)(2,1)S(1)}, u32[]{:S(2)}, u32[]{:S(2)}) collective-permute-start(bf16[2,160,128]{2,1,0:T(8,128)(2,1)S(1)} %get-tuple-element.37), channel_id=1, source_target_pairs={{0,4},{2,6},{4,0},{6,2},{8,12},{10,14},{12,8},{14,10},{1,5},{3,7},... | collective-permute-start | bytes 245768 | tf_op jit(solution)/shard_map/ppermute | solution.py:506
  22.2 5.3 %collective-permute-start.6 = (bf16[2,160,128]{2,1,0:T(8,128)(2,1)S(1)}, bf16[2,160,128]{2,1,0:T(8,128)(2,1)S(1)}, u32[]{:S(2)}, u32[]{:S(2)}) collective-permute-start(bf16[2,160,128]{2,1,0:T(8,128)(2,1)S(1)} %get-tuple-element.38), channel_id=1, source_target_pairs={{0,6},{2,4},{4,2},{6,0},{8,14},{10,12},{12,10},{14,8},{1,7},{3,5},... | collective-permute-start | bytes 245768 | tf_op jit(solution)/shard_map/ppermute | solution.py:506

commit v6 on v5

--- a/solution.py
+++ b/solution.py
@@ -67,6 +67,7 @@
     queries = keys * twice[:, None]
     queries[EDGE, constant + 1] = 1.0
     queries[EDGE + 1, constant + 2] = 1.0
+    keys = np.concatenate([keys, np.zeros((256 - ROWS, keys.shape[1]), np.float32)])
     return jnp.asarray(keys, BF16), jnp.asarray(queries, BF16)
 
 
@@ -121,7 +122,7 @@
     return jnp.where(iota(x.shape, 0) < by, 0.0, pltpu.roll(x, by, 0))
 
 
-def quarter_states(quarter, out_ref, k_ref, turned_ref, v_ref, w_ref, cum_ref, norm_ref, pick):
+def quarter_states(quarter, out_ref, k_ref, turned_ref, v_ref, w_ref, cum_ref, pick):
     rows, wide = k_ref.shape
     heads = cum_ref.shape[0]
     width = wide // heads
@@ -147,16 +148,16 @@
         values.append(v)
         keeps.append(keep)
         lasts.append(last)
-    states = nn(pick, jnp.concatenate(wides, axis=1))
+    states = nn(pick[:ROWS], jnp.concatenate(wides, axis=1))
     line = iota(norms[0].shape, 0)
     mixed = jnp.zeros(norms[0].shape, F32)
     for j, norm in enumerate(norms):
         high = norm.astype(BF16).astype(F32)
         mixed = jnp.where(line == 2 * j, high, jnp.where(line == 2 * j + 1, norm - high, mixed))
-    norm_ref[:, 0:ROWS] = nt(mixed.astype(BF16), pick)
+    norm = nt(mixed.astype(BF16), pick)
     for j in range(count):
         head = quarter * count + j
-        high, low = norm_ref[2 * j : 2 * j + 1, :], norm_ref[2 * j + 1 : 2 * j + 2, :]
+        high, low = norm[2 * j : 2 * j + 1], norm[2 * j + 1 : 2 * j + 2]
         turned = pltpu.roll(keys8, (wide - head * width) % wide, 1)
         turned2 = pltpu.roll(keys8, (wide - head * width + width) % wide, 1)
         misc = jnp.where(lane1 < width, turned[0:1], 0.0)
@@ -184,13 +185,11 @@
     turned_ref[...] = k_ref[...].astype(F32).T
 
 
-def state_kernel(order, place_ref, k_ref, turned_ref, v_ref, cum_ref, w_ref, pick_ref, after_ref, *refs):
-    outs, norm_ref = refs[:-1], refs[-1]
-    norm_ref[...] = jnp.zeros(norm_ref.shape, F32)
+def state_kernel(order, place_ref, k_ref, turned_ref, v_ref, cum_ref, w_ref, pick_ref, after_ref, *outs):
     pick = pick_ref[...]
-    for i, (out_ref, distance) in enumerate(zip(outs, order)):
+    for out_ref, distance in zip(outs, order):
         quarter = (place_ref[0] & 3) ^ distance
-        quarter_states(quarter, out_ref, k_ref, turned_ref, v_ref, w_ref, cum_ref, norm_ref.at[i], pick)
+        quarter_states(quarter, out_ref, k_ref, turned_ref, v_ref, w_ref, cum_ref, pick)
 
 
 def edge_kernel(win_key_ref, v_ref, after_ref, edge_ref):
@@ -515,22 +514,28 @@
         us=0.01,
     )
 
-    sent = call(
-        lambda *refs: state_kernel((1, 2, 3), *refs),
-        (place, k_feat, turned, values, cum, conv_weight, pick_keys, cum),
-        [shape] * 3,
-        [pltpu.VMEM((3, 8, 256), F32)],
-        smem=(0,),
-        free=(7,),
-        name="states",
-        us=2.0,
-    )
+    def states(order, after, name, us):
+        return call(
+            lambda *refs: state_kernel(order, *refs),
+            (place, k_feat, turned, values, cum, conv_weight, pick_keys, after),
+            [shape] * len(order),
+            smem=(0,),
+            free=(7,),
+            name=name,
+            us=us,
+        )
+
+    made = {}
+    after = cum
+    for number, order in enumerate(((3,), (1, 2))):
+        made.update(zip(order, states(order, after, f"states{number}", 0.3 + 0.5 * len(order))))
+        after = made[order[0]]
+    sent = [made[d] for d in (1, 2, 3)]
     others = [swap(x, d) for d, x in zip((1, 2, 3), sent)]
     (own,) = call(
         lambda *refs: state_kernel((0,), *refs),
-        (place, k_feat, turned, values, cum, conv_weight, pick_keys, sent[0]),
+        (place, k_feat, turned, values, cum, conv_weight, pick_keys, after),
         [shape],
-        [pltpu.VMEM((1, 8, 256), F32)],
         smem=(0,),
         free=(7,),
         name="own_states",

time: 29.7 us -> 29.2 us (0.983)
  waiting for transfers between devices: 2.81 us -> 2.04 us
  starting transfers between devices: 13.5 us -> 13.9 us
    ppermute x7, waiting for transfers between devices: 2.81 us -> 2.03 us  [swap(): return lax.ppermute(x, 'seq', [(i, i ^ distance) for i in range(count)])]
    ppermute x1, starting transfers between devices: 2.55 us -> 2.93 us  [local(): halo = lax.ppermute(edge, 'seq', [(i, i + 1) for i in range(count - 1)])]
    pallas_call x12 -> x13, Pallas kernels: 11.8 us -> 11.9 us  [call(): pl.pallas_call(kernel, out_shape=outs, in_specs=[pl.BlockSpec(memory_spac...]
  transfers between devices with their start and end apart: 8 -> 8, of which waited for: 4 -> 4; matrix products, arithmetic and copies ran while one was open for 0% -> 0% of each run, Pallas kernels for 25% -> 28%
where the time goes in v6:
time: 29.2 us; the launch traced here: 29.1 us
  starting transfers between devices  13.9 us (48%)
  Pallas kernels  11.9 us (41%)
  waiting for transfers between devices  2.04 us (7%)
  local copies, waits for them, and re-layouts  1.05 us (4%)
    pallas_call x13, Pallas kernels, call(): pl.pallas_call(kernel, out_shape=outs, in_specs=[pl.BlockSpec(memory_spac...  11.9 us
    ppermute x7, starting transfers between devices, swap(): return lax.ppermute(x, 'seq', [(i, i ^ distance) for i in range(count)])  10.9 us
    ppermute x1, starting transfers between devices, local(): halo = lax.ppermute(edge, 'seq', [(i, i + 1) for i in range(count - 1)])  2.93 us
    ppermute x7, waiting for transfers between devices, swap(): return lax.ppermute(x, 'seq', [(i, i ^ distance) for i in range(count)])  2.03 us
    unnamed x22, local copies, waits for them, and re-layouts  1.05 us
  transfers between devices with their start and end apart: 8, of which 4 were waited for; matrix products, arithmetic and copies ran while one was open for 0% of the time, Pallas kernels for 28%

profile of v6, /device:TPU:0, one launch (start us, length us, event | category | flops | bytes accessed | tf_op | source)
XLA Modules:
  0.0 29.1 jit_solution(13408167133268537590)
XLA Ops:
  0.0 0.9 %copy-done.3 = bf16[512,128]{1,0:T(8,128)(2,1)S(1)} copy-done((bf16[512,128]{1,0:T(8,128)(2,1)S(1)}, bf16[512,128]{1,0:T(8,128)(2,1)}, u32[]{:S(2)}) %copy-start.3) | copy-done | bytes 131096
  0.9 0.4 %gates.1 = (f32[8,512]{1,0:T(8,128)S(1)}, f32[128,512]{1,0:T(8,128)S(1)}) custom-call(f32[8,512]{1,0:T(8,128)S(1)} %bitcast.2, bf16[512,128]{1,0:T(8,128)(2,1)S(1)} %copy-done.3, f32[8,128]{1,0:T(8,128)S(1)} %open.1.after_ref), custom_call_target="tpu_custom_call" | custom-call | flops 30000000 | bytes 90000 | tf_op jit(solution)/shard_map/gates/pallas_call | solution.py:478
  1.3 0.0 copy-done.1
  1.3 0.6 %states0.1.refs_7_ = bf16[2,160,128]{2,1,0:T(8,128)(2,1)S(1)} custom-call(s32[1]{0:T(128)} %bitcast.place_ref.refs_0_, bf16[512,128]{1,0:T(8,128)(2,1)S(1)} %copy-done.3, f32[128,512]{1,0:T(8,128)S(1)} %get-tuple-element.23.refs_2_.turned_ref, bf16[512,1024]{1,0:T(8,128)(2,1)S(1)} %copy-done.1, f32[8,512]{1,0:T(8,128)S(1)} %get-tuple-element.22.refs_4_.refs_7_.cum_ref, ...), custom_call_target="tpu_custom_call" | custom-call | flops 2400000000 | bytes 7200000 | tf_op jit(solution)/shard_map/states0/pallas_call | solution.py:478
  2.0 4.0 %collective-permute-start.2 = (bf16[2,160,128]{2,1,0:T(8,128)(2,1)S(1)}, bf16[2,160,128]{2,1,0:T(8,128)(2,1)S(1)}, u32[]{:S(2)}, u32[]{:S(2)}) collective-permute-start(bf16[2,160,128]{2,1,0:T(8,128)(2,1)S(1)} %states0.1.refs_7_), channel_id=1, source_target_pairs={{0,6},{2,4},{4,2},{6,0},{8,14},{10,12},{12,10},{14,8},{1,7},{3,5},... | collective-permute-start | bytes 245768 | tf_op jit(solution)/shard_map/ppermute | solution.py:505
  6.0 1.1 %states1.1 = (bf16[2,160,128]{2,1,0:T(8,128)(2,1)S(1)}, bf16[2,160,128]{2,1,0:T(8,128)(2,1)S(1)}) custom-call(s32[1]{0:T(128)} %bitcast.place_ref.refs_0_, bf16[512,128]{1,0:T(8,128)(2,1)S(1)} %copy-done.3, f32[128,512]{1,0:T(8,128)S(1)} %get-tuple-element.23.refs_2_.turned_ref, bf16[512,1024]{1,0:T(8,128)(2,1)S(1)} %copy-done.1, ...), custom_call_target="tpu_custom_call" | custom-call | flops 3900000000 | bytes 11700000 | tf_op jit(solution)/shard_map/states1/pallas_call | solution.py:478
  7.1 0.5 %collective-permute-start.1 = (bf16[2,160,128]{2,1,0:T(8,128)(2,1)S(1)}, bf16[2,160,128]{2,1,0:T(8,128)(2,1)S(1)}, u32[]{:S(2)}, u32[]{:S(2)}) collective-permute-start(bf16[2,160,128]{2,1,0:T(8,128)(2,1)S(1)} %get-tuple-element.25), channel_id=1, source_target_pairs={{0,4},{2,6},{4,0},{6,2},{8,12},{10,14},{12,8},{14,10},{1,5},{3,7},... | collective-permute-start | bytes 245768 | tf_op jit(solution)/shard_map/ppermute | solution.py:505
  7.6 0.1 collective-permute-start
  7.7 0.6 %own_states.1.after_ref.refs_4_ = bf16[2,160,128]{2,1,0:T(8,128)(2,1)S(1)} custom-call(s32[1]{0:T(128)} %bitcast.place_ref.refs_0_, bf16[512,128]{1,0:T(8,128)(2,1)S(1)} %copy-done.3, f32[128,512]{1,0:T(8,128)S(1)} %get-tuple-element.23.refs_2_.turned_ref, bf16[512,1024]{1,0:T(8,128)(2,1)S(1)} %copy-done.1, ...), custom_call_target="tpu_custom_call" | custom-call | flops 2400000000 | bytes 7200000 | tf_op jit(solution)/shard_map/own_states/pallas_call | solution.py:478
  8.3 0.1 copy-done.5
  8.5 2.7 %block.1 = (f32[512,1024]{1,0:T(8,128)S(1)}, f32[512,1024]{1,0:T(8,128)S(1)}, f32[8,128]{1,0:T(8,128)S(1)}) custom-call(bf16[512,128]{1,0:T(8,128)(2,1)S(1)} %copy-done.5, f32[128,512]{1,0:T(8,128)S(1)} %get-tuple-element.23.refs_2_.turned_ref, bf16[512,1024]{1,0:T(8,128)(2,1)S(1)} %copy-done.1, f32[3,1024]{1,0:T(4,128)S(1)} %copy-done.6, ...), custom_call_target="tpu_custom_call" | custom-call | flops 8099999744 | bytes 24300000 | tf_op jit(solution)/shard_map/block/pallas_call | solution.py:478
  11.1 0.0 collective-permute-done.2.refs_7_
  11.2 0.4 %collective-permute-done.1.refs_6_ = bf16[2,160,128]{2,1,0:T(8,128)(2,1)S(1)} collective-permute-done((bf16[2,160,128]{2,1,0:T(8,128)(2,1)S(1)}, bf16[2,160,128]{2,1,0:T(8,128)(2,1)S(1)}, u32[]{:S(2)}, u32[]{:S(2)}) %collective-permute-start.1) | collective-permute-done | bytes 81952 | tf_op jit(solution)/shard_map/ppermute | solution.py:505
  11.5 0.5 %collective-permute-done.refs_5_ = bf16[2,160,128]{2,1,0:T(8,128)(2,1)S(1)} collective-permute-done((bf16[2,160,128]{2,1,0:T(8,128)(2,1)S(1)}, bf16[2,160,128]{2,1,0:T(8,128)(2,1)S(1)}, u32[]{:S(2)}, u32[]{:S(2)}) %collective-permute-start) | collective-permute-done | bytes 81952 | tf_op jit(solution)/shard_map/ppermute | solution.py:505
  12.0 0.9 %merge_group.1 = (bf16[2,160,128]{2,1,0:T(8,128)(2,1)S(1)}, f32[3,2,160,128]{3,2,1,0:T(8,128)S(1)}, f32[2,2,160,128]{3,2,1,0:T(8,128)S(1)}, f32[2,8,128]{2,1,0:T(8,128)S(1)}) custom-call(s32[1]{0:T(128)} %bitcast.place_ref.refs_0_, f32[3,1024]{1,0:T(4,128)S(1)} %copy-done.6, bf16[640,128]{1,0:T(8,128)(2,1)S(1)} %copy-done.8, f32[3,160,8]{2,1,0:T(8,128)S(1)} %copy-done.7, ...), custom_call_target="tpu_custom_call" | custom-call | flops 6000000000 | bytes 18000000 | tf_op jit(solution)/shard_map/merge_group/pallas_call | solution.py:478
  12.9 0.0 copy-start.10
  12.9 2.6 %collective-permute-start.3 = (bf16[2,160,128]{2,1,0:T(8,128)(2,1)S(1)}, bf16[2,160,128]{2,1,0:T(8,128)(2,1)S(1)}, u32[]{:S(2)}, u32[]{:S(2)}) collective-permute-start(bf16[2,160,128]{2,1,0:T(8,128)(2,1)S(1)} %get-tuple-element.27.after_ref), channel_id=1, source_target_pairs={{0,8},{2,10},{4,12},{6,14},{8,0},{10,2},{12,4},{14,6},{1,9},{3,11}... | collective-permute-start | bytes 245768 | tf_op jit(solution)/shard_map/ppermute | solution.py:505
  15.6 2.9 %collective-permute-start.7 = (bf16[128,1024]{1,0:T(8,128)(2,1)S(1)}, bf16[128,1024]{1,0:T(8,128)(2,1)S(1)}, u32[]{:S(2)}, u32[]{:S(2)}) collective-permute-start(bf16[128,1024]{1,0:T(8,128)(2,1)S(1)} %edge.1.after_ref), channel_id=1, source_target_pairs={{0,2},{2,4},{4,6},{6,8},{8,10},{10,12},{12,14},{1,3},{3,5},{5,7},{... | collective-permute-start | bytes 786440 | tf_op jit(solution)/shard_map/ppermute | solution.py:595
  18.5 1.1 %query_features.1 = (bf16[8,512,256]{2,1,0:T(8,128)(2,1)S(1)}, f32[8,128]{1,0:T(8,128)S(1)}) custom-call(bf16[512,128]{1,0:T(8,128)(2,1)S(1)} %copy-done.5, bf16[512,128]{1,0:T(8,128)(2,1)S(1)} %copy-done.3, f32[8,512]{1,0:T(8,128)S(1)} %get-tuple-element.22.refs_4_.refs_7_.cum_ref, bf16[160,224]{1,0:T(8,128)(2,1)S(1)} %copy-done.10, ...), custom_call_target="tpu_custom_call" | custom-call | flops 4499999744 | bytes 13500000 | tf_op jit(solution)/shard_map/query_features/pallas_call | solution.py:478
  19.7 0.0 collective-permute-done.3.base_ref
  19.7 0.0 copy-start.2
  19.7 0.1 spread.1
  19.8 2.1 %collective-permute-start.4 = (bf16[2,160,128]{2,1,0:T(8,128)(2,1)S(1)}, bf16[2,160,128]{2,1,0:T(8,128)(2,1)S(1)}, u32[]{:S(2)}, u32[]{:S(2)}) collective-permute-start(bf16[2,160,128]{2,1,0:T(8,128)(2,1)S(1)} %get-tuple-element.34), channel_id=1, source_target_pairs={{0,2},{2,0},{4,6},{6,4},{8,10},{10,8},{12,14},{14,12},{1,3},{3,1},... | collective-permute-start | bytes 245768 | tf_op jit(solution)/shard_map/ppermute | solution.py:505
  21.9 0.1 collective-permute-start.5
  22.0 1.5 %collective-permute-start.6 = (bf16[2,160,128]{2,1,0:T(8,128)(2,1)S(1)}, bf16[2,160,128]{2,1,0:T(8,128)(2,1)S(1)}, u32[]{:S(2)}, u32[]{:S(2)}) collective-permute-start(bf16[2,160,128]{2,1,0:T(8,128)(2,1)S(1)} %get-tuple-element.36), channel_id=1, source_target_pairs={{0,6},{2,4},{4,2},{6,0},{8,14},{10,12},{12,10},{14,8},{1,7},{3,5},... | collective-permute-start | bytes 245768 | tf_op jit(solution)/shard_map/ppermute | solution.py:505
  23.5 1.9 %window.1.after_ref.win_ref = f32[448,1024]{1,0:T(8,128)S(1)} custom-call(bf16[512,1024]{1,0:T(8,128)(2,1)S(1)} %copy-done.2, bf16[512,1024]{1,0:T(8,128)(2,1)S(1)} %copy-done, bf16[512,1024]{1,0:T(8,128)(2,1)S(1)} %copy-done.1, bf16[2,160,128]{2,1,0:T(8,128)(2,1)S(1)} %get-tuple-element.33.after_ref.x0), custom_call_target="tpu_custom_call" | custom-call | flops 6000000000 | bytes 18000000 | tf_op jit(solution)/shard_map/window/pallas_call | solution.py:478
  25.4 0.0 collective-permute-done.7.halo_ref
  25.4 0.7 %window_first.1.early_ref = f32[64,1024]{1,0:T(8,128)S(1)} custom-call(s32[1]{0:T(128)} %bitcast.place_ref.refs_0_, bf16[512,1024]{1,0:T(8,128)(2,1)S(1)} %copy-done.2, bf16[512,1024]{1,0:T(8,128)(2,1)S(1)} %copy-done, bf16[512,1024]{1,0:T(8,128)(2,1)S(1)} %copy-done.1, bf16[128,1024]{1,0:T(8,128)(2,1)S(1)} %collective-permute-done.7.halo_ref, ...), custom_call_target="tpu_custom_call" | custom-call | flops 1200000000 | bytes 3600000 | tf_op jit(solution)/shard_map/window_first/pallas_call | solution.py:478
  26.1 0.0 collective-permute-done.4.x1
  26.1 0.2 collective-permute-done.5.x2
  26.4 1.0 %collective-permute-done.6.x3 = bf16[2,160,128]{2,1,0:T(8,128)(2,1)S(1)} collective-permute-done((bf16[2,160,128]{2,1,0:T(8,128)(2,1)S(1)}, bf16[2,160,128]{2,1,0:T(8,128)(2,1)S(1)}, u32[]{:S(2)}, u32[]{:S(2)}) %collective-permute-start.6) | collective-permute-done | bytes 81952 | tf_op jit(solution)/shard_map/ppermute | solution.py:505
  27.3 1.7 %finish.1 = bf16[512,1024]{1,0:T(8,128)(2,1)} custom-call(s32[1]{0:T(128)} %bitcast.place_ref.refs_0_, bf16[8,512,256]{2,1,0:T(8,128)(2,1)S(1)} %get-tuple-element.28.phi_ref, bf16[2,160,128]{2,1,0:T(8,128)(2,1)S(1)} %get-tuple-element.33.after_ref.x0, bf16[2,160,128]{2,1,0:T(8,128)(2,1)S(1)} %collective-permute-done.4.x1, ...), custom_call_target="tpu_custom_call" | custom-call | flops 6300000256 | bytes 18900000 | tf_op jit(solution)/shard_map/finish/pallas_call | solution.py:478
  (19 shorter events, 0.1 us)
Async XLA Ops:
  0.0 0.9 %copy-start.3 = (bf16[512,128]{1,0:T(8,128)(2,1)S(1)}, bf16[512,128]{1,0:T(8,128)(2,1)}, u32[]{:S(2)}) copy-start(bf16[512,128]{1,0:T(8,128)(2,1)} %k_ref.3) | copy-start | bytes 393220
  0.0 0.9 %copy-start.4 = (f32[512,8]{0,1:T(8,128)S(1)}, f32[512,8]{0,1:T(8,128)}, u32[]{:S(2)}) copy-start(f32[512,8]{0,1:T(8,128)} %param.16) | copy-start | bytes 49156
  0.0 1.3 %copy-start.1 = (bf16[512,1024]{1,0:T(8,128)(2,1)S(1)}, bf16[512,1024]{1,0:T(8,128)(2,1)}, u32[]{:S(2)}) copy-start(bf16[512,1024]{1,0:T(8,128)(2,1)} %v_ref.7) | copy-start | bytes 3145732
  0.0 1.3 %copy-start.6 = (f32[3,1024]{1,0:T(4,128)S(1)}, f32[3,1024]{1,0:T(4,128)}, u32[]{:S(2)}) copy-start(f32[3,1024]{1,0:T(4,128)} %w_ref.3) | copy-start | bytes 36868
  0.0 1.3 %copy-start.9 = (bf16[256,224]{1,0:T(8,128)(2,1)S(1)}, bf16[256,224]{1,0:T(8,128)(2,1)}, u32[]{:S(2)}) copy-start(bf16[256,224]{1,0:T(8,128)(2,1)} %constant.16.clone.refs_6_) | copy-start | bytes 344068
  2.0 9.2 %collective-permute-start.2 = (bf16[2,160,128]{2,1,0:T(8,128)(2,1)S(1)}, bf16[2,160,128]{2,1,0:T(8,128)(2,1)S(1)}, u32[]{:S(2)}, u32[]{:S(2)}) collective-permute-start(bf16[2,160,128]{2,1,0:T(8,128)(2,1)S(1)} %states0.1.refs_7_), channel_id=1, source_target_pairs={{0,6},{2,4},{4,2},{6,0},{8,14},{10,12},{12,10},{14,8},{1,7},{3,5},... | collective-permute-start | bytes 245768 | tf_op jit(solution)/shard_map/ppermute | solution.py:505
  7.1 4.5 %collective-permute-start.1 = (bf16[2,160,128]{2,1,0:T(8,128)(2,1)S(1)}, bf16[2,160,128]{2,1,0:T(8,128)(2,1)S(1)}, u32[]{:S(2)}, u32[]{:S(2)}) collective-permute-start(bf16[2,160,128]{2,1,0:T(8,128)(2,1)S(1)} %get-tuple-element.25), channel_id=1, source_target_pairs={{0,4},{2,6},{4,0},{6,2},{8,12},{10,14},{12,8},{14,10},{1,5},{3,7},... | collective-permute-start | bytes 245768 | tf_op jit(solution)/shard_map/ppermute | solution.py:505
  7.6 0.9 %copy-start.5 = (bf16[512,128]{1,0:T(8,128)(2,1)S(1)}, bf16[512,128]{1,0:T(8,128)(2,1)}, u32[]{:S(2)}) copy-start(bf16[512,128]{1,0:T(8,128)(2,1)} %q_ref.3) | copy-start | bytes 393220
  7.6 4.4 %collective-permute-start = (bf16[2,160,128]{2,1,0:T(8,128)(2,1)S(1)}, bf16[2,160,128]{2,1,0:T(8,128)(2,1)S(1)}, u32[]{:S(2)}, u32[]{:S(2)}) collective-permute-start(bf16[2,160,128]{2,1,0:T(8,128)(2,1)S(1)} %get-tuple-element.24.refs_7_), channel_id=1, source_target_pairs={{0,2},{2,0},{4,6},{6,4},{8,10},{10,8},{12,14},{14,12},{1,3},{3,1},... | collective-permute-start | bytes 245768 | tf_op jit(solution)/shard_map/ppermute | solution.py:505
  8.5 3.5 %copy-start.7 = (f32[3,160,8]{2,1,0:T(8,128)S(1)}, f32[3,160,8]{2,1,0:T(8,128)}, u32[]{:S(2)}) copy-start(f32[3,160,8]{2,1,0:T(8,128)} %constant.15.clone.refs_3_) | copy-start | bytes 46084
  8.5 3.5 %copy-start.8 = (bf16[640,128]{1,0:T(8,128)(2,1)S(1)}, bf16[640,128]{1,0:T(8,128)(2,1)}, u32[]{:S(2)}) copy-start(bf16[640,128]{1,0:T(8,128)(2,1)} %constant.14.clone.refs_2_) | copy-start | bytes 491524
  12.0 3.6 %copy-start = (bf16[512,1024]{1,0:T(8,128)(2,1)S(1)}, bf16[512,1024]{1,0:T(8,128)(2,1)}, u32[]{:S(2)}) copy-start(bf16[512,1024]{1,0:T(8,128)(2,1)} %wk_ref.3) | copy-start | bytes 3145732
  12.9 5.6 %copy-start.10 = (bf16[160,224]{1,0:T(8,128)(2,1)S(1)}, bf16[160,224]{1,0:T(8,128)(2,1)}, u32[]{:S(2)}) copy-start(bf16[160,224]{1,0:T(8,128)(2,1)} %constant.17.clone.pick_ref) | copy-start | bytes 215044
  12.9 6.7 %collective-permute-start.3 = (bf16[2,160,128]{2,1,0:T(8,128)(2,1)S(1)}, bf16[2,160,128]{2,1,0:T(8,128)(2,1)S(1)}, u32[]{:S(2)}, u32[]{:S(2)}) collective-permute-start(bf16[2,160,128]{2,1,0:T(8,128)(2,1)S(1)} %get-tuple-element.27.after_ref), channel_id=1, source_target_pairs={{0,8},{2,10},{4,12},{6,14},{8,0},{10,2},{12,4},{14,6},{1,9},{3,11}... | collective-permute-start | bytes 245768 | tf_op jit(solution)/shard_map/ppermute | solution.py:505
  15.6 9.8 %collective-permute-start.7 = (bf16[128,1024]{1,0:T(8,128)(2,1)S(1)}, bf16[128,1024]{1,0:T(8,128)(2,1)S(1)}, u32[]{:S(2)}, u32[]{:S(2)}) collective-permute-start(bf16[128,1024]{1,0:T(8,128)(2,1)S(1)} %edge.1.after_ref), channel_id=1, source_target_pairs={{0,2},{2,4},{4,6},{6,8},{8,10},{10,12},{12,14},{1,3},{3,5},{5,7},{... | collective-permute-start | bytes 786440 | tf_op jit(solution)/shard_map/ppermute | solution.py:595
  19.7 3.8 %copy-start.2 = (bf16[512,1024]{1,0:T(8,128)(2,1)S(1)}, bf16[512,1024]{1,0:T(8,128)(2,1)}, u32[]{:S(2)}) copy-start(bf16[512,1024]{1,0:T(8,128)(2,1)} %wq_ref.3) | copy-start | bytes 3145732
  19.8 6.3 %collective-permute-start.4 = (bf16[2,160,128]{2,1,0:T(8,128)(2,1)S(1)}, bf16[2,160,128]{2,1,0:T(8,128)(2,1)S(1)}, u32[]{:S(2)}, u32[]{:S(2)}) collective-permute-start(bf16[2,160,128]{2,1,0:T(8,128)(2,1)S(1)} %get-tuple-element.34), channel_id=1, source_target_pairs={{0,2},{2,0},{4,6},{6,4},{8,10},{10,8},{12,14},{14,12},{1,3},{3,1},... | collective-permute-start | bytes 245768 | tf_op jit(solution)/shard_map/ppermute | solution.py:505
  21.9 4.4 %collective-permute-start.5 = (bf16[2,160,128]{2,1,0:T(8,128)(2,1)S(1)}, bf16[2,160,128]{2,1,0:T(8,128)(2,1)S(1)}, u32[]{:S(2)}, u32[]{:S(2)}) collective-permute-start(bf16[2,160,128]{2,1,0:T(8,128)(2,1)S(1)} %get-tuple-element.35), channel_id=1, source_target_pairs={{0,4},{2,6},{4,0},{6,2},{8,12},{10,14},{12,8},{14,10},{1,5},{3,7},... | collective-permute-start | bytes 245768 | tf_op jit(solution)/shard_map/ppermute | solution.py:505
  22.0 5.3 %collective-permute-start.6 = (bf16[2,160,128]{2,1,0:T(8,128)(2,1)S(1)}, bf16[2,160,128]{2,1,0:T(8,128)(2,1)S(1)}, u32[]{:S(2)}, u32[]{:S(2)}) collective-permute-start(bf16[2,160,128]{2,1,0:T(8,128)(2,1)S(1)} %get-tuple-element.36), channel_id=1, source_target_pairs={{0,6},{2,4},{4,2},{6,0},{8,14},{10,12},{12,10},{14,8},{1,7},{3,5},... | collective-permute-start | bytes 245768 | tf_op jit(solution)/shard_map/ppermute | solution.py:505

commit v7 on v6

--- a/solution.py
+++ b/solution.py
@@ -383,19 +383,19 @@
     cum_row = cum_ref[...] * LOG2E
     cum_col = cum_row.T
     token_ref[...] = jnp.zeros(token_ref.shape, F32)
-    level = iota(turned_ref.shape, 0)
     step, piece = 256, 128
     ones = jnp.ones((rows, 128), BF16)
     causal = iota((piece, piece), 0) >= iota((piece, piece), 1)
     for h in range(heads):
         at = slice(128 * h, 128 * h + 128)
-        here = (level >= h * width) & (level < (h + 1) * width)
-        k_here = jnp.where(here, turned_ref[...] * width ** (-0.5), 0.0).astype(BF16)
+        mine = (turned_ref[h * width : (h + 1) * width] * width ** (-0.5)).astype(BF16)
+        pieces = [jnp.zeros((h * width, rows), BF16), mine, jnp.zeros((wide - (h + 1) * width, rows), BF16)]
+        k_here = jnp.concatenate([x for x in pieces if x.shape[0]])
         v = v_ref[:, at].astype(F32)
         w = w_ref[:, at]
         conv = w[0:1] * v + w[1:2] * shifted(v, 1) + w[2:3] * shifted(v, 2)
         right = jnp.concatenate([conv.astype(BF16), ones], axis=1)
-        column = jnp.broadcast_to(cum_col[:, h : h + 1], (rows, piece))
+        column = jnp.broadcast_to(cum_col[:, h : h + 1] - 1.0, (rows, piece))
         total = None
         for low in range(0, rows, step):
             x = nn(q[low:], k_here[:, low : low + step])
@@ -410,7 +410,8 @@
                     gap = column[i : i + piece] - cum_row[h : h + 1, j : j + piece]
                     if i == j:
                         gap = jnp.where(causal, gap, -jnp.inf)
-                    line.append((((0.5 * here + 1.0) * here + 1.0) * jnp.exp2(gap)).astype(BF16))
+                    here = here + 1.0
+                    line.append(((here * here + 1.0) * jnp.exp2(gap)).astype(BF16))
                 lines.append(jnp.concatenate(line, axis=1))
             both = nn(jnp.concatenate(lines), right[low : low + step])
             total = both if total is None else jnp.concatenate([total[:low], total[low:] + both])
@@ -594,17 +595,9 @@
     )
     halo = lax.ppermute(edge, "seq", [(i, i + 1) for i in range(count - 1)])
 
-    phi, token = call(
-        query_kernel,
-        (q_feat, k_feat, cum, pick_queries, edge),
-        [jax.ShapeDtypeStruct((heads, rows, 256), BF16), wide(8, 128)],
-        free=(4,),
-        name="query_features",
-        us=1.5,
-    )
     here, *sent = call(
         spread_kernel,
-        (place, conv_weight, base, before, keys, small, token),
+        (place, conv_weight, base, before, keys, small, edge),
         [shape] * 4,
         [held],
         smem=(0,),
@@ -613,9 +606,17 @@
         us=1.0,
     )
     prefixes = [here] + [swap(x, d) for d, x in zip((1, 2, 3), sent)]
+    phi, token = call(
+        query_kernel,
+        (q_feat, k_feat, cum, pick_queries, here),
+        [jax.ShapeDtypeStruct((heads, rows, 256), BF16), wide(8, 128)],
+        free=(4,),
+        name="query_features",
+        us=1.5,
+    )
     win = call(
         window_kernel,
-        (win_query, win_key, values, here),
+        (win_query, win_key, values, token),
         wide(rows - WINDOW, values.shape[1]),
         free=(3,),
         name="window",

time: 29.2 us -> 29.2 us (level)
  transfers between devices with their start and end apart: 8 -> 8, of which waited for: 4 -> 5; matrix products, arithmetic and copies ran while one was open for 0% -> 0% of each run, Pallas kernels for 28% -> 28%
where the time goes in v7:
time: 29.2 us; the launch traced here: 29 us
  starting transfers between devices  13.9 us (48%)
  Pallas kernels  11.9 us (41%)
  waiting for transfers between devices  1.94 us (7%)
  local copies, waits for them, and re-layouts  1.19 us (4%)
    pallas_call x13, Pallas kernels, call(): pl.pallas_call(kernel, out_shape=outs, in_specs=[pl.BlockSpec(memory_spac...  11.9 us
    ppermute x7, starting transfers between devices, swap(): return lax.ppermute(x, 'seq', [(i, i ^ distance) for i in range(count)])  11 us
    ppermute x1, starting transfers between devices, local(): halo = lax.ppermute(edge, 'seq', [(i, i + 1) for i in range(count - 1)])  2.91 us
    ppermute x7, waiting for transfers between devices, swap(): return lax.ppermute(x, 'seq', [(i, i ^ distance) for i in range(count)])  1.83 us
    unnamed x22, local copies, waits for them, and re-layouts  1.19 us
  transfers between devices with their start and end apart: 8, of which 5 were waited for; matrix products, arithmetic and copies ran while one was open for 0% of the time, Pallas kernels for 28%

profile of v7, /device:TPU:0, one launch (start us, length us, event | category | flops | bytes accessed | tf_op | source)
XLA Modules:
  0.0 29.0 jit_solution(12113478029440463115)
XLA Ops:
  0.0 0.9 %copy-done.3 = bf16[512,128]{1,0:T(8,128)(2,1)S(1)} copy-done((bf16[512,128]{1,0:T(8,128)(2,1)S(1)}, bf16[512,128]{1,0:T(8,128)(2,1)}, u32[]{:S(2)}) %copy-start.3) | copy-done | bytes 131096
  0.9 0.4 %gates.1 = (f32[8,512]{1,0:T(8,128)S(1)}, f32[128,512]{1,0:T(8,128)S(1)}) custom-call(f32[8,512]{1,0:T(8,128)S(1)} %bitcast.2, bf16[512,128]{1,0:T(8,128)(2,1)S(1)} %copy-done.3, f32[8,128]{1,0:T(8,128)S(1)} %open.1.after_ref), custom_call_target="tpu_custom_call" | custom-call | flops 30000000 | bytes 90000 | tf_op jit(solution)/shard_map/gates/pallas_call | solution.py:479
  1.3 0.0 copy-done
  1.3 0.6 %states0.1.refs_7_ = bf16[2,160,128]{2,1,0:T(8,128)(2,1)S(1)} custom-call(s32[1]{0:T(128)} %bitcast.place_ref.refs_0_, bf16[512,128]{1,0:T(8,128)(2,1)S(1)} %copy-done.3, f32[128,512]{1,0:T(8,128)S(1)} %get-tuple-element.23.refs_2_.turned_ref, bf16[512,1024]{1,0:T(8,128)(2,1)S(1)} %copy-done, f32[8,512]{1,0:T(8,128)S(1)} %get-tuple-element.22.refs_4_.refs_7_.cum_ref, ...), custom_call_target="tpu_custom_call" | custom-call | flops 2400000000 | bytes 7200000 | tf_op jit(solution)/shard_map/states0/pallas_call | solution.py:479
  2.0 4.0 %collective-permute-start.2 = (bf16[2,160,128]{2,1,0:T(8,128)(2,1)S(1)}, bf16[2,160,128]{2,1,0:T(8,128)(2,1)S(1)}, u32[]{:S(2)}, u32[]{:S(2)}) collective-permute-start(bf16[2,160,128]{2,1,0:T(8,128)(2,1)S(1)} %states0.1.refs_7_), channel_id=1, source_target_pairs={{0,6},{2,4},{4,2},{6,0},{8,14},{10,12},{12,10},{14,8},{1,7},{3,5},... | collective-permute-start | bytes 245768 | tf_op jit(solution)/shard_map/ppermute | solution.py:506
  6.0 1.1 %states1.1 = (bf16[2,160,128]{2,1,0:T(8,128)(2,1)S(1)}, bf16[2,160,128]{2,1,0:T(8,128)(2,1)S(1)}) custom-call(s32[1]{0:T(128)} %bitcast.place_ref.refs_0_, bf16[512,128]{1,0:T(8,128)(2,1)S(1)} %copy-done.3, f32[128,512]{1,0:T(8,128)S(1)} %get-tuple-element.23.refs_2_.turned_ref, bf16[512,1024]{1,0:T(8,128)(2,1)S(1)} %copy-done, ...), custom_call_target="tpu_custom_call" | custom-call | flops 3900000000 | bytes 11700000 | tf_op jit(solution)/shard_map/states1/pallas_call | solution.py:479
  7.1 0.5 %collective-permute-start.1 = (bf16[2,160,128]{2,1,0:T(8,128)(2,1)S(1)}, bf16[2,160,128]{2,1,0:T(8,128)(2,1)S(1)}, u32[]{:S(2)}, u32[]{:S(2)}) collective-permute-start(bf16[2,160,128]{2,1,0:T(8,128)(2,1)S(1)} %get-tuple-element.25), channel_id=1, source_target_pairs={{0,4},{2,6},{4,0},{6,2},{8,12},{10,14},{12,8},{14,10},{1,5},{3,7},... | collective-permute-start | bytes 245768 | tf_op jit(solution)/shard_map/ppermute | solution.py:506
  7.6 0.1 collective-permute-start
  7.7 0.6 %own_states.1.after_ref.refs_4_ = bf16[2,160,128]{2,1,0:T(8,128)(2,1)S(1)} custom-call(s32[1]{0:T(128)} %bitcast.place_ref.refs_0_, bf16[512,128]{1,0:T(8,128)(2,1)S(1)} %copy-done.3, f32[128,512]{1,0:T(8,128)S(1)} %get-tuple-element.23.refs_2_.turned_ref, bf16[512,1024]{1,0:T(8,128)(2,1)S(1)} %copy-done, ...), custom_call_target="tpu_custom_call" | custom-call | flops 2400000000 | bytes 7200000 | tf_op jit(solution)/shard_map/own_states/pallas_call | solution.py:479
  8.3 0.1 copy-done.5
  8.5 2.7 %block.1 = (f32[512,1024]{1,0:T(8,128)S(1)}, f32[512,1024]{1,0:T(8,128)S(1)}, f32[8,128]{1,0:T(8,128)S(1)}) custom-call(bf16[512,128]{1,0:T(8,128)(2,1)S(1)} %copy-done.5, f32[128,512]{1,0:T(8,128)S(1)} %get-tuple-element.23.refs_2_.turned_ref, bf16[512,1024]{1,0:T(8,128)(2,1)S(1)} %copy-done, f32[3,1024]{1,0:T(4,128)S(1)} %copy-done.6, ...), custom_call_target="tpu_custom_call" | custom-call | flops 8099999744 | bytes 24300000 | tf_op jit(solution)/shard_map/block/pallas_call | solution.py:479
  11.1 0.0 collective-permute-done.2.refs_7_
  11.1 0.4 %collective-permute-done.1.refs_6_ = bf16[2,160,128]{2,1,0:T(8,128)(2,1)S(1)} collective-permute-done((bf16[2,160,128]{2,1,0:T(8,128)(2,1)S(1)}, bf16[2,160,128]{2,1,0:T(8,128)(2,1)S(1)}, u32[]{:S(2)}, u32[]{:S(2)}) %collective-permute-start.1) | collective-permute-done | bytes 81952 | tf_op jit(solution)/shard_map/ppermute | solution.py:506
  11.5 0.5 %collective-permute-done.refs_5_ = bf16[2,160,128]{2,1,0:T(8,128)(2,1)S(1)} collective-permute-done((bf16[2,160,128]{2,1,0:T(8,128)(2,1)S(1)}, bf16[2,160,128]{2,1,0:T(8,128)(2,1)S(1)}, u32[]{:S(2)}, u32[]{:S(2)}) %collective-permute-start) | collective-permute-done | bytes 81952 | tf_op jit(solution)/shard_map/ppermute | solution.py:506
  12.0 0.9 %merge_group.1 = (bf16[2,160,128]{2,1,0:T(8,128)(2,1)S(1)}, f32[3,2,160,128]{3,2,1,0:T(8,128)S(1)}, f32[2,2,160,128]{3,2,1,0:T(8,128)S(1)}, f32[2,8,128]{2,1,0:T(8,128)S(1)}) custom-call(s32[1]{0:T(128)} %bitcast.place_ref.refs_0_, f32[3,1024]{1,0:T(4,128)S(1)} %copy-done.6, bf16[640,128]{1,0:T(8,128)(2,1)S(1)} %copy-done.8, f32[3,160,8]{2,1,0:T(8,128)S(1)} %copy-done.7, ...), custom_call_target="tpu_custom_call" | custom-call | flops 6000000000 | bytes 18000000 | tf_op jit(solution)/shard_map/merge_group/pallas_call | solution.py:479
  12.9 2.6 %collective-permute-start.3 = (bf16[2,160,128]{2,1,0:T(8,128)(2,1)S(1)}, bf16[2,160,128]{2,1,0:T(8,128)(2,1)S(1)}, u32[]{:S(2)}, u32[]{:S(2)}) collective-permute-start(bf16[2,160,128]{2,1,0:T(8,128)(2,1)S(1)} %get-tuple-element.27.after_ref), channel_id=1, source_target_pairs={{0,8},{2,10},{4,12},{6,14},{8,0},{10,2},{12,4},{14,6},{1,9},{3,11}... | collective-permute-start | bytes 245768 | tf_op jit(solution)/shard_map/ppermute | solution.py:506
  15.6 2.9 %collective-permute-start.7 = (bf16[128,1024]{1,0:T(8,128)(2,1)S(1)}, bf16[128,1024]{1,0:T(8,128)(2,1)S(1)}, u32[]{:S(2)}, u32[]{:S(2)}) collective-permute-start(bf16[128,1024]{1,0:T(8,128)(2,1)S(1)} %edge.1.after_ref), channel_id=1, source_target_pairs={{0,2},{2,4},{4,6},{6,8},{8,10},{10,12},{12,14},{1,3},{3,5},{5,7},{... | collective-permute-start | bytes 786440 | tf_op jit(solution)/shard_map/ppermute | solution.py:596
  18.5 0.0 collective-permute-done.3.base_ref
  18.5 0.0 copy-start.10
  18.5 0.1 spread.1
  18.7 2.1 %collective-permute-start.4 = (bf16[2,160,128]{2,1,0:T(8,128)(2,1)S(1)}, bf16[2,160,128]{2,1,0:T(8,128)(2,1)S(1)}, u32[]{:S(2)}, u32[]{:S(2)}) collective-permute-start(bf16[2,160,128]{2,1,0:T(8,128)(2,1)S(1)} %get-tuple-element.33), channel_id=1, source_target_pairs={{0,2},{2,0},{4,6},{6,4},{8,10},{10,8},{12,14},{14,12},{1,3},{3,1},... | collective-permute-start | bytes 245768 | tf_op jit(solution)/shard_map/ppermute | solution.py:506
  20.8 1.2 %collective-permute-start.5 = (bf16[2,160,128]{2,1,0:T(8,128)(2,1)S(1)}, bf16[2,160,128]{2,1,0:T(8,128)(2,1)S(1)}, u32[]{:S(2)}, u32[]{:S(2)}) collective-permute-start(bf16[2,160,128]{2,1,0:T(8,128)(2,1)S(1)} %get-tuple-element.34), channel_id=1, source_target_pairs={{0,4},{2,6},{4,0},{6,2},{8,12},{10,14},{12,8},{14,10},{1,5},{3,7},... | collective-permute-start | bytes 245768 | tf_op jit(solution)/shard_map/ppermute | solution.py:506
  21.9 0.4 %collective-permute-start.6 = (bf16[2,160,128]{2,1,0:T(8,128)(2,1)S(1)}, bf16[2,160,128]{2,1,0:T(8,128)(2,1)S(1)}, u32[]{:S(2)}, u32[]{:S(2)}) collective-permute-start(bf16[2,160,128]{2,1,0:T(8,128)(2,1)S(1)} %get-tuple-element.35), channel_id=1, source_target_pairs={{0,6},{2,4},{4,2},{6,0},{8,14},{10,12},{12,10},{14,8},{1,7},{3,5},... | collective-permute-start | bytes 245768 | tf_op jit(solution)/shard_map/ppermute | solution.py:506
  22.3 1.1 %query_features.1 = (bf16[8,512,256]{2,1,0:T(8,128)(2,1)S(1)}, f32[8,128]{1,0:T(8,128)S(1)}) custom-call(bf16[512,128]{1,0:T(8,128)(2,1)S(1)} %copy-done.5, bf16[512,128]{1,0:T(8,128)(2,1)S(1)} %copy-done.3, f32[8,512]{1,0:T(8,128)S(1)} %get-tuple-element.22.refs_4_.refs_7_.cum_ref, bf16[160,224]{1,0:T(8,128)(2,1)S(1)} %copy-done.10, ...), custom_call_target="tpu_custom_call" | custom-call | flops 4499999744 | bytes 13500000 | tf_op jit(solution)/shard_map/query_features/pallas_call | solution.py:479
  23.4 0.1 copy-done.2
  23.6 1.9 %window.1.after_ref.win_ref = f32[448,1024]{1,0:T(8,128)S(1)} custom-call(bf16[512,1024]{1,0:T(8,128)(2,1)S(1)} %copy-done.2, bf16[512,1024]{1,0:T(8,128)(2,1)S(1)} %copy-done.1, bf16[512,1024]{1,0:T(8,128)(2,1)S(1)} %copy-done, f32[8,128]{1,0:T(8,128)S(1)} %get-tuple-element.38.after_ref), custom_call_target="tpu_custom_call" | custom-call | flops 6000000000 | bytes 18000000 | tf_op jit(solution)/shard_map/window/pallas_call | solution.py:479
  25.5 0.1 collective-permute-done.7.halo_ref
  25.6 0.7 %window_first.1.early_ref = f32[64,1024]{1,0:T(8,128)S(1)} custom-call(s32[1]{0:T(128)} %bitcast.place_ref.refs_0_, bf16[512,1024]{1,0:T(8,128)(2,1)S(1)} %copy-done.2, bf16[512,1024]{1,0:T(8,128)(2,1)S(1)} %copy-done.1, bf16[512,1024]{1,0:T(8,128)(2,1)S(1)} %copy-done, bf16[128,1024]{1,0:T(8,128)(2,1)S(1)} %collective-permute-done.7.halo_ref, ...), custom_call_target="tpu_custom_call" | custom-call | flops 1200000000 | bytes 3600000 | tf_op jit(solution)/shard_map/window_first/pallas_call | solution.py:479
  26.3 0.1 collective-permute-done.4.x1
  26.4 0.0 collective-permute-done.5.x2
  26.4 0.9 %collective-permute-done.6.x3 = bf16[2,160,128]{2,1,0:T(8,128)(2,1)S(1)} collective-permute-done((bf16[2,160,128]{2,1,0:T(8,128)(2,1)S(1)}, bf16[2,160,128]{2,1,0:T(8,128)(2,1)S(1)}, u32[]{:S(2)}, u32[]{:S(2)}) %collective-permute-start.6) | collective-permute-done | bytes 81952 | tf_op jit(solution)/shard_map/ppermute | solution.py:506
  27.3 1.7 %finish.1 = bf16[512,1024]{1,0:T(8,128)(2,1)} custom-call(s32[1]{0:T(128)} %bitcast.place_ref.refs_0_, bf16[8,512,256]{2,1,0:T(8,128)(2,1)S(1)} %get-tuple-element.32.phi_ref, bf16[2,160,128]{2,1,0:T(8,128)(2,1)S(1)} %get-tuple-element.31.after_ref.x0, bf16[2,160,128]{2,1,0:T(8,128)(2,1)S(1)} %collective-permute-done.4.x1, ...), custom_call_target="tpu_custom_call" | custom-call | flops 6300000256 | bytes 18900000 | tf_op jit(solution)/shard_map/finish/pallas_call | solution.py:479
  (19 shorter events, 0.1 us)
Async XLA Ops:
  0.0 0.9 %copy-start.3 = (bf16[512,128]{1,0:T(8,128)(2,1)S(1)}, bf16[512,128]{1,0:T(8,128)(2,1)}, u32[]{:S(2)}) copy-start(bf16[512,128]{1,0:T(8,128)(2,1)} %k_ref.3) | copy-start | bytes 393220
  0.0 0.9 %copy-start.4 = (f32[512,8]{0,1:T(8,128)S(1)}, f32[512,8]{0,1:T(8,128)}, u32[]{:S(2)}) copy-start(f32[512,8]{0,1:T(8,128)} %param.16) | copy-start | bytes 49156
  0.0 1.3 %copy-start = (bf16[512,1024]{1,0:T(8,128)(2,1)S(1)}, bf16[512,1024]{1,0:T(8,128)(2,1)}, u32[]{:S(2)}) copy-start(bf16[512,1024]{1,0:T(8,128)(2,1)} %v_ref.7) | copy-start | bytes 3145732
  0.0 1.3 %copy-start.6 = (f32[3,1024]{1,0:T(4,128)S(1)}, f32[3,1024]{1,0:T(4,128)}, u32[]{:S(2)}) copy-start(f32[3,1024]{1,0:T(4,128)} %w_ref.3) | copy-start | bytes 36868
  0.0 1.3 %copy-start.9 = (bf16[256,224]{1,0:T(8,128)(2,1)S(1)}, bf16[256,224]{1,0:T(8,128)(2,1)}, u32[]{:S(2)}) copy-start(bf16[256,224]{1,0:T(8,128)(2,1)} %constant.16.clone.refs_6_) | copy-start | bytes 344068
  2.0 9.1 %collective-permute-start.2 = (bf16[2,160,128]{2,1,0:T(8,128)(2,1)S(1)}, bf16[2,160,128]{2,1,0:T(8,128)(2,1)S(1)}, u32[]{:S(2)}, u32[]{:S(2)}) collective-permute-start(bf16[2,160,128]{2,1,0:T(8,128)(2,1)S(1)} %states0.1.refs_7_), channel_id=1, source_target_pairs={{0,6},{2,4},{4,2},{6,0},{8,14},{10,12},{12,10},{14,8},{1,7},{3,5},... | collective-permute-start | bytes 245768 | tf_op jit(solution)/shard_map/ppermute | solution.py:506
  7.1 4.5 %collective-permute-start.1 = (bf16[2,160,128]{2,1,0:T(8,128)(2,1)S(1)}, bf16[2,160,128]{2,1,0:T(8,128)(2,1)S(1)}, u32[]{:S(2)}, u32[]{:S(2)}) collective-permute-start(bf16[2,160,128]{2,1,0:T(8,128)(2,1)S(1)} %get-tuple-element.25), channel_id=1, source_target_pairs={{0,4},{2,6},{4,0},{6,2},{8,12},{10,14},{12,8},{14,10},{1,5},{3,7},... | collective-permute-start | bytes 245768 | tf_op jit(solution)/shard_map/ppermute | solution.py:506
  7.6 0.9 %copy-start.5 = (bf16[512,128]{1,0:T(8,128)(2,1)S(1)}, bf16[512,128]{1,0:T(8,128)(2,1)}, u32[]{:S(2)}) copy-start(bf16[512,128]{1,0:T(8,128)(2,1)} %q_ref.3) | copy-start | bytes 393220
  7.6 4.4 %collective-permute-start = (bf16[2,160,128]{2,1,0:T(8,128)(2,1)S(1)}, bf16[2,160,128]{2,1,0:T(8,128)(2,1)S(1)}, u32[]{:S(2)}, u32[]{:S(2)}) collective-permute-start(bf16[2,160,128]{2,1,0:T(8,128)(2,1)S(1)} %get-tuple-element.24.refs_7_), channel_id=1, source_target_pairs={{0,2},{2,0},{4,6},{6,4},{8,10},{10,8},{12,14},{14,12},{1,3},{3,1},... | collective-permute-start | bytes 245768 | tf_op jit(solution)/shard_map/ppermute | solution.py:506
  8.5 3.5 %copy-start.7 = (f32[3,160,8]{2,1,0:T(8,128)S(1)}, f32[3,160,8]{2,1,0:T(8,128)}, u32[]{:S(2)}) copy-start(f32[3,160,8]{2,1,0:T(8,128)} %constant.15.clone.refs_3_) | copy-start | bytes 46084
  8.5 3.5 %copy-start.8 = (bf16[640,128]{1,0:T(8,128)(2,1)S(1)}, bf16[640,128]{1,0:T(8,128)(2,1)}, u32[]{:S(2)}) copy-start(bf16[640,128]{1,0:T(8,128)(2,1)} %constant.14.clone.refs_2_) | copy-start | bytes 491524
  12.0 3.6 %copy-start.1 = (bf16[512,1024]{1,0:T(8,128)(2,1)S(1)}, bf16[512,1024]{1,0:T(8,128)(2,1)}, u32[]{:S(2)}) copy-start(bf16[512,1024]{1,0:T(8,128)(2,1)} %wk_ref.3) | copy-start | bytes 3145732
  12.9 5.6 %collective-permute-start.3 = (bf16[2,160,128]{2,1,0:T(8,128)(2,1)S(1)}, bf16[2,160,128]{2,1,0:T(8,128)(2,1)S(1)}, u32[]{:S(2)}, u32[]{:S(2)}) collective-permute-start(bf16[2,160,128]{2,1,0:T(8,128)(2,1)S(1)} %get-tuple-element.27.after_ref), channel_id=1, source_target_pairs={{0,8},{2,10},{4,12},{6,14},{8,0},{10,2},{12,4},{14,6},{1,9},{3,11}... | collective-permute-start | bytes 245768 | tf_op jit(solution)/shard_map/ppermute | solution.py:506
  15.6 10.0 %collective-permute-start.7 = (bf16[128,1024]{1,0:T(8,128)(2,1)S(1)}, bf16[128,1024]{1,0:T(8,128)(2,1)S(1)}, u32[]{:S(2)}, u32[]{:S(2)}) collective-permute-start(bf16[128,1024]{1,0:T(8,128)(2,1)S(1)} %edge.1.after_ref), channel_id=1, source_target_pairs={{0,2},{2,4},{4,6},{6,8},{8,10},{10,12},{12,14},{1,3},{3,5},{5,7},{... | collective-permute-start | bytes 786440 | tf_op jit(solution)/shard_map/ppermute | solution.py:596
  18.5 3.8 %copy-start.10 = (bf16[160,224]{1,0:T(8,128)(2,1)S(1)}, bf16[160,224]{1,0:T(8,128)(2,1)}, u32[]{:S(2)}) copy-start(bf16[160,224]{1,0:T(8,128)(2,1)} %constant.17.clone.pick_ref) | copy-start | bytes 215044
  18.7 7.7 %collective-permute-start.4 = (bf16[2,160,128]{2,1,0:T(8,128)(2,1)S(1)}, bf16[2,160,128]{2,1,0:T(8,128)(2,1)S(1)}, u32[]{:S(2)}, u32[]{:S(2)}) collective-permute-start(bf16[2,160,128]{2,1,0:T(8,128)(2,1)S(1)} %get-tuple-element.33), channel_id=1, source_target_pairs={{0,2},{2,0},{4,6},{6,4},{8,10},{10,8},{12,14},{14,12},{1,3},{3,1},... | collective-permute-start | bytes 245768 | tf_op jit(solution)/shard_map/ppermute | solution.py:506
  20.8 5.6 %collective-permute-start.5 = (bf16[2,160,128]{2,1,0:T(8,128)(2,1)S(1)}, bf16[2,160,128]{2,1,0:T(8,128)(2,1)S(1)}, u32[]{:S(2)}, u32[]{:S(2)}) collective-permute-start(bf16[2,160,128]{2,1,0:T(8,128)(2,1)S(1)} %get-tuple-element.34), channel_id=1, source_target_pairs={{0,4},{2,6},{4,0},{6,2},{8,12},{10,14},{12,8},{14,10},{1,5},{3,7},... | collective-permute-start | bytes 245768 | tf_op jit(solution)/shard_map/ppermute | solution.py:506
  21.9 5.3 %collective-permute-start.6 = (bf16[2,160,128]{2,1,0:T(8,128)(2,1)S(1)}, bf16[2,160,128]{2,1,0:T(8,128)(2,1)S(1)}, u32[]{:S(2)}, u32[]{:S(2)}) collective-permute-start(bf16[2,160,128]{2,1,0:T(8,128)(2,1)S(1)} %get-tuple-element.35), channel_id=1, source_target_pairs={{0,6},{2,4},{4,2},{6,0},{8,14},{10,12},{12,10},{14,8},{1,7},{3,5},... | collective-permute-start | bytes 245768 | tf_op jit(solution)/shard_map/ppermute | solution.py:506
  22.3 1.2 %copy-start.2 = (bf16[512,1024]{1,0:T(8,128)(2,1)S(1)}, bf16[512,1024]{1,0:T(8,128)(2,1)}, u32[]{:S(2)}) copy-start(bf16[512,1024]{1,0:T(8,128)(2,1)} %wq_ref.3) | copy-start | bytes 3145732

commit v8 on v7

--- a/solution.py
+++ b/solution.py
@@ -7,6 +7,7 @@
 from jax.sharding import PartitionSpec as P
 
 WINDOW = 64
+PARTS = 2
 ROWS = 160
 EDGE = 158
 LOG2E = float(np.log2(np.e))
@@ -458,15 +459,24 @@
         tail = tile[ROWS - 16 :].astype(F32)[8:]
         lines.append(jnp.concatenate([tail[1:2] + tail[3:4], tail[2:3] + tail[4:5]], axis=1))
     norms = jnp.concatenate(lines).T
+    rights = []
+    for h in range(heads):
+        norm = jnp.broadcast_to(norms[:ROWS, h : h + 1], (ROWS, 128)).astype(BF16)
+        rights.append(jnp.concatenate([tiles[h], norm], axis=1))
     copies = []
-    for h in range(heads):
-        at = slice(128 * h, 128 * h + 128)
-        norm = jnp.broadcast_to(norms[:ROWS, h : h + 1], (ROWS, 128)).astype(BF16)
-        both = nn(phi_ref[h][:, :ROWS], jnp.concatenate([tiles[h], norm], axis=1))
-        out = (num_ref[:, at] + both[:, :128]) / (den_ref[:, at] + both[:, 128:])
-        out = out + jnp.concatenate([early_ref[:, at], win_ref[:, at]])
-        out_ref[h] = out.astype(BF16)
-        copies.append(pltpu.make_async_copy(out_ref.at[h], out_far.at[:, pl.ds(128 * h, 128)], sems.at[h]))
+    rows = phi_ref.shape[1]
+    for low in range(0, rows, rows // PARTS):
+        here = slice(low, low + rows // PARTS)
+        for h in range(heads):
+            at = slice(128 * h, 128 * h + 128)
+            both = nn(phi_ref[h, here][:, :ROWS], rights[h])
+            out = (num_ref[here, at] + both[:, :128]) / (den_ref[here, at] + both[:, 128:])
+            if low:
+                out = out + win_ref[low - WINDOW : low - WINDOW + rows // PARTS, at]
+            else:
+                out = out + jnp.concatenate([early_ref[:, at], win_ref[: rows // PARTS - WINDOW, at]])
+            out_ref[here, at] = out.astype(BF16)
+        copies.append(pltpu.make_async_copy(out_ref.at[pl.ds(low, rows // PARTS)], out_far.at[pl.ds(low, rows // PARTS)], sems.at[len(copies)]))
         copies[-1].start()
     for copy in copies:
         copy.wait()
@@ -635,7 +645,7 @@
         finish_kernel,
         (place, phi, *prefixes, num, den, win, early),
         jax.ShapeDtypeStruct(values.shape, BF16),
-        [held, pltpu.VMEM((heads, rows, 128), BF16), pltpu.SemaphoreType.DMA((heads,))],
+        [held, pltpu.VMEM(values.shape, BF16), pltpu.SemaphoreType.DMA((PARTS,))],
         smem=(0,),
         out_space=pltpu.HBM,
         name="finish",

time: 29.2 us -> 29.3 us (level)
  no operation moved by 1% of the time
where the time goes in v8:
time: 29.3 us; the launch traced here: 29.1 us
  starting transfers between devices  13.9 us (47%)
  Pallas kernels  11.9 us (41%)
  waiting for transfers between devices  1.94 us (7%)
  local copies, waits for them, and re-layouts  1.19 us (4%)
    pallas_call x13, Pallas kernels, call(): pl.pallas_call(kernel, out_shape=outs, in_specs=[pl.BlockSpec(memory_spac...  11.9 us
    ppermute x7, starting transfers between devices, swap(): return lax.ppermute(x, 'seq', [(i, i ^ distance) for i in range(count)])  11 us
    ppermute x1, starting transfers between devices, local(): halo = lax.ppermute(edge, 'seq', [(i, i + 1) for i in range(count - 1)])  2.91 us
    ppermute x7, waiting for transfers between devices, swap(): return lax.ppermute(x, 'seq', [(i, i ^ distance) for i in range(count)])  1.83 us
    unnamed x22, local copies, waits for them, and re-layouts  1.19 us
  transfers between devices with their start and end apart: 8, of which 5 were waited for; matrix products, arithmetic and copies ran while one was open for 0% of the time, Pallas kernels for 28%

profile of v8, /device:TPU:0, one launch (start us, length us, event | category | flops | bytes accessed | tf_op | source)
XLA Modules:
  0.0 29.1 jit_solution(9057421373559144928)
XLA Ops:
  0.0 0.9 %copy-done.3 = bf16[512,128]{1,0:T(8,128)(2,1)S(1)} copy-done((bf16[512,128]{1,0:T(8,128)(2,1)S(1)}, bf16[512,128]{1,0:T(8,128)(2,1)}, u32[]{:S(2)}) %copy-start.3) | copy-done | bytes 131096
  0.9 0.4 %gates.1 = (f32[8,512]{1,0:T(8,128)S(1)}, f32[128,512]{1,0:T(8,128)S(1)}) custom-call(f32[8,512]{1,0:T(8,128)S(1)} %bitcast.2, bf16[512,128]{1,0:T(8,128)(2,1)S(1)} %copy-done.3, f32[8,128]{1,0:T(8,128)S(1)} %open.1.after_ref), custom_call_target="tpu_custom_call" | custom-call | flops 30000000 | bytes 90000 | tf_op jit(solution)/shard_map/gates/pallas_call | solution.py:489
  1.3 0.0 copy-done
  1.3 0.6 %states0.1.refs_7_ = bf16[2,160,128]{2,1,0:T(8,128)(2,1)S(1)} custom-call(s32[1]{0:T(128)} %bitcast.place_ref.refs_0_, bf16[512,128]{1,0:T(8,128)(2,1)S(1)} %copy-done.3, f32[128,512]{1,0:T(8,128)S(1)} %get-tuple-element.23.refs_2_.turned_ref, bf16[512,1024]{1,0:T(8,128)(2,1)S(1)} %copy-done, f32[8,512]{1,0:T(8,128)S(1)} %get-tuple-element.22.refs_4_.refs_7_.cum_ref, ...), custom_call_target="tpu_custom_call" | custom-call | flops 2400000000 | bytes 7200000 | tf_op jit(solution)/shard_map/states0/pallas_call | solution.py:489
  2.0 4.0 %collective-permute-start.2 = (bf16[2,160,128]{2,1,0:T(8,128)(2,1)S(1)}, bf16[2,160,128]{2,1,0:T(8,128)(2,1)S(1)}, u32[]{:S(2)}, u32[]{:S(2)}) collective-permute-start(bf16[2,160,128]{2,1,0:T(8,128)(2,1)S(1)} %states0.1.refs_7_), channel_id=1, source_target_pairs={{0,6},{2,4},{4,2},{6,0},{8,14},{10,12},{12,10},{14,8},{1,7},{3,5},... | collective-permute-start | bytes 245768 | tf_op jit(solution)/shard_map/ppermute | solution.py:516
  6.0 1.1 %states1.1 = (bf16[2,160,128]{2,1,0:T(8,128)(2,1)S(1)}, bf16[2,160,128]{2,1,0:T(8,128)(2,1)S(1)}) custom-call(s32[1]{0:T(128)} %bitcast.place_ref.refs_0_, bf16[512,128]{1,0:T(8,128)(2,1)S(1)} %copy-done.3, f32[128,512]{1,0:T(8,128)S(1)} %get-tuple-element.23.refs_2_.turned_ref, bf16[512,1024]{1,0:T(8,128)(2,1)S(1)} %copy-done, ...), custom_call_target="tpu_custom_call" | custom-call | flops 3900000000 | bytes 11700000 | tf_op jit(solution)/shard_map/states1/pallas_call | solution.py:489
  7.1 0.5 %collective-permute-start.1 = (bf16[2,160,128]{2,1,0:T(8,128)(2,1)S(1)}, bf16[2,160,128]{2,1,0:T(8,128)(2,1)S(1)}, u32[]{:S(2)}, u32[]{:S(2)}) collective-permute-start(bf16[2,160,128]{2,1,0:T(8,128)(2,1)S(1)} %get-tuple-element.25), channel_id=1, source_target_pairs={{0,4},{2,6},{4,0},{6,2},{8,12},{10,14},{12,8},{14,10},{1,5},{3,7},... | collective-permute-start | bytes 245768 | tf_op jit(solution)/shard_map/ppermute | solution.py:516
  7.6 0.1 collective-permute-start
  7.7 0.6 %own_states.1.after_ref.refs_4_ = bf16[2,160,128]{2,1,0:T(8,128)(2,1)S(1)} custom-call(s32[1]{0:T(128)} %bitcast.place_ref.refs_0_, bf16[512,128]{1,0:T(8,128)(2,1)S(1)} %copy-done.3, f32[128,512]{1,0:T(8,128)S(1)} %get-tuple-element.23.refs_2_.turned_ref, bf16[512,1024]{1,0:T(8,128)(2,1)S(1)} %copy-done, ...), custom_call_target="tpu_custom_call" | custom-call | flops 2400000000 | bytes 7200000 | tf_op jit(solution)/shard_map/own_states/pallas_call | solution.py:489
  8.3 0.1 copy-done.5
  8.5 2.7 %block.1 = (f32[512,1024]{1,0:T(8,128)S(1)}, f32[512,1024]{1,0:T(8,128)S(1)}, f32[8,128]{1,0:T(8,128)S(1)}) custom-call(bf16[512,128]{1,0:T(8,128)(2,1)S(1)} %copy-done.5, f32[128,512]{1,0:T(8,128)S(1)} %get-tuple-element.23.refs_2_.turned_ref, bf16[512,1024]{1,0:T(8,128)(2,1)S(1)} %copy-done, f32[3,1024]{1,0:T(4,128)S(1)} %copy-done.6, ...), custom_call_target="tpu_custom_call" | custom-call | flops 8099999744 | bytes 24300000 | tf_op jit(solution)/shard_map/block/pallas_call | solution.py:489
  11.1 0.0 collective-permute-done.2.refs_7_
  11.1 0.4 %collective-permute-done.1.refs_6_ = bf16[2,160,128]{2,1,0:T(8,128)(2,1)S(1)} collective-permute-done((bf16[2,160,128]{2,1,0:T(8,128)(2,1)S(1)}, bf16[2,160,128]{2,1,0:T(8,128)(2,1)S(1)}, u32[]{:S(2)}, u32[]{:S(2)}) %collective-permute-start.1) | collective-permute-done | bytes 81952 | tf_op jit(solution)/shard_map/ppermute | solution.py:516
  11.5 0.5 %collective-permute-done.refs_5_ = bf16[2,160,128]{2,1,0:T(8,128)(2,1)S(1)} collective-permute-done((bf16[2,160,128]{2,1,0:T(8,128)(2,1)S(1)}, bf16[2,160,128]{2,1,0:T(8,128)(2,1)S(1)}, u32[]{:S(2)}, u32[]{:S(2)}) %collective-permute-start) | collective-permute-done | bytes 81952 | tf_op jit(solution)/shard_map/ppermute | solution.py:516
  12.0 0.9 %merge_group.1 = (bf16[2,160,128]{2,1,0:T(8,128)(2,1)S(1)}, f32[3,2,160,128]{3,2,1,0:T(8,128)S(1)}, f32[2,2,160,128]{3,2,1,0:T(8,128)S(1)}, f32[2,8,128]{2,1,0:T(8,128)S(1)}) custom-call(s32[1]{0:T(128)} %bitcast.place_ref.refs_0_, f32[3,1024]{1,0:T(4,128)S(1)} %copy-done.6, bf16[640,128]{1,0:T(8,128)(2,1)S(1)} %copy-done.8, f32[3,160,8]{2,1,0:T(8,128)S(1)} %copy-done.7, ...), custom_call_target="tpu_custom_call" | custom-call | flops 6000000000 | bytes 18000000 | tf_op jit(solution)/shard_map/merge_group/pallas_call | solution.py:489
  12.9 2.6 %collective-permute-start.3 = (bf16[2,160,128]{2,1,0:T(8,128)(2,1)S(1)}, bf16[2,160,128]{2,1,0:T(8,128)(2,1)S(1)}, u32[]{:S(2)}, u32[]{:S(2)}) collective-permute-start(bf16[2,160,128]{2,1,0:T(8,128)(2,1)S(1)} %get-tuple-element.27.after_ref), channel_id=1, source_target_pairs={{0,8},{2,10},{4,12},{6,14},{8,0},{10,2},{12,4},{14,6},{1,9},{3,11}... | collective-permute-start | bytes 245768 | tf_op jit(solution)/shard_map/ppermute | solution.py:516
  15.6 2.9 %collective-permute-start.7 = (bf16[128,1024]{1,0:T(8,128)(2,1)S(1)}, bf16[128,1024]{1,0:T(8,128)(2,1)S(1)}, u32[]{:S(2)}, u32[]{:S(2)}) collective-permute-start(bf16[128,1024]{1,0:T(8,128)(2,1)S(1)} %edge.1.after_ref), channel_id=1, source_target_pairs={{0,2},{2,4},{4,6},{6,8},{8,10},{10,12},{12,14},{1,3},{3,5},{5,7},{... | collective-permute-start | bytes 786440 | tf_op jit(solution)/shard_map/ppermute | solution.py:606
  18.5 0.0 collective-permute-done.3.base_ref
  18.5 0.0 copy-start.10
  18.5 0.1 spread.1
  18.7 2.1 %collective-permute-start.4 = (bf16[2,160,128]{2,1,0:T(8,128)(2,1)S(1)}, bf16[2,160,128]{2,1,0:T(8,128)(2,1)S(1)}, u32[]{:S(2)}, u32[]{:S(2)}) collective-permute-start(bf16[2,160,128]{2,1,0:T(8,128)(2,1)S(1)} %get-tuple-element.33), channel_id=1, source_target_pairs={{0,2},{2,0},{4,6},{6,4},{8,10},{10,8},{12,14},{14,12},{1,3},{3,1},... | collective-permute-start | bytes 245768 | tf_op jit(solution)/shard_map/ppermute | solution.py:516
  20.8 1.2 %collective-permute-start.5 = (bf16[2,160,128]{2,1,0:T(8,128)(2,1)S(1)}, bf16[2,160,128]{2,1,0:T(8,128)(2,1)S(1)}, u32[]{:S(2)}, u32[]{:S(2)}) collective-permute-start(bf16[2,160,128]{2,1,0:T(8,128)(2,1)S(1)} %get-tuple-element.34), channel_id=1, source_target_pairs={{0,4},{2,6},{4,0},{6,2},{8,12},{10,14},{12,8},{14,10},{1,5},{3,7},... | collective-permute-start | bytes 245768 | tf_op jit(solution)/shard_map/ppermute | solution.py:516
  21.9 0.4 %collective-permute-start.6 = (bf16[2,160,128]{2,1,0:T(8,128)(2,1)S(1)}, bf16[2,160,128]{2,1,0:T(8,128)(2,1)S(1)}, u32[]{:S(2)}, u32[]{:S(2)}) collective-permute-start(bf16[2,160,128]{2,1,0:T(8,128)(2,1)S(1)} %get-tuple-element.35), channel_id=1, source_target_pairs={{0,6},{2,4},{4,2},{6,0},{8,14},{10,12},{12,10},{14,8},{1,7},{3,5},... | collective-permute-start | bytes 245768 | tf_op jit(solution)/shard_map/ppermute | solution.py:516
  22.3 1.1 %query_features.1 = (bf16[8,512,256]{2,1,0:T(8,128)(2,1)S(1)}, f32[8,128]{1,0:T(8,128)S(1)}) custom-call(bf16[512,128]{1,0:T(8,128)(2,1)S(1)} %copy-done.5, bf16[512,128]{1,0:T(8,128)(2,1)S(1)} %copy-done.3, f32[8,512]{1,0:T(8,128)S(1)} %get-tuple-element.22.refs_4_.refs_7_.cum_ref, bf16[160,224]{1,0:T(8,128)(2,1)S(1)} %copy-done.10, ...), custom_call_target="tpu_custom_call" | custom-call | flops 4499999744 | bytes 13500000 | tf_op jit(solution)/shard_map/query_features/pallas_call | solution.py:489
  23.4 0.1 copy-done.2
  23.6 1.9 %window.1.after_ref.win_ref = f32[448,1024]{1,0:T(8,128)S(1)} custom-call(bf16[512,1024]{1,0:T(8,128)(2,1)S(1)} %copy-done.2, bf16[512,1024]{1,0:T(8,128)(2,1)S(1)} %copy-done.1, bf16[512,1024]{1,0:T(8,128)(2,1)S(1)} %copy-done, f32[8,128]{1,0:T(8,128)S(1)} %get-tuple-element.38.after_ref), custom_call_target="tpu_custom_call" | custom-call | flops 6000000000 | bytes 18000000 | tf_op jit(solution)/shard_map/window/pallas_call | solution.py:489
  25.5 0.1 collective-permute-done.7.halo_ref
  25.6 0.7 %window_first.1.early_ref = f32[64,1024]{1,0:T(8,128)S(1)} custom-call(s32[1]{0:T(128)} %bitcast.place_ref.refs_0_, bf16[512,1024]{1,0:T(8,128)(2,1)S(1)} %copy-done.2, bf16[512,1024]{1,0:T(8,128)(2,1)S(1)} %copy-done.1, bf16[512,1024]{1,0:T(8,128)(2,1)S(1)} %copy-done, bf16[128,1024]{1,0:T(8,128)(2,1)S(1)} %collective-permute-done.7.halo_ref, ...), custom_call_target="tpu_custom_call" | custom-call | flops 1200000000 | bytes 3600000 | tf_op jit(solution)/shard_map/window_first/pallas_call | solution.py:489
  26.3 0.1 collective-permute-done.4.x1
  26.4 0.0 collective-permute-done.5.x2
  26.4 0.9 %collective-permute-done.6.x3 = bf16[2,160,128]{2,1,0:T(8,128)(2,1)S(1)} collective-permute-done((bf16[2,160,128]{2,1,0:T(8,128)(2,1)S(1)}, bf16[2,160,128]{2,1,0:T(8,128)(2,1)S(1)}, u32[]{:S(2)}, u32[]{:S(2)}) %collective-permute-start.6) | collective-permute-done | bytes 81952 | tf_op jit(solution)/shard_map/ppermute | solution.py:516
  27.3 1.8 %finish.1 = bf16[512,1024]{1,0:T(8,128)(2,1)} custom-call(s32[1]{0:T(128)} %bitcast.place_ref.refs_0_, bf16[8,512,256]{2,1,0:T(8,128)(2,1)S(1)} %get-tuple-element.32.phi_ref, bf16[2,160,128]{2,1,0:T(8,128)(2,1)S(1)} %get-tuple-element.31.after_ref.x0, bf16[2,160,128]{2,1,0:T(8,128)(2,1)S(1)} %collective-permute-done.4.x1, ...), custom_call_target="tpu_custom_call" | custom-call | flops 6300000256 | bytes 18900000 | tf_op jit(solution)/shard_map/finish/pallas_call | solution.py:489
  (19 shorter events, 0.1 us)
Async XLA Ops:
  0.0 0.9 %copy-start.3 = (bf16[512,128]{1,0:T(8,128)(2,1)S(1)}, bf16[512,128]{1,0:T(8,128)(2,1)}, u32[]{:S(2)}) copy-start(bf16[512,128]{1,0:T(8,128)(2,1)} %k_ref.3) | copy-start | bytes 393220
  0.0 0.9 %copy-start.4 = (f32[512,8]{0,1:T(8,128)S(1)}, f32[512,8]{0,1:T(8,128)}, u32[]{:S(2)}) copy-start(f32[512,8]{0,1:T(8,128)} %param.16) | copy-start | bytes 49156
  0.0 1.3 %copy-start = (bf16[512,1024]{1,0:T(8,128)(2,1)S(1)}, bf16[512,1024]{1,0:T(8,128)(2,1)}, u32[]{:S(2)}) copy-start(bf16[512,1024]{1,0:T(8,128)(2,1)} %v_ref.7) | copy-start | bytes 3145732
  0.0 1.3 %copy-start.6 = (f32[3,1024]{1,0:T(4,128)S(1)}, f32[3,1024]{1,0:T(4,128)}, u32[]{:S(2)}) copy-start(f32[3,1024]{1,0:T(4,128)} %w_ref.3) | copy-start | bytes 36868
  0.0 1.3 %copy-start.9 = (bf16[256,224]{1,0:T(8,128)(2,1)S(1)}, bf16[256,224]{1,0:T(8,128)(2,1)}, u32[]{:S(2)}) copy-start(bf16[256,224]{1,0:T(8,128)(2,1)} %constant.16.clone.refs_6_) | copy-start | bytes 344068
  2.0 9.1 %collective-permute-start.2 = (bf16[2,160,128]{2,1,0:T(8,128)(2,1)S(1)}, bf16[2,160,128]{2,1,0:T(8,128)(2,1)S(1)}, u32[]{:S(2)}, u32[]{:S(2)}) collective-permute-start(bf16[2,160,128]{2,1,0:T(8,128)(2,1)S(1)} %states0.1.refs_7_), channel_id=1, source_target_pairs={{0,6},{2,4},{4,2},{6,0},{8,14},{10,12},{12,10},{14,8},{1,7},{3,5},... | collective-permute-start | bytes 245768 | tf_op jit(solution)/shard_map/ppermute | solution.py:516
  7.1 4.5 %collective-permute-start.1 = (bf16[2,160,128]{2,1,0:T(8,128)(2,1)S(1)}, bf16[2,160,128]{2,1,0:T(8,128)(2,1)S(1)}, u32[]{:S(2)}, u32[]{:S(2)}) collective-permute-start(bf16[2,160,128]{2,1,0:T(8,128)(2,1)S(1)} %get-tuple-element.25), channel_id=1, source_target_pairs={{0,4},{2,6},{4,0},{6,2},{8,12},{10,14},{12,8},{14,10},{1,5},{3,7},... | collective-permute-start | bytes 245768 | tf_op jit(solution)/shard_map/ppermute | solution.py:516
  7.6 0.9 %copy-start.5 = (bf16[512,128]{1,0:T(8,128)(2,1)S(1)}, bf16[512,128]{1,0:T(8,128)(2,1)}, u32[]{:S(2)}) copy-start(bf16[512,128]{1,0:T(8,128)(2,1)} %q_ref.3) | copy-start | bytes 393220
  7.6 4.4 %collective-permute-start = (bf16[2,160,128]{2,1,0:T(8,128)(2,1)S(1)}, bf16[2,160,128]{2,1,0:T(8,128)(2,1)S(1)}, u32[]{:S(2)}, u32[]{:S(2)}) collective-permute-start(bf16[2,160,128]{2,1,0:T(8,128)(2,1)S(1)} %get-tuple-element.24.refs_7_), channel_id=1, source_target_pairs={{0,2},{2,0},{4,6},{6,4},{8,10},{10,8},{12,14},{14,12},{1,3},{3,1},... | collective-permute-start | bytes 245768 | tf_op jit(solution)/shard_map/ppermute | solution.py:516
  8.5 3.5 %copy-start.7 = (f32[3,160,8]{2,1,0:T(8,128)S(1)}, f32[3,160,8]{2,1,0:T(8,128)}, u32[]{:S(2)}) copy-start(f32[3,160,8]{2,1,0:T(8,128)} %constant.15.clone.refs_3_) | copy-start | bytes 46084
  8.5 3.5 %copy-start.8 = (bf16[640,128]{1,0:T(8,128)(2,1)S(1)}, bf16[640,128]{1,0:T(8,128)(2,1)}, u32[]{:S(2)}) copy-start(bf16[640,128]{1,0:T(8,128)(2,1)} %constant.14.clone.refs_2_) | copy-start | bytes 491524
  12.0 3.6 %copy-start.1 = (bf16[512,1024]{1,0:T(8,128)(2,1)S(1)}, bf16[512,1024]{1,0:T(8,128)(2,1)}, u32[]{:S(2)}) copy-start(bf16[512,1024]{1,0:T(8,128)(2,1)} %wk_ref.3) | copy-start | bytes 3145732
  12.9 5.6 %collective-permute-start.3 = (bf16[2,160,128]{2,1,0:T(8,128)(2,1)S(1)}, bf16[2,160,128]{2,1,0:T(8,128)(2,1)S(1)}, u32[]{:S(2)}, u32[]{:S(2)}) collective-permute-start(bf16[2,160,128]{2,1,0:T(8,128)(2,1)S(1)} %get-tuple-element.27.after_ref), channel_id=1, source_target_pairs={{0,8},{2,10},{4,12},{6,14},{8,0},{10,2},{12,4},{14,6},{1,9},{3,11}... | collective-permute-start | bytes 245768 | tf_op jit(solution)/shard_map/ppermute | solution.py:516
  15.6 10.0 %collective-permute-start.7 = (bf16[128,1024]{1,0:T(8,128)(2,1)S(1)}, bf16[128,1024]{1,0:T(8,128)(2,1)S(1)}, u32[]{:S(2)}, u32[]{:S(2)}) collective-permute-start(bf16[128,1024]{1,0:T(8,128)(2,1)S(1)} %edge.1.after_ref), channel_id=1, source_target_pairs={{0,2},{2,4},{4,6},{6,8},{8,10},{10,12},{12,14},{1,3},{3,5},{5,7},{... | collective-permute-start | bytes 786440 | tf_op jit(solution)/shard_map/ppermute | solution.py:606
  18.5 3.8 %copy-start.10 = (bf16[160,224]{1,0:T(8,128)(2,1)S(1)}, bf16[160,224]{1,0:T(8,128)(2,1)}, u32[]{:S(2)}) copy-start(bf16[160,224]{1,0:T(8,128)(2,1)} %constant.17.clone.pick_ref) | copy-start | bytes 215044
  18.7 7.7 %collective-permute-start.4 = (bf16[2,160,128]{2,1,0:T(8,128)(2,1)S(1)}, bf16[2,160,128]{2,1,0:T(8,128)(2,1)S(1)}, u32[]{:S(2)}, u32[]{:S(2)}) collective-permute-start(bf16[2,160,128]{2,1,0:T(8,128)(2,1)S(1)} %get-tuple-element.33), channel_id=1, source_target_pairs={{0,2},{2,0},{4,6},{6,4},{8,10},{10,8},{12,14},{14,12},{1,3},{3,1},... | collective-permute-start | bytes 245768 | tf_op jit(solution)/shard_map/ppermute | solution.py:516
  20.8 5.6 %collective-permute-start.5 = (bf16[2,160,128]{2,1,0:T(8,128)(2,1)S(1)}, bf16[2,160,128]{2,1,0:T(8,128)(2,1)S(1)}, u32[]{:S(2)}, u32[]{:S(2)}) collective-permute-start(bf16[2,160,128]{2,1,0:T(8,128)(2,1)S(1)} %get-tuple-element.34), channel_id=1, source_target_pairs={{0,4},{2,6},{4,0},{6,2},{8,12},{10,14},{12,8},{14,10},{1,5},{3,7},... | collective-permute-start | bytes 245768 | tf_op jit(solution)/shard_map/ppermute | solution.py:516
  21.9 5.3 %collective-permute-start.6 = (bf16[2,160,128]{2,1,0:T(8,128)(2,1)S(1)}, bf16[2,160,128]{2,1,0:T(8,128)(2,1)S(1)}, u32[]{:S(2)}, u32[]{:S(2)}) collective-permute-start(bf16[2,160,128]{2,1,0:T(8,128)(2,1)S(1)} %get-tuple-element.35), channel_id=1, source_target_pairs={{0,6},{2,4},{4,2},{6,0},{8,14},{10,12},{12,10},{14,8},{1,7},{3,5},... | collective-permute-start | bytes 245768 | tf_op jit(solution)/shard_map/ppermute | solution.py:516
  22.3 1.2 %copy-start.2 = (bf16[512,1024]{1,0:T(8,128)(2,1)S(1)}, bf16[512,1024]{1,0:T(8,128)(2,1)}, u32[]{:S(2)}) copy-start(bf16[512,1024]{1,0:T(8,128)(2,1)} %wq_ref.3) | copy-start | bytes 3145732
